TPU v7x, 32 devices: a whole 2x2x4 slice. The times are simulated.
32 devices in a mesh: seq: 8 (over z, y), batch: 4 (over x, core).
Axes of the slice: x: 2, y: 2, z: 4, core: 2. Of those that a mesh axis runs over, the one named last changes fastest.
Arguments:
- inputs: bfloat16 [16, 1024, 768], P('batch', 'seq'), may hold values from -6 to 6
- cotangent: bfloat16 [16, 1024, 768], P('batch', 'seq'), may hold values from -6 to 6
- doc_lengths: int32 [16, 8], P('batch'), may hold values from 1 to 512, 1024 in all within a row
- qkv_weight: float32 [896, 768], P('seq'), may hold values from -0.3125 to 0.3125
- out_weight: float32 [768, 768], P('seq'), may hold values from -0.625 to 0.625
- up_weight: float32 [3072, 768], P('seq'), may hold values from -0.21875 to 0.21875
- down_weight: float32 [768, 3072], P(None, 'seq'), may hold values from -0.109375 to 0.109375
- vectors: float32 [8576], P('seq'), may hold values from -0.9 to 1.6, as said below
- bases: float32 [4, 768, 768], replicated, may hold values from -1 to 1, as said below
- qkv_first: float32 [896, 768], P('seq'), may hold values from -64 to 64
- out_first: float32 [768, 768], P('seq'), may hold values from -20 to 20
- up_first: float32 [3072, 768], P('seq'), may hold values from -24 to 24
- down_first: float32 [768, 3072], P(None, 'seq'), may hold values from -40 to 40
- vector_first: float32 [8576], P('seq'), may hold values from -64 to 64
- qkv_second: float32 [896, 768], P('seq'), may hold values from 819.2 to 8192
- out_second: float32 [768, 768], P('seq'), may hold values from 81.92 to 1310.72
- up_second: float32 [3072, 768], P('seq'), may hold values from 131.072 to 1966.08
- down_second: float32 [768, 3072], P(None, 'seq'), may hold values from 409.6 to 6553.6
- vector_second: float32 [8576], P('seq'), may hold values from 327.68 to 16384
Outputs:
- outputs: bfloat16 [16, 1024, 768], P('batch', 'seq')
- input_grad: bfloat16 [16, 1024, 768], P('batch', 'seq')
- qkv_grad: float32 [896, 768], P('seq')
- out_grad: float32 [768, 768], P('seq')
- up_grad: float32 [3072, 768], P('seq')
- down_grad: float32 [768, 3072], P(None, 'seq')
- vector_grad: float32 [8576], P('seq')
- qkv_first_new: float32 [896, 768], P('seq')
- out_first_new: float32 [768, 768], P('seq')
- up_first_new: float32 [3072, 768], P('seq')
- down_first_new: float32 [768, 3072], P(None, 'seq')
- vector_first_new: float32 [8576], P('seq')
- qkv_second_new: float32 [896, 768], P('seq')
- out_second_new: float32 [768, 768], P('seq')
- up_second_new: float32 [3072, 768], P('seq')
- down_second_new: float32 [768, 3072], P(None, 'seq')
- vector_second_new: float32 [8576], P('seq')
- qkv_new: float32 [896, 768], P('seq')
- out_new: float32 [768, 768], P('seq')
- up_new: float32 [3072, 768], P('seq')
- down_new: float32 [768, 3072], P(None, 'seq')
- vector_new: float32 [8576], P('seq')
Inputs may be any that keep to these rules, and one draw needn't show every extreme that they name: `doc_lengths`: the 8 lengths of a row sum to 1024, and in every row the longest document has exactly half of 1024 positions. `vectors`: entries 0 to 767 and 1536 to 2303 are the two norms' gains, all others shifts and biases. `bases`: each of the four matrices is orthogonal.
All inputs are finite; a program needn't handle non-finite values.
Results may differ from a plain program's by a relative error of at most 0.006.
The roundings to bfloat16 on the way count: a program that leaves them out, or rounds other values in their place, can miss the bound.
Values may be sent and summed in bfloat16 or wider, within the bound.
No kernel may reach another device: no remote copies, remote signals or barrier semaphores. Data moves between devices by JAX's collectives and lax.ppermute only.
A program may use at most 192 MiB of HBM per device.

v0:
```python
import functools

import jax
import jax.numpy as jnp
from jax import lax
from jax.experimental import pallas as pl
from jax.experimental.pallas import tpu as pltpu
from jax.sharding import PartitionSpec as P

D = 768
HEADS = 12
HEAD = 64
ROT = 16
FF = 3072
STEP = 10

layer_eps = 1e-05
adam_eps = 1e-08
beta_first = 0.95
beta_second = 0.95
matrix_rate = 0.08
vector_rate = 0.3
rope_base = 10000.0
masked_score = -1e30
low = jnp.bfloat16
f32 = jnp.float32
VMEM_LIMIT = 56 * 1024 * 1024
FEED_VMEM = 56 * 1024 * 1024
UPDATE_VMEM = 28 * 1024 * 1024


def swap(value, bit):
    axis, step = bit
    return lax.ppermute(value, axis, [(i, i ^ step) for i in range(lax.axis_size(axis))])


def mine(bit):
    axis, step = bit
    return lax.rem(lax.axis_index(axis) // step, 2)


def flow(first, *others):
    return lax.optimization_barrier((first, *others))[0]


def swap_z(value, step):
    size = lax.axis_size("seq")
    return lax.ppermute(value, "seq", [(i, i ^ (2 * step)) for i in range(size)])


def z_index():
    return lax.axis_index("seq") // 2


def gather_z(piece):
    return [piece] + [swap_z(piece, k) for k in range(1, lax.axis_size("seq") // 2)]


def gather_bit(value, bit, axis, absolute=False, after=()):
    got = swap(value, bit)
    if after:
        got = flow(got, *after)
    if absolute:
        upper = mine(bit) == 1
        return jnp.stack([jnp.where(upper, got, value), jnp.where(upper, value, got)], axis=axis)
    return jnp.stack([value, got], axis=axis)


def split_bit(value, bit, axis, absolute=False):
    if absolute:
        own = mine(bit)
        return (
            lax.dynamic_index_in_dim(value, own, axis, keepdims=False),
            lax.dynamic_index_in_dim(value, 1 - own, axis, keepdims=False).astype(low),
        )
    return lax.index_in_dim(value, 0, axis, keepdims=False), lax.index_in_dim(value, 1, axis, keepdims=False).astype(low)


def sum_bit(value, bit, axis, absolute=False, after=()):
    kept, sent = split_bit(value, bit, axis, absolute)
    got = swap(sent, bit)
    if after:
        got = flow(got, *after)
    return kept.astype(f32) + got.astype(f32)


def sum_z(value, absolute=False):
    count = value.shape[0]
    own = z_index() if absolute else 0
    pick = lambda k: lax.dynamic_index_in_dim(value, own ^ k, 0, keepdims=False) if absolute else value[k]
    total = pick(0).astype(f32)
    for k in range(1, count):
        total = total + swap_z(pick(k).astype(low), k).astype(f32)
    return total


def bit_names(axis, size):
    return [(axis, 1 << k) for k in range(size.bit_length() - 1)]


def moments(rotated, first, second):
    new_first = beta_first * first + (1.0 - beta_first) * rotated
    new_second = beta_second * second + (1.0 - beta_second) * rotated * rotated
    first_scale, second_scale = 1.0 / (1.0 - beta_first**STEP), 1.0 / (1.0 - beta_second**STEP)
    ratio = new_first * first_scale / (jnp.sqrt(new_second * second_scale) + adam_eps)
    return ratio, new_first, new_second


def adam_step(weight, grad, first, second):
    ratio, new_first, new_second = moments(grad, first, second)
    return (weight - vector_rate * ratio, new_first, new_second)


def attention_kernel(blocks, width, q_ref, do_ref, start_ref, cos_ref, sin_ref, kv_ref, context_ref, dq_ref, dkv_own_ref, dkv_ref):
    length = q_ref.shape[1]
    keys = blocks * length
    key_t = jnp.concatenate([kv_ref[k, :HEAD, :] for k in reversed(range(blocks))], axis=1)
    value_t = jnp.concatenate([kv_ref[k, HEAD:, :] for k in reversed(range(blocks))], axis=1)
    key = key_t.astype(f32).T.astype(low)
    value = value_t.astype(f32).T.astype(low)
    key_pos = lax.broadcasted_iota(jnp.int32, (keys, length), 0) - (blocks - 1) * length
    query_pos = lax.broadcasted_iota(jnp.int32, (keys, length), 1)
    allowed = (key_pos >= start_ref[0]) & (key_pos <= query_pos)
    bias = jnp.where(allowed, 0.0, masked_score)
    cosine, sine = cos_ref[...], sin_ref[...]
    d_key = jnp.zeros((keys, HEAD), f32)
    d_value = jnp.zeros((keys, HEAD), f32)
    last = (((1,), (1,)), ((), ()))
    for first in range(0, HEADS, width):
        heads = range(first, first + width)
        query = jnp.concatenate([q_ref[h * HEAD : (h + 1) * HEAD, :] for h in heads], axis=1)
        d_out = jnp.concatenate([do_ref[h * HEAD : (h + 1) * HEAD, :] for h in heads], axis=1)
        scores = jnp.dot(key, query, preferred_element_type=f32)
        scores = scores + jnp.concatenate([bias] * width, axis=1)
        weights = jnp.exp(scores - jnp.max(scores, axis=0, keepdims=True))
        probs = weights * (1.0 / jnp.sum(weights, axis=0, keepdims=True))
        probs_low = probs.astype(low)
        context_t = jnp.dot(value_t, probs_low, preferred_element_type=f32)
        d_probs = jnp.dot(value, d_out, preferred_element_type=f32)
        inner = jnp.sum(probs * d_probs, axis=0, keepdims=True)
        d_scores = (probs * (d_probs - inner)).astype(low)
        d_query = jnp.dot(key_t, d_scores, preferred_element_type=f32) * HEAD ** (-0.5)
        d_value = d_value + lax.dot_general(probs_low, d_out, last, preferred_element_type=f32)
        d_key = d_key + lax.dot_general(d_scores, query, last, preferred_element_type=f32)
        for k, h in enumerate(heads):
            lanes = slice(k * length, (k + 1) * length)
            part = d_query[:, lanes]
            a, b = part[: ROT // 2], part[ROT // 2 : ROT]
            turned = jnp.concatenate([a * cosine + b * sine, b * cosine - a * sine, part[ROT:]], axis=0)
            dq_ref[h * HEAD : (h + 1) * HEAD, :] = turned.astype(low)
        for k in range(0, width, 2):
            h = first + k
            two = jnp.concatenate(
                [context_t[:, k * length : (k + 1) * length], context_t[:, (k + 1) * length : (k + 2) * length]], axis=0
            )
            context_ref[:, h * HEAD : (h + 2) * HEAD] = two.T.astype(low)
    d_kv = jnp.concatenate([d_key, d_value], axis=1).T
    for k in range(blocks):
        part = d_kv[:, (blocks - 1 - k) * length : (blocks - k) * length]
        if k == 0:
            dkv_own_ref[...] = part
        else:
            dkv_ref[k - 1] = part.astype(low)


def attention(q_t, do_t, start, cosine, sine, kv):
    rows, _, length = start.shape
    blocks = kv.shape[0]
    tokens = q_t.shape[1]
    by_row = lambda height: pl.BlockSpec((height, length), lambda r: (0, r))
    return pl.pallas_call(
        functools.partial(attention_kernel, blocks, HEADS),
        grid=(rows,),
        in_specs=[by_row(D), by_row(D), pl.BlockSpec((1, 1, length), lambda r: (r, 0, 0)), by_row(ROT // 2), by_row(ROT // 2)]
        + [pl.BlockSpec((blocks, 2 * HEAD, length), lambda r: (0, 0, r))],
        out_specs=[
            pl.BlockSpec((length, D), lambda r: (r, 0)),
            by_row(D),
            by_row(2 * HEAD),
            pl.BlockSpec((blocks - 1, 2 * HEAD, length), lambda r: (0, 0, r)),
        ],
        out_shape=[
            jax.ShapeDtypeStruct((tokens, D), low),
            jax.ShapeDtypeStruct((D, tokens), low),
            jax.ShapeDtypeStruct((2 * HEAD, tokens), f32),
            jax.ShapeDtypeStruct((blocks - 1, 2 * HEAD, tokens), low),
        ],
        compiler_params=pltpu.CompilerParams(vmem_limit_bytes=VMEM_LIMIT),
        cost_estimate=pl.CostEstimate(
            flops=4 * 7 * tokens * HEADS * blocks * length * HEAD * 2, bytes_accessed=8 << 20, transcendentals=0
        ),
        name="attention",
    )(q_t, do_t, start, cosine, sine, kv)


def feed_kernel(depths, n_ref, dy_ref, far_ref, near_ref, bias_far_ref, bias_near_ref, *refs):
    before = refs[: len(refs) - 11]
    out_ref, dn_ref, far_grad_ref, near_grad_ref, bias_far_grad_ref, bias_near_grad_ref = refs[-11:-5]
    weights, far_sum, near_sum, held, sems = refs[-5:]
    plane = weights.shape[2]
    last = (((1,), (1,)), ((), ()))
    first = (((0,), (0,)), ((), ()))
    loads = []
    for side, ref in enumerate((far_ref, near_ref)):
        loads.append(
            [
                pltpu.make_async_copy(
                    ref.at[:, k, pl.ds(depths[0], len(depths)), pl.ds(0, weights.shape[4])], weights.at[side, :, k], sems.at[side, k]
                )
                for k in range(plane)
            ]
        )
    fetches = [pltpu.make_async_copy(ref, held.at[k], sems.at[2, k]) for k, ref in enumerate(before)]
    for copy in loads[0] + loads[1] + fetches:
        copy.start()
    normed, d_out = n_ref[...], dy_ref[...]
    units = far_sum.shape[1]
    out, d_normed = 0.0, 0.0
    stores = []
    for side, (bias_ref, bias_grad_ref, buffer, grad_ref) in enumerate(
        (
            (bias_far_ref, bias_far_grad_ref, far_sum, far_grad_ref),
            (bias_near_ref, bias_near_grad_ref, near_sum, near_grad_ref),
        )
    ):
        for copy in loads[side]:
            copy.wait()
        up, down = weights[side, 0].reshape(units, D), weights[side, 1].reshape(units, D)
        hidden = lax.dot_general(normed, up, last, preferred_element_type=f32) + bias_ref[...]
        share = 0.5 * (1.0 + lax.erf(hidden * (0.5**0.5)))
        slope = share + hidden * (jnp.exp(-0.5 * hidden * hidden) * (0.5 / 3.141592653589793) ** 0.5)
        active = (hidden * share).astype(low)
        d_active = lax.dot_general(d_out, down, last, preferred_element_type=f32)
        d_hidden = (d_active * slope).astype(low)
        for k, part in enumerate(
            (
                lax.dot_general(d_hidden, normed, first, preferred_element_type=f32),
                lax.dot_general(active, d_out, first, preferred_element_type=f32),
            )
        ):
            buffer[k] = part.astype(buffer.dtype)
            copy = pltpu.make_async_copy(buffer.at[k], grad_ref.at[k], sems.at[3, 2 * side + k])
            copy.start()
            stores.append(copy)
        bias_grad_ref[...] = jnp.sum(d_hidden.astype(f32), axis=0, keepdims=True)
        out = out + jnp.dot(active, down, preferred_element_type=f32)
        d_normed = d_normed + jnp.dot(d_hidden, up, preferred_element_type=f32)
    for copy in fetches:
        copy.wait()
    out_ref[...] = held[0] + out if before else out
    dn_ref[...] = held[1] + d_normed if before else d_normed
    for copy in stores:
        copy.wait()


def feed(normed, d_out, far, near, bias_far, bias_near, depths, rows, before):
    tokens = normed.shape[0]
    plane = far.shape[1]
    units = plane * len(depths) * rows
    before = before or []
    vmem, hbm = pl.BlockSpec(memory_space=pltpu.VMEM), pl.BlockSpec(memory_space=pl.ANY)
    return pl.pallas_call(
        functools.partial(feed_kernel, depths),
        in_specs=[vmem, vmem, hbm, hbm, vmem, vmem] + [hbm] * len(before),
        out_specs=[vmem, vmem, hbm, hbm, vmem, vmem],
        out_shape=[
            jax.ShapeDtypeStruct((tokens, D), f32),
            jax.ShapeDtypeStruct((tokens, D), f32),
            jax.ShapeDtypeStruct((2, units, D), low),
            jax.ShapeDtypeStruct((2, units, D), f32),
            jax.ShapeDtypeStruct((1, units), f32),
            jax.ShapeDtypeStruct((1, units), f32),
        ],
        scratch_shapes=[
            pltpu.VMEM((2, 2, plane, len(depths), rows, D), low),
            pltpu.VMEM((2, units, D), low),
            pltpu.VMEM((2, units, D), f32),
            pltpu.VMEM((2, tokens, D), f32),
            pltpu.SemaphoreType.DMA((4, max(plane, 4))),
        ],
        compiler_params=pltpu.CompilerParams(vmem_limit_bytes=FEED_VMEM),
        cost_estimate=pl.CostEstimate(flops=4 * 24 * tokens * units * D, bytes_accessed=8 << 20, transcendentals=0),
        name="feed",
    )(normed, d_out, far, near, bias_far, bias_near, *before)


def head_kernel(
    vec_len, group_pieces, offset, out_rows, device_ref, x_ref, near_ref, far_ref, cos_ref, sin_ref, n_one_ref, n_two_ref,
    q_ref, kv_ref, w_ref, gain_ref, bias_ref, *refs
):
    *bias_refs, out_ref, flat, units, held, pieces_of, outs_of, sems = refs if out_rows else (*refs[:-6], None, *refs[-6:])
    _, _, plane, depth, size, _ = held.shape
    copies = [
        pltpu.make_async_copy(ref.at[:, :, :, pl.ds(offset, size)], held.at[side], sems.at[side])
        for side, ref in enumerate((near_ref, far_ref))
    ]
    for copy in copies:
        copy.start()
    x = x_ref[...].astype(f32)
    center = x - jnp.mean(x, axis=-1, keepdims=True)
    xhat = center * lax.rsqrt(jnp.mean(center * center, axis=-1, keepdims=True) + layer_eps)
    for copy in copies:
        copy.wait()
    for side in range(2):
        for k in range(plane):
            for z in range(depth):
                number = device_ref[(side * plane + k) * depth + z]
                pieces_of[number] = held[side, 0, k, z].astype(f32)
                if out_rows:
                    outs_of[number] = held[side, 1, k, z][:out_rows].astype(f32)
    if out_rows:
        out_ref[...] = outs_of[...].reshape(out_ref.shape).astype(low)
    shards_of = (flat.shape[1]) // vec_len
    rows = (D + 2 * HEAD) // shards_of
    whole = pieces_of[...].reshape(shards_of, -1, D)
    for s in range(shards_of):
        left, row = vec_len, rows
        while left > 0:
            size = min(left, D)
            begin = s * vec_len + (row - rows) * D
            flat[:, begin : begin + size] = whole[s, row : row + 1, :size]
            left -= size
            row += 1
    vector = lambda begin, size: flat[:, begin : begin + size]
    gain_one, shift_one, gain_two, shift_two = [vector(k * D, D) for k in range(4)]
    gain_ref[0:1] = gain_one
    gain_ref[1:2] = gain_two
    qkv_bias = vector(4 * D, D + 2 * HEAD)
    offset = 4 * D + D + 2 * HEAD
    bias_ref[...] = vector(offset, D) + vector(offset + D + FF, D)
    count, size = units.shape
    for k in range(count):
        units[k : k + 1, :] = vector(offset + D + k * size, size)
    sides = len(bias_refs) // len(group_pieces)
    for k, ref in enumerate(bias_refs):
        side, pieces = k // len(group_pieces), group_pieces[k % len(group_pieces)]
        for i, piece in enumerate(pieces):
            ref[:, i * size : (i + 1) * size] = units[pl.ds(device_ref[side * (count // sides) + piece], 1), :]
    n_one = (xhat * gain_one + shift_one).astype(low)
    n_one_ref[...] = n_one
    n_two_ref[...] = (xhat * gain_two + shift_two).astype(low)
    weight = whole[:, :rows].reshape(shards_of * rows, D).astype(low)
    w_ref[...] = weight
    column = jnp.broadcast_to(qkv_bias, (8, qkv_bias.shape[1])).T[:, 0:1]
    projected = lax.dot_general(weight, n_one, (((1,), (1,)), ((), ())), preferred_element_type=f32) + column
    cosine, sine = cos_ref[...], sin_ref[...]
    half = ROT // 2

    def turned(first):
        a, b = projected[first : first + half], projected[first + half : first + ROT]
        rest = projected[first + ROT : first + HEAD]
        return jnp.concatenate([a * cosine - b * sine, b * cosine + a * sine, rest], axis=0).astype(low)

    for h in range(HEADS):
        q_ref[h * HEAD : (h + 1) * HEAD, :] = turned(h * HEAD) * jnp.asarray(HEAD ** (-0.5), low)
    kv_ref[:HEAD, :] = turned(D)
    kv_ref[HEAD:, :] = projected[D + HEAD :].astype(low)


def head(device, x, near, far, offset, size, out_rows, cosine, sine, group_pieces, vec_len, shards_of):
    tokens = x.shape[0]
    count = device.shape[0]
    _, plane, depth = near.shape[:3]
    width = FF // count
    vmem, hbm = pl.BlockSpec(memory_space=pltpu.VMEM), pl.BlockSpec(memory_space=pl.ANY)
    bias_rows = [jax.ShapeDtypeStruct((1, len(pieces) * width), f32) for pieces in group_pieces] * 2
    return pl.pallas_call(
        functools.partial(head_kernel, vec_len, group_pieces, offset, out_rows),
        in_specs=[pl.BlockSpec(memory_space=pltpu.SMEM), vmem, hbm, hbm, vmem, vmem],
        out_shape=[
            jax.ShapeDtypeStruct((tokens, D), low),
            jax.ShapeDtypeStruct((tokens, D), low),
            jax.ShapeDtypeStruct((D, tokens), low),
            jax.ShapeDtypeStruct((2 * HEAD, tokens), low),
            jax.ShapeDtypeStruct((D + 2 * HEAD, D), low),
            jax.ShapeDtypeStruct((2, D), f32),
            jax.ShapeDtypeStruct((1, D), f32),
            *bias_rows,
        ]
        + [jax.ShapeDtypeStruct((D, D), low)] * (out_rows > 0),
        scratch_shapes=[
            pltpu.VMEM((1, shards_of * vec_len), f32),
            pltpu.VMEM((count, width), f32),
            pltpu.VMEM((2, 2, plane, depth, size, D), low),
            pltpu.VMEM((count, size, D), f32),
            pltpu.VMEM((count, max(out_rows, 8), D), f32),
            pltpu.SemaphoreType.DMA((2,)),
        ],
        compiler_params=pltpu.CompilerParams(vmem_limit_bytes=FEED_VMEM),
        cost_estimate=pl.CostEstimate(flops=4 * 2 * tokens * 896 * D, bytes_accessed=8 << 20, transcendentals=0),
        name="head",
    )(device, x, near, far, cosine, sine)


def back_kernel(dq_ref, dkv_ref, cos_ref, sin_ref, w_ref, n_ref, grad_ref, dn_ref, sum_ref):
    shards_of = grad_ref.shape[0]
    rows = (D + 2 * HEAD) // shards_of
    d_kv = dkv_ref[...]
    a, b = d_kv[: ROT // 2], d_kv[ROT // 2 : ROT]
    cosine, sine = cos_ref[...], sin_ref[...]
    d_kv = jnp.concatenate([a * cosine + b * sine, b * cosine - a * sine, d_kv[ROT:]], axis=0).astype(low)
    d_proj = jnp.concatenate([dq_ref[...], d_kv], axis=0)
    weight = w_ref[...]
    grad = jnp.dot(d_proj, n_ref[...], preferred_element_type=f32)
    grad_ref[...] = jnp.zeros_like(grad_ref)
    for s in range(shards_of):
        grad_ref[s, :rows, :] = grad[s * rows : (s + 1) * rows]
    dn_ref[...] = lax.dot_general(d_proj, weight, (((0,), (0,)), ((), ())), preferred_element_type=f32)
    ones = jnp.ones((8, d_proj.shape[1]), low)
    sum_ref[...] = lax.dot_general(ones, d_proj, (((1,), (1,)), ((), ())), preferred_element_type=f32)[0:1]


def back(dq_t, dkv, cosine, sine, weight, normed, shards_of, padded):
    tokens = normed.shape[0]
    width = D + 2 * HEAD
    return pl.pallas_call(
        back_kernel,
        out_shape=[
            jax.ShapeDtypeStruct((shards_of, padded, D), f32),
            jax.ShapeDtypeStruct((tokens, D), f32),
            jax.ShapeDtypeStruct((1, width), f32),
        ],
        compiler_params=pltpu.CompilerParams(vmem_limit_bytes=VMEM_LIMIT),
        cost_estimate=pl.CostEstimate(flops=4 * 4 * tokens * 896 * D, bytes_accessed=8 << 20, transcendentals=0),
        name="back",
    )(dq_t, dkv, cosine, sine, weight, normed)


def tail_kernel(group_pieces, entry_ref, x_ref, dy_ref, d_one_ref, d_two_ref, gain_ref, sum_ref, *refs):
    bias_refs, (in_grad_ref, flat, units) = refs[:-3], refs[-3:]
    d_one, d_two = d_one_ref[...], d_two_ref[...]
    x = x_ref[...].astype(f32)
    dy = dy_ref[...].astype(f32)
    center = x - jnp.mean(x, axis=-1, keepdims=True)
    inv_sigma = lax.rsqrt(jnp.mean(center * center, axis=-1, keepdims=True) + layer_eps)
    xhat = center * inv_sigma
    d_hat = d_one * gain_ref[0:1] + d_two * gain_ref[1:2]
    d_in = (
        d_hat - jnp.mean(d_hat, axis=-1, keepdims=True) - xhat * jnp.mean(d_hat * xhat, axis=-1, keepdims=True)
    ) * inv_sigma
    in_grad_ref[...] = (dy + d_in).astype(low)
    columns = lambda v: jnp.sum(v, axis=0, keepdims=True)
    dy_column = columns(dy)
    pieces = [columns(d_one * xhat), columns(d_one), columns(d_two * xhat), columns(d_two)]
    pieces += [sum_ref[...], dy_column, None, dy_column]
    count, size = units.shape
    sides = len(bias_refs) // len(group_pieces)
    for k, ref in enumerate(bias_refs):
        side, members = k // len(group_pieces), group_pieces[k % len(group_pieces)]
        for i, member in enumerate(members):
            place = side * (count // sides) + member
            units[place : place + 1, :] = ref[:, i * size : (i + 1) * size]
    offset = 0
    for piece in pieces:
        if piece is None:
            for k in range(count):
                flat[:, offset : offset + size] = units[pl.ds(entry_ref[k], 1), :]
                offset += size
        else:
            flat[:, offset : offset + piece.shape[1]] = piece
            offset += piece.shape[1]


def tail(entry, x, dy, d_one, d_two, gains, proj_sum, bias_grads, group_pieces, total):
    tokens = x.shape[0]
    count = entry.shape[0]
    operands = (entry, x, dy, d_one, d_two, gains, proj_sum, *sum(bias_grads, []))
    return pl.pallas_call(
        functools.partial(tail_kernel, group_pieces),
        in_specs=[pl.BlockSpec(memory_space=pltpu.SMEM)] + [pl.BlockSpec(memory_space=pltpu.VMEM)] * (len(operands) - 1),
        out_shape=[jax.ShapeDtypeStruct((tokens, D), low), jax.ShapeDtypeStruct((1, total), f32)],
        scratch_shapes=[pltpu.VMEM((count, FF // count), f32)],
        compiler_params=pltpu.CompilerParams(vmem_limit_bytes=VMEM_LIMIT),
        cost_estimate=pl.CostEstimate(flops=4 * tokens * 896 * D, bytes_accessed=8 << 20, transcendentals=0),
        name="tail",
    )(*operands)


def split_low(value):
    high = value.astype(low)
    return high, (value - high.astype(f32)).astype(low)


def update_step(across, grad, high, rest, w_ref, first_ref, second_ref, grad_ref, first_new_ref, second_new_ref, w_new_ref):
    rotated = jnp.dot(grad, high, preferred_element_type=f32) + jnp.dot(grad, rest, preferred_element_type=f32)
    grad = grad.astype(f32)
    if across:
        rotated, grad = rotated.T, grad.T
    grad_ref[...] = grad
    ratio, first_new, second_new = moments(rotated, first_ref[...], second_ref[...])
    first_new_ref[...] = first_new
    second_new_ref[...] = second_new
    r_high, r_rest = split_low(ratio)
    if across:
        product = lambda r, b: jnp.dot(b, r, preferred_element_type=f32)
    else:
        product = lambda r, b: lax.dot_general(r, b, (((1,), (1,)), ((), ())), preferred_element_type=f32)
    unrotated = product(r_high, high) + (product(r_high, rest) + product(r_rest, high))
    w_new_ref[...] = w_ref[...] - matrix_rate * unrotated


def update_kernel(across, number, grad_ref, bases_ref, *refs):
    *refs, basis, sem = refs
    copy = pltpu.make_async_copy(bases_ref.at[number], basis, sem)
    copy.start()
    copy.wait()
    high, rest = split_low(basis[...])
    update_step(across, grad_ref[...], high, rest, *refs)


def update(grad, bases, number, weight, first, second, across=False):
    vmem = pl.BlockSpec(memory_space=pltpu.VMEM)
    return pl.pallas_call(
        functools.partial(update_kernel, across, number),
        in_specs=[vmem, pl.BlockSpec(memory_space=pl.ANY), vmem, vmem, vmem],
        out_shape=[jax.ShapeDtypeStruct(weight.shape, f32)] * 4,
        scratch_shapes=[pltpu.VMEM((D, D), f32), pltpu.SemaphoreType.DMA(())],
        compiler_params=pltpu.CompilerParams(vmem_limit_bytes=UPDATE_VMEM),
        cost_estimate=pl.CostEstimate(flops=10 * grad.shape[0] * D * D, bytes_accessed=8 << 20, transcendentals=0),
        name="update",
    )(grad, bases, weight, first, second)


def shards(
    inputs,
    cotangent,
    doc_lengths,
    qkv_weight,
    out_weight,
    up_weight,
    down_weight,
    vectors,
    bases,
    qkv_first,
    out_first,
    up_first,
    down_first,
    vector_first,
    qkv_second,
    out_second,
    up_second,
    down_second,
    vector_second,
):
    seq_count, batch_count = lax.axis_size("seq"), lax.axis_size("batch")
    seq_index, batch_index = lax.axis_index("seq"), lax.axis_index("batch")
    row_count, shard_len = inputs.shape[:2]
    tokens = row_count * shard_len
    y_bit, *z_bits = bit_names("seq", seq_count)
    core_bit, *x_bits = bit_names("batch", batch_count)
    near = [core_bit] + x_bits[::-1] + [y_bit] + z_bits[::-1]
    depth = seq_count // 2
    plane = 2 ** (len(x_bits) + 1)
    group_depths = (range(depth // 2, depth), range(depth // 2))
    group_pieces = [[k * depth + z for k in range(plane) for z in depths] for depths in group_depths]
    x_low = inputs.reshape(tokens, D)
    dy = cotangent.reshape(tokens, D)

    first_pos = seq_index * shard_len
    query_pos = first_pos + jnp.arange(shard_len, dtype=jnp.int32)
    docs = doc_lengths.shape[1]
    earlier = jnp.arange(docs)[:, None] < jnp.arange(docs)[None, :]
    doc_starts = jnp.sum(jnp.where(earlier[None], doc_lengths[:, :, None], 0), axis=1)
    start = jnp.max(
        jnp.where(doc_starts[:, None, :] <= query_pos[None, :, None], doc_starts[:, None, :], 0), axis=-1
    )
    offsets = (query_pos[None, :] - start).reshape(tokens)
    inverse = 1.0 / rope_base ** (jnp.arange(0, ROT, 2).astype(f32) / ROT)
    angles = offsets.astype(f32)[None, :] * inverse[:, None]
    cosine, sine = jnp.cos(angles), jnp.sin(angles)
    start_here = (start - first_pos).astype(jnp.int32)[:, None, :]
    number = jnp.arange(seq_count * batch_count, dtype=jnp.int32)

    def bits_of(value, place_of):
        total = 0
        for k, (axis_name, step) in enumerate(near[::-1]):
            total = total + place_of(value, k, axis_name, step)
        return total

    differs = {"seq": (number // batch_count) ^ seq_index, "batch": (number % batch_count) ^ batch_index}
    entry = bits_of(number, lambda v, k, name, step: (differs[name] // step) % 2 << k).astype(jnp.int32)
    xor_of = lambda name: sum((number >> k) % 2 * step for k, (axis_name, step) in enumerate(near[::-1]) if axis_name == name)
    device = ((xor_of("seq") ^ seq_index) * batch_count + (xor_of("batch") ^ batch_index)).astype(jnp.int32)

    qkv_rows, out_rows, up_rows, vec_len = qkv_weight.shape[0], out_weight.shape[0], up_weight.shape[0], vectors.shape[0]
    vec_rows = -(-vec_len // D)
    used = qkv_rows + vec_rows
    head_rows = -(-used // (8 * batch_count)) * 8 * batch_count
    vec_pad = vec_rows * D - vec_len

    def own_part(rows):
        size = rows.shape[0] // batch_count
        return lax.dynamic_slice_in_dim(rows, batch_index * size, size, axis=0)

    head_shard = jnp.concatenate(
        [qkv_weight, jnp.pad(vectors, (0, vec_pad)).reshape(vec_rows, D), jnp.zeros((head_rows - used, D), f32)], axis=0
    ).astype(low)
    head_part_rows = head_rows // batch_count
    unit_rows = up_rows // batch_count
    out_own = out_rows // batch_count
    part = jnp.concatenate(
        [
            own_part(up_weight.astype(low)),
            own_part(head_shard),
            own_part(down_weight.T.astype(low)),
            own_part(out_weight.astype(low)),
            jnp.zeros((head_part_rows - out_own, D), low),
        ],
        axis=0,
    )
    parts, cosine, sine, start_here, entry, device = lax.optimization_barrier(
        (jnp.stack(gather_z(part)), cosine, sine, start_here, entry, device)
    )
    half = part.shape[0] // 2
    up_near, down_near = parts[:, :half], parts[:, half:]
    up_near = gather_bit(up_near, y_bit, 0)
    for bit in x_bits:
        down_near = gather_bit(down_near, bit, 0)
    for bit in x_bits:
        up_near = gather_bit(up_near, bit, 0)
    down_near = gather_bit(down_near, y_bit, len(x_bits))
    near_all = jnp.stack([up_near, down_near]).reshape(2, plane, depth, half, D)
    far_all = swap(near_all, core_bit)
    aligned = unit_rows % 16 == 0 and head_part_rows % 16 == 0
    trim = lambda value, begin, end: value if aligned else value[..., begin:end, :]
    near_weight, far_weight = trim(near_all, 0, unit_rows), trim(far_all, 0, unit_rows)

    inside = out_own % 8 == 0
    normed_one, normed_two, q_t, kv_own, qkv_full, gains, out_bias, *bias_rows = head(
        device, x_low, trim(near_all, unit_rows, half), trim(far_all, unit_rows, half), unit_rows if aligned else 0,
        head_part_rows, out_own if inside else 0, cosine, sine, group_pieces, vec_len, seq_count,
    )
    if inside:
        out_full = bias_rows.pop()
    else:
        out_full = jnp.concatenate([v[1, ..., unit_rows : unit_rows + out_own, :] for v in (near_all, far_all)], axis=0)
        chosen = (entry[:, None] == number[None, :]).astype(low)
        out_full = jnp.dot(chosen, out_full.reshape(-1, out_own * D), preferred_element_type=f32).astype(low).reshape(D, D)
    bias_rows = [bias_rows[: len(group_pieces)], bias_rows[len(group_pieces) :]]
    reach = seq_count // 2

    def shifted(value, step, back=False):
        pairs = [(j, j + step) for j in range(seq_count - step)]
        return lax.ppermute(value, "seq", [(b, a) for a, b in pairs] if back else pairs)

    kv = kv_own[None]
    farthest = shifted(kv_own, reach)
    pair = shifted(kv, 1)
    kv = jnp.concatenate([kv, pair], axis=0)
    while kv.shape[0] < reach:
        kv = jnp.concatenate([kv, shifted(kv, kv.shape[0])], axis=0)
    kv = jnp.concatenate([kv, farthest[None]], axis=0)

    last = (((1,), (1,)), ((), ()))
    bias_grads, halves_of = [[], []], []

    def feed_group(g, sums, *earlier):
        depths = group_depths[g]
        *sums, far_grad, near_grad, bias_far, bias_here = feed(
            flow(normed_two, *earlier), dy, far_weight, near_weight, bias_rows[1][g], bias_rows[0][g], depths, unit_rows, sums
        )
        bias_grads[0].append(bias_here)
        bias_grads[1].append(bias_far)
        grad_sum = near_grad + swap(far_grad, core_bit).astype(f32)
        half_shape = (2,) * len(x_bits) + (2, len(depths), unit_rows, D)
        halves_of.append(
            [
                split_bit(grad_sum[0].reshape(half_shape), x_bits[-1], 0),
                split_bit(grad_sum[1].reshape(half_shape), y_bit, len(x_bits)),
            ]
        )
        return sums

    def feed_first(halves):
        (up_kept, up_sent), (down_kept, down_sent) = halves
        up_sum = up_kept + swap(up_sent, x_bits[-1]).astype(f32)
        for bit in x_bits[-2::-1]:
            up_sum = sum_bit(up_sum, bit, 0)
        return up_sum, down_kept + swap(down_sent, y_bit).astype(f32)

    def feed_halves(up_sum, down_sum):
        return split_bit(up_sum, y_bit, 0), split_bit(down_sum, x_bits[-1], 0)

    def feed_second(halves, after):
        (up_kept, up_sent), (down_kept, down_sent) = halves
        up_sum = up_kept + flow(swap(up_sent, y_bit), *after).astype(f32)
        down_sum = down_kept + flow(swap(down_sent, x_bits[-1]), *after).astype(f32)
        for bit in x_bits[-2::-1]:
            down_sum = sum_bit(down_sum, bit, 0, after=after)
        return jnp.concatenate([up_sum, down_sum], axis=1)

    sums = feed_group(0, None, pair, farthest)
    first_sent = (halves_of[0][0][1], halves_of[0][1][1])

    do_t = lax.dot_general(out_full, dy, (((0,), (1,)), ((), ())), preferred_element_type=f32).astype(low)
    context, dq_t, dkv_own, dkv_sent = attention(flow(q_t, *first_sent), do_t, start_here, cosine, sine, kv)
    first_halves = feed_halves(*feed_first(halves_of[0]))
    mlp_out, d_normed_two = feed_group(1, sums, dq_t, first_halves[0][1], first_halves[1][1])

    dkv_far = flow(shifted(dkv_sent[reach - 1], reach, True), d_normed_two)
    dkv = jnp.concatenate([dkv_own[None], dkv_sent[: reach - 1].astype(f32)], axis=0)
    while dkv.shape[0] > 1:
        both = dkv.shape[0] // 2
        dkv = dkv[:both] + flow(shifted(dkv[both:].astype(low), both, True), d_normed_two).astype(f32)
    dkv = dkv[0] + dkv_far.astype(f32)

    last_step = feed_second(first_halves, (d_normed_two,))
    dkv, last_step = lax.optimization_barrier((dkv, last_step))
    last_steps = [last_step]

    shape = (depth, 2) + (2,) * len(x_bits) + (2, -1, D)
    qkv_own = -(-qkv_rows // (8 * batch_count)) * 8
    qkv_part, d_normed_one, proj_sum = back(
        dq_t, dkv, cosine, sine, qkv_full, normed_one, seq_count, qkv_own * batch_count
    )
    out_part = lax.dot_general(dy, context, (((0,), (0,)), ((), ())), preferred_element_type=f32)
    both = jnp.concatenate([qkv_part.reshape(shape), out_part.reshape(shape)], axis=len(shape) - 2)
    both = sum_bit(both, core_bit, len(shape) - 3, True)

    def spread(part):
        value = part.astype(low)
        for k, bit in enumerate(x_bits):
            value = gather_bit(value, bit, 0, True)
        value = gather_bit(value, core_bit, len(x_bits), True)
        return value.reshape(batch_count, -1, D)

    qkv_sum, out_sum = both[..., :qkv_own, :], both[..., qkv_own:, :]
    for bit in x_bits[::-1]:
        qkv_sum = sum_bit(qkv_sum, bit, 2, True)
    out_sum = sum_bit(out_sum, y_bit, 1, True)
    sent = (halves_of[1][0][1], halves_of[1][1][1])
    input_grad, vector_part = tail(
        entry, x_low, dy, d_normed_one, flow(d_normed_two, *sent), gains, proj_sum, bias_grads, group_pieces,
        seq_count * vec_len,
    )
    vector_parts = lax.all_gather(vector_part[0], ("seq", "batch"))
    qkv_sum = sum_bit(qkv_sum, y_bit, 1, True, after=sent)
    for bit in x_bits[::-1]:
        out_sum = sum_bit(out_sum, bit, 1, True, after=sent)
    both = sum_z(jnp.concatenate([qkv_sum, out_sum], axis=1), True)
    second_halves = feed_halves(*feed_first(halves_of[1]))
    last_steps.append(feed_second(second_halves, (both, vector_part)))
    feed_sum = 0.0
    for depths, last_step in zip(group_depths, last_steps):
        for k, z in enumerate(depths):
            feed_sum = feed_sum + (last_step[k] if z == 0 else swap_z(last_step[k].astype(low), z).astype(f32))
    others = spread(both)
    qkv_low = others[:, :qkv_own].reshape(-1, D)[:qkv_rows]
    out_low = others[:, qkv_own:].reshape(-1, D)
    out_grad, *out_states = update(out_low, bases, 1, out_weight, out_first, out_second)
    qkv_grad, *qkv_states = update(qkv_low, bases, 0, qkv_weight, qkv_first, qkv_second)
    attn_out = lax.dot_general(context, out_full, last, preferred_element_type=f32)
    outputs = (x_low.astype(f32) + attn_out + flow(mlp_out, both) + out_bias).astype(low)
    feed_grads = spread(flow(feed_sum, out_grad, qkv_grad, outputs))
    up_low = feed_grads[:, :unit_rows].reshape(-1, D)
    down_low = feed_grads[:, unit_rows:].reshape(-1, D)
    up_grad, *up_states = update(up_low, bases, 2, up_weight, up_first, up_second)
    down_grad, *down_states = update(down_low, bases, 3, down_weight, down_first, down_second, True)
    vector_grad = jnp.sum(lax.dynamic_slice_in_dim(vector_parts, seq_index * vec_len, vec_len, axis=1), axis=0)
    vector_new, *vector_states = adam_step(vectors, vector_grad, vector_first, vector_second)
    states = (qkv_states, out_states, up_states, down_states, (*vector_states, vector_new))
    return (
        outputs.reshape(inputs.shape),
        input_grad.reshape(inputs.shape),
        qkv_grad,
        out_grad,
        up_grad,
        down_grad,
        vector_grad,
        *(state[0] for state in states),
        *(state[1] for state in states),
        *(state[2] for state in states),
    )


def solution(mesh):
    tokens = P("batch", "seq", None)
    rows, columns, flat = P("seq", None), P(None, "seq"), P("seq")
    params = (rows, rows, rows, columns, flat)
    return jax.shard_map(
        shards,
        mesh=mesh,
        in_specs=(tokens, tokens, P("batch", None)) + params + (P(),) + params + params,
        out_specs=(tokens, tokens) + params * 4,
        check_vma=False,
    )
```

profile of v0, /device:TPU:0, one launch (start us, length us, event | category | flops | bytes accessed | tf_op | source)
XLA Modules:
  0.0 393.0 jit_solution(6309918053857043750)
XLA Ops:
  11.5 3.1 collective-permute-start
  14.5 2.6 collective-permute-start.1
  19.2 12.1 %collective-permute-done = bf16[256,768]{0,1:T(8,128)(2,1)S(1)} collective-permute-done((bf16[256,768]{0,1:T(8,128)(2,1)S(1)}, bf16[256,768]{0,1:T(8,128)(2,1)S(1)}, u32[]{:S(2)}, u32[]{:S(2)}) %collective-permute-start) | collective-permute-done | bytes 393248 | tf_op jit(solution)/shard_map/ppermute | solution.py:48
  31.3 13.0 %collective-permute-done.1 = bf16[256,768]{0,1:T(8,128)(2,1)S(1)} collective-permute-done((bf16[256,768]{0,1:T(8,128)(2,1)S(1)}, bf16[256,768]{0,1:T(8,128)(2,1)S(1)}, u32[]{:S(2)}, u32[]{:S(2)}) %collective-permute-start.1) | collective-permute-done | bytes 393248 | tf_op jit(solution)/shard_map/ppermute | solution.py:48
  45.2 1.6 collective-permute-start.3
  46.7 1.5 collective-permute-start.5
  48.2 13.8 %collective-permute-done.3 = bf16[4,128,768]{1,2,0:T(8,128)(2,1)S(1)} collective-permute-done((bf16[4,128,768]{1,2,0:T(8,128)(2,1)S(1)}, bf16[4,128,768]{1,2,0:T(8,128)(2,1)S(1)}, u32[]{:S(2)}, u32[]{:S(2)}) %collective-permute-start.3) | collective-permute-done | bytes 786464 | tf_op jit(solution)/shard_map/ppermute | solution.py:34
  62.2 1.6 collective-permute-start.4
  65.1 1.4 fusion.78
  66.7 30.3 %collective-permute-done.4 = bf16[2,4,128,768]{2,3,1,0:T(8,128)(2,1)S(1)} collective-permute-done((bf16[2,4,128,768]{2,3,1,0:T(8,128)(2,1)S(1)}, bf16[2,4,128,768]{2,3,1,0:T(8,128)(2,1)S(1)}, u32[]{:S(2)}, u32[]{:S(2)}) %collective-permute-start.4) | collective-permute-done | bytes 1572896 | tf_op jit(solution)/shard_map/ppermute | solution.py:34
  97.0 1.9 pad_maximum_fusion.1
  98.9 4.7 %copy.91 = bf16[2,2,4,128,768]{4,3,2,1,0:T(8,128)(2,1)} copy(bf16[2,2,4,128,768]{3,4,2,1,0:T(8,128)(2,1)} %pad_maximum_fusion.1) | data formatting | bytes 6291456 | tf_op jit(solution)/shard_map/stack | solution.py:66
  103.6 3.4 pad_maximum_fusion.2
  106.9 4.7 %copy.92 = bf16[2,2,4,128,768]{4,3,2,1,0:T(8,128)(2,1)} copy(bf16[2,2,4,128,768]{3,4,2,0,1:T(8,128)(2,1)} %pad_maximum_fusion.2) | data formatting | bytes 6291456 | tf_op jit(solution)/shard_map/stack | solution.py:66
  111.7 3.4 pad_maximum_fusion.near_ref
  115.1 2.6 copy-done.15
  117.7 10.2 %collective-permute-done.7.far_ref = bf16[2,4,4,128,768]{4,3,2,1,0:T(8,128)(2,1)S(1)} collective-permute-done((bf16[2,4,4,128,768]{4,3,2,1,0:T(8,128)(2,1)S(1)}, bf16[2,4,4,128,768]{4,3,2,1,0:T(8,128)(2,1)S(1)}, u32[]{:S(2)}, u32[]{:S(2)}) %collective-permute-start.7) | collective-permute-done | bytes 6291488 | tf_op jit(solution)/shard_map/ppermute | solution.py:34
  127.9 2.7 copy-done.18
  130.6 6.5 %head.1 = (bf16[512,768]{1,0:T(8,128)(2,1)}, bf16[512,768]{1,0:T(8,128)(2,1)}, bf16[768,512]{1,0:T(8,128)(2,1)}, bf16[128,512]{1,0:T(8,128)(2,1)}, bf16[896,768]...) custom-call(s32[32]{0:T(128)} %get-tuple-element.94.device_ref, ...), custom_call_target="tpu_custom_call" | custom-call | flops 2818572288 | bytes 8388608 | tf_op jit(solution)/shard_map/head/pallas_call | solution.py:367
  137.0 2.4 collective-permute-start.8
  139.5 12.7 %collective-permute-start.9 = (bf16[128,512]{1,0:T(8,128)(2,1)}, bf16[128,512]{1,0:T(8,128)(2,1)S(1)}, u32[]{:S(2)}, u32[]{:S(2)}) collective-permute-start(bf16[128,512]{1,0:T(8,128)(2,1)} %get-tuple-element.100), channel_id=1, source_target_pairs={{0,16},{4,20},{8,24},{12,28},{1,17},{5,21},{9,25},{13,29},{2,18},{... | collective-permute-start | bytes 393224 | tf_op jit(solution)/shard_map/ppermute | solution.py:644
  152.2 2.6 collective-permute-done.9
  154.8 12.9 %feed.2 = (f32[512,768]{1,0:T(8,128)}, f32[512,768]{1,0:T(8,128)}, bf16[2,768,768]{2,1,0:T(8,128)(2,1)}, f32[2,768,768]{2,1,0:T(8,128)}, f32[1,768]{1,0:T(1,128)}, /*index=5*/f32[1,768]{1,0:T(1,128)}) custom-call(bf16[512,768]{1,0:T(8,128)(2,1)} %get-tuple-element.111.n_ref, bf16[512,768]{1,0:T(8,128)(2,1)} %bitcast.188, ...), custom_call_target="tpu_custom_call" | custom-call | flops 28991029248 | bytes 8388608 | tf_op jit(solution)/shard_map/feed/pallas_call | solution.py:262
  167.8 2.0 collective-permute-start.11
  169.8 3.1 convolution_convert_fusion.do_ref
  173.0 3.0 collective-permute-done.11
  176.9 2.3 convert_add_fusion.1
  180.9 5.1 %collective-permute-start.13 = (bf16[2,2,96,768]{3,2,1,0:T(8,128)(2,1)S(1)}, bf16[2,2,96,768]{3,2,1,0:T(8,128)(2,1)}, u32[]{:S(2)}, u32[]{:S(2)}) collective-permute-start(bf16[2,2,96,768]{3,2,1,0:T(8,128)(2,1)S(1)} %fusion.12), channel_id=1, source_target_pairs={{0,4},{4,0},{8,12},{12,8},{16,20},{20,16},{24,28},{28,24},{1,5},{5... | collective-permute-start | bytes 1769480 | tf_op jit(solution)/shard_map/ppermute | solution.py:34
  185.9 1.5 collective-permute-start.12
  187.4 18.3 %attention.1 = (bf16[512,768]{1,0:T(8,128)(2,1)}, bf16[768,512]{1,0:T(8,128)(2,1)}, f32[128,512]{1,0:T(8,128)}, bf16[4,128,512]{2,1,0:T(8,128)(2,1)}) custom-call(bf16[768,512]{1,0:T(8,128)(2,1)} %get-tuple-element.106.q_ref, bf16[768,512]{1,0:T(8,128)(2,1)} %convolution_convert_fusion.do_ref, s32[4,1,128]{2,1,0:T(1,128)} %bitcast.206, ...), custom_call_target="tpu_custom_call" | custom-call | flops 14092861440 | bytes 8388608 | tf_op jit(solution)/shard_map/attention/pallas_call | solution.py:171
  208.1 1.5 collective-permute-start.14
  214.1 13.1 %feed.3 = (f32[512,768]{1,0:T(8,128)}, f32[512,768]{1,0:T(8,128)}, bf16[2,768,768]{2,1,0:T(8,128)(2,1)}, f32[2,768,768]{2,1,0:T(8,128)}, f32[1,768]{1,0:T(1,128)}, /*index=5*/f32[1,768]{1,0:T(1,128)}) custom-call(bf16[512,768]{1,0:T(8,128)(2,1)} %get-tuple-element.111.n_ref, bf16[512,768]{1,0:T(8,128)(2,1)} %bitcast.189, ...), custom_call_target="tpu_custom_call" | custom-call | flops 28991029248 | bytes 8388608 | tf_op jit(solution)/shard_map/feed/pallas_call | solution.py:262
  227.4 1.6 collective-permute-start.15
  230.5 3.9 collective-permute-done.15
  234.4 1.6 fusion.28.dkv_ref
  238.1 5.2 %back.1 = (f32[8,128,768]{2,1,0:T(8,128)}, f32[512,768]{1,0:T(8,128)}, f32[1,896]{1,0:T(1,128)}) custom-call(bf16[768,512]{1,0:T(8,128)(2,1)} %get-tuple-element.110.dq_ref, f32[128,512]{1,0:T(8,128)} %fusion.28.dkv_ref, f32[8,512]{1,0:T(8,128)} %get-tuple-element.96.cos_ref, f32[8,512]{1,0:T(8,128)} %get-tuple-element.97.sin_ref, ...), custom_call_target="tpu_custom_call" | custom-call | flops 5637144576 | bytes 8388608 | tf_op jit(solution)/shard_map/back/pallas_call | solution.py:416
  243.3 2.8 fusion.5
  247.2 3.4 fusion.82
  250.6 2.3 fusion.4
  253.3 2.4 collective-permute-start.23
  257.2 4.9 %collective-permute-start.30 = (bf16[192,768]{1,0:T(8,128)(2,1)}, bf16[192,768]{1,0:T(8,128)(2,1)}, u32[]{:S(2)}, u32[]{:S(2)}) collective-permute-start(bf16[192,768]{1,0:T(8,128)(2,1)} %get-tuple-element.186), channel_id=1, source_target_pairs={{0,16},{4,20},{8,24},{12,28},{16,0},{20,4},{24,8},{28,12},{1,17},{... | collective-permute-start | bytes 884744 | tf_op jit(solution)/shard_map/ppermute | solution.py:48
  262.1 1.5 collective-permute-start.31
  263.7 1.6 collective-permute-start.24
  265.3 2.2 collective-permute-done.20
  267.7 2.3 convert_add_fusion
  274.1 3.4 collective-permute-start.25
  277.5 3.6 collective-permute-start.26
  281.1 5.0 %tail.1 = (bf16[512,768]{1,0:T(8,128)(2,1)}, f32[1,8576]{1,0:T(1,128)}) custom-call(s32[32]{0:T(128)} %get-tuple-element.135.entry_ref, bf16[512,768]{1,0:T(8,128)(2,1)} %bitcast.181, bf16[512,768]{1,0:T(8,128)(2,1)} %bitcast.190, f32[512,768]{1,0:T(8,128)} %get-tuple-element.136.d_one_ref, f32[512,768]{1,0:T(8,128)} %get-tuple-element.137.d_two_ref, ...), custom_call_target="tpu_custom_call" | custom-call | flops 1409286144 | bytes 8388608 | tf_op jit(solution)/shard_map/tail/pallas_call | solution.py:468
  287.2 7.3 %collective-permute-done.26 = bf16[56,768]{1,0:T(8,128)(2,1)} collective-permute-done((bf16[56,768]{1,0:T(8,128)(2,1)}, bf16[56,768]{1,0:T(8,128)(2,1)}, u32[]{:S(2)}, u32[]{:S(2)}) %collective-permute-start.26) | collective-permute-done | bytes 86048 | tf_op jit(solution)/shard_map/ppermute | solution.py:48
  294.5 1.5 collective-permute-start.32
  297.6 2.7 add_convert_fusion
  300.3 9.5 %collective-permute-done.28 = bf16[56,768]{1,0:T(8,128)(2,1)S(1)} collective-permute-done((bf16[56,768]{1,0:T(8,128)(2,1)S(1)}, bf16[56,768]{1,0:T(8,128)(2,1)S(1)}, u32[]{:S(2)}, u32[]{:S(2)}) %collective-permute-start.28) | collective-permute-done | bytes 86048 | tf_op jit(solution)/shard_map/ppermute | solution.py:34
  310.0 1.6 collective-permute-start.35
  312.7 4.1 %collective-permute-done.35 = bf16[2,96,768]{2,1,0:T(8,128)(2,1)S(1)} collective-permute-done((bf16[2,96,768]{2,1,0:T(8,128)(2,1)S(1)}, bf16[2,96,768]{2,1,0:T(8,128)(2,1)S(1)}, u32[]{:S(2)}, u32[]{:S(2)}) %collective-permute-start.35) | collective-permute-done | bytes 294944 | tf_op jit(solution)/shard_map/ppermute | solution.py:34
  316.8 1.7 collective-permute-done.33
  318.7 2.8 collective-permute-start.36
  321.7 3.0 update.5
  324.8 2.8 update.4
  329.4 6.2 %collective-permute-done.37 = bf16[192,768]{1,0:T(8,128)(2,1)S(1)} collective-permute-done((bf16[192,768]{1,0:T(8,128)(2,1)S(1)}, bf16[192,768]{1,0:T(8,128)(2,1)S(1)}, u32[]{:S(2)}, u32[]{:S(2)}) %collective-permute-start.37) | collective-permute-done | bytes 294944 | tf_op jit(solution)/shard_map/ppermute | solution.py:34
  335.8 2.0 collective-permute-done.38
  340.0 3.7 copy-done
  343.7 4.9 %update.6 = (f32[384,768]{1,0:T(8,128)}, f32[384,768]{1,0:T(8,128)}, f32[384,768]{1,0:T(8,128)}, f32[384,768]{1,0:T(8,128)}) custom-call(bf16[384,768]{1,0:T(8,128)(2,1)S(1)} %bitcast.163, f32[4,768,768]{2,1,0:T(8,128)S(1)} %copy-done, f32[384,768]{1,0:T(8,128)S(1)} %copy-done.2, f32[384,768]{1,0:T(8,128)S(1)} %copy-done.4, f32[384,768]{1,0:T(8,128)S(1)} %copy-done.5), custom_call_target="tpu_custom_call" | custom-call | flops 2264924160 | bytes 8388608 | tf_op jit(solution)/shard_map/update/pallas_call | solution.py:513
  348.6 5.2 %update.7 = (f32[768,384]{1,0:T(8,128)}, f32[768,384]{1,0:T(8,128)}, f32[768,384]{1,0:T(8,128)}, f32[768,384]{1,0:T(8,128)}) custom-call(bf16[384,768]{1,0:T(8,128)(2,1)S(1)} %bitcast.162, f32[4,768,768]{2,1,0:T(8,128)S(1)} %copy-done, f32[768,384]{1,0:T(8,128)S(1)} %copy-done.1, f32[768,384]{1,0:T(8,128)S(1)} %copy-done.6, f32[768,384]{1,0:T(8,128)S(1)} %copy-done.7), custom_call_target="tpu_custom_call" | custom-call | flops 2264924160 | bytes 8388608 | tf_op jit(solution)/shard_map/update/pallas_call | solution.py:513
  353.8 30.0 %all-gather.3.cloned.1.call-done = f32[32,1,8576]{2,1,0:T(1,128)} async-done(((f32[1,1,8576]{2,1,0:T(1,128)}), f32[32,1,8576]{2,1,0:T(1,128)}) %all-gather.3.cloned.1.call-update) | async-done | bytes 1097744 | tf_op jit(solution)/shard_map/all_gather | solution.py:736
  (208 shorter events, 39.5 us)
Async XLA Ops:
  7.2 3.4 copy-start.1
  7.2 3.5 copy-start.8
  7.2 376.7 %all-gather.3.cloned.1.call-start = ((), (), s32[]{:S(2)}) async-start(), calls=%async_computation | async-start | bytes 1132032 | tf_op jit(solution)/shard_map/all_gather | solution.py:736
  9.3 7.9 %copy-start.33 = (s32[4,8]{1,0:T(4,128)S(1)}, s32[4,8]{1,0:T(4,128)}, u32[]{:S(2)}) copy-start(s32[4,8]{1,0:T(4,128)} %param.21) | copy-start | bytes 388
  11.5 19.9 %collective-permute-start = (bf16[256,768]{0,1:T(8,128)(2,1)S(1)}, bf16[256,768]{0,1:T(8,128)(2,1)S(1)}, u32[]{:S(2)}, u32[]{:S(2)}) collective-permute-start(bf16[256,768]{0,1:T(8,128)(2,1)S(1)} %concatenate.31), channel_id=1, source_target_pairs={{0,8},{4,12},{8,0},{12,4},{16,24},{20,28},{24,16},{28,20},{1,9},{5... | collective-permute-start | bytes 1179656 | tf_op jit(solution)/shard_map/ppermute | solution.py:48
  14.5 29.8 %collective-permute-start.1 = (bf16[256,768]{0,1:T(8,128)(2,1)S(1)}, bf16[256,768]{0,1:T(8,128)(2,1)S(1)}, u32[]{:S(2)}, u32[]{:S(2)}) collective-permute-start(bf16[256,768]{0,1:T(8,128)(2,1)S(1)} %concatenate.31), channel_id=1, source_target_pairs={{0,16},{4,20},{8,24},{12,28},{16,0},{20,4},{24,8},{28,12},{1,17},{... | collective-permute-start | bytes 1179656 | tf_op jit(solution)/shard_map/ppermute | solution.py:48
  17.1 27.2 %collective-permute-start.2 = (bf16[256,768]{0,1:T(8,128)(2,1)S(1)}, bf16[256,768]{0,1:T(8,128)(2,1)S(1)}, u32[]{:S(2)}, u32[]{:S(2)}) collective-permute-start(bf16[256,768]{0,1:T(8,128)(2,1)S(1)} %concatenate.31), channel_id=1, source_target_pairs={{0,24},{4,28},{8,16},{12,20},{16,8},{20,12},{24,0},{28,4},{1,25},{... | collective-permute-start | bytes 1179656 | tf_op jit(solution)/shard_map/ppermute | solution.py:48
  45.2 16.9 %collective-permute-start.3 = (bf16[4,128,768]{1,2,0:T(8,128)(2,1)S(1)}, bf16[4,128,768]{1,2,0:T(8,128)(2,1)S(1)}, u32[]{:S(2)}, u32[]{:S(2)}) collective-permute-start(bf16[4,128,768]{1,2,0:T(8,128)(2,1)S(1)} %get-tuple-element.174), channel_id=1, source_target_pairs={{0,4},{4,0},{8,12},{12,8},{16,20},{20,16},{24,28},{28,24},{1,5},{5... | collective-permute-start | bytes 2359304 | tf_op jit(solution)/shard_map/ppermute | solution.py:34
  46.7 18.4 %collective-permute-start.5 = (bf16[4,128,768]{1,2,0:T(8,128)(2,1)S(1)}, bf16[4,128,768]{1,2,0:T(8,128)(2,1)S(1)}, u32[]{:S(2)}, u32[]{:S(2)}) collective-permute-start(bf16[4,128,768]{1,2,0:T(8,128)(2,1)S(1)} %get-tuple-element.173), channel_id=1, source_target_pairs={{0,2},{1,3},{2,0},{3,1},{4,6},{5,7},{6,4},{7,5},{8,10},{9,11},{10,... | collective-permute-start | bytes 2359304 | tf_op jit(solution)/shard_map/ppermute | solution.py:34
  62.2 34.7 %collective-permute-start.4 = (bf16[2,4,128,768]{2,3,1,0:T(8,128)(2,1)S(1)}, bf16[2,4,128,768]{2,3,1,0:T(8,128)(2,1)S(1)}, u32[]{:S(2)}, u32[]{:S(2)}) collective-permute-start(bf16[2,4,128,768]{2,3,1,0:T(8,128)(2,1)S(1)} %get-tuple-element.170), channel_id=1, source_target_pairs={{0,2},{1,3},{2,0},{3,1},{4,6},{5,7},{6,4},{7,5},{8,10},{9,11},{10,... | collective-permute-start | bytes 4718600 | tf_op jit(solution)/shard_map/ppermute | solution.py:34
  66.5 37.1 %collective-permute-start.6 = (bf16[2,4,128,768]{2,3,1,0:T(8,128)(2,1)}, bf16[2,4,128,768]{2,3,1,0:T(8,128)(2,1)}, u32[]{:S(2)}, u32[]{:S(2)}) collective-permute-start(bf16[2,4,128,768]{2,3,1,0:T(8,128)(2,1)} %get-tuple-element.176), channel_id=1, source_target_pairs={{0,4},{4,0},{8,12},{12,8},{16,20},{20,16},{24,28},{28,24},{1,5},{5... | collective-permute-start | bytes 4718600 | tf_op jit(solution)/shard_map/ppermute | solution.py:34
  117.7 10.2 %collective-permute-start.7 = (bf16[2,4,4,128,768]{4,3,2,1,0:T(8,128)(2,1)S(1)}, bf16[2,4,4,128,768]{4,3,2,1,0:T(8,128)(2,1)S(1)}, u32[]{:S(2)}, u32[]{:S(2)}) collective-permute-start(bf16[2,4,4,128,768]{4,3,2,1,0:T(8,128)(2,1)S(1)} %pad_maximum_fusion.near_ref), channel_id=1, source_target_pairs={{0,1},{1,0},{2,3},{3,2},{4,5},{5,4},{6,7},{7,6},{8,9},{9,8},{10,11... | collective-permute-start | bytes 18874376 | tf_op jit(solution)/shard_map/ppermute | solution.py:34
  137.0 15.1 %collective-permute-start.8 = (bf16[1,128,512]{2,1,0:T(8,128)(2,1)}, bf16[1,128,512]{2,1,0:T(8,128)(2,1)S(1)}, u32[]{:S(2)}, u32[]{:S(2)}) collective-permute-start(bf16[1,128,512]{2,1,0:T(8,128)(2,1)} %bitcast.197), channel_id=1, source_target_pairs={{0,4},{4,8},{8,12},{12,16},{16,20},{20,24},{24,28},{1,5},{5,9},{9,... | collective-permute-start | bytes 393224 | tf_op jit(solution)/shard_map/ppermute | solution.py:644
  139.5 15.3 %collective-permute-start.9 = (bf16[128,512]{1,0:T(8,128)(2,1)}, bf16[128,512]{1,0:T(8,128)(2,1)S(1)}, u32[]{:S(2)}, u32[]{:S(2)}) collective-permute-start(bf16[128,512]{1,0:T(8,128)(2,1)} %get-tuple-element.100), channel_id=1, source_target_pairs={{0,16},{4,20},{8,24},{12,28},{1,17},{5,21},{9,25},{13,29},{2,18},{... | collective-permute-start | bytes 393224 | tf_op jit(solution)/shard_map/ppermute | solution.py:644
  154.7 13.0 %copy-start.26 = (bf16[128,512]{1,0:T(8,128)(2,1)S(1)}, bf16[128,512]{1,0:T(8,128)(2,1)}, u32[]{:S(2)}) copy-start(bf16[128,512]{1,0:T(8,128)(2,1)} %get-tuple-element.100) | copy-start | bytes 393220
  154.8 15.1 %copy-start.24 = (bf16[4,128,768]{2,1,0:T(8,128)(2,1)S(1)}, bf16[4,128,768]{2,1,0:T(8,128)(2,1)}, u32[]{:S(2)}) copy-start(bf16[4,128,768]{2,1,0:T(8,128)(2,1)} %param.20) | copy-start | bytes 2359300
  167.7 9.2 %collective-permute-start.10 = (bf16[2,768,768]{2,1,0:T(8,128)(2,1)}, bf16[2,768,768]{2,1,0:T(8,128)(2,1)}, u32[]{:S(2)}, u32[]{:S(2)}) collective-permute-start(bf16[2,768,768]{2,1,0:T(8,128)(2,1)} %get-tuple-element.105), channel_id=1, source_target_pairs={{0,1},{1,0},{2,3},{3,2},{4,5},{5,4},{6,7},{7,6},{8,9},{9,8},{10,11... | collective-permute-start | bytes 7077896 | tf_op jit(solution)/shard_map/ppermute | solution.py:34
  167.8 8.2 %collective-permute-start.11 = (bf16[2,128,512]{2,1,0:T(8,128)(2,1)S(1)}, bf16[2,128,512]{2,1,0:T(8,128)(2,1)S(1)}, u32[]{:S(2)}, u32[]{:S(2)}) collective-permute-start(bf16[2,128,512]{2,1,0:T(8,128)(2,1)S(1)} %pad_maximum_fusion.13), channel_id=1, source_target_pairs={{0,8},{4,12},{8,16},{12,20},{16,24},{20,28},{1,9},{5,13},{9,17},{1... | collective-permute-start | bytes 786440 | tf_op jit(solution)/shard_map/ppermute | solution.py:644
  169.8 7.1 %copy-start.19 = (f32[2,768,768]{2,1,0:T(8,128)S(1)}, f32[2,768,768]{2,1,0:T(8,128)}, u32[]{:S(2)}) copy-start(f32[2,768,768]{2,1,0:T(8,128)} %get-tuple-element.104) | copy-start | bytes 14155780
  180.9 30.0 %collective-permute-start.13 = (bf16[2,2,96,768]{3,2,1,0:T(8,128)(2,1)S(1)}, bf16[2,2,96,768]{3,2,1,0:T(8,128)(2,1)}, u32[]{:S(2)}, u32[]{:S(2)}) collective-permute-start(bf16[2,2,96,768]{3,2,1,0:T(8,128)(2,1)S(1)} %fusion.12), channel_id=1, source_target_pairs={{0,4},{4,0},{8,12},{12,8},{16,20},{20,16},{24,28},{28,24},{1,5},{5... | collective-permute-start | bytes 1769480 | tf_op jit(solution)/shard_map/ppermute | solution.py:34
  185.9 26.2 %collective-permute-start.12 = (bf16[2,2,96,768]{3,2,1,0:T(8,128)(2,1)S(1)}, bf16[2,2,96,768]{3,2,1,0:T(8,128)(2,1)}, u32[]{:S(2)}, u32[]{:S(2)}) collective-permute-start(bf16[2,2,96,768]{3,2,1,0:T(8,128)(2,1)S(1)} %bitcast.196), channel_id=1, source_target_pairs={{0,2},{1,3},{2,0},{3,1},{4,6},{5,7},{6,4},{7,5},{8,10},{9,11},{10,... | collective-permute-start | bytes 1769480 | tf_op jit(solution)/shard_map/ppermute | solution.py:34
  206.9 4.0 %copy-start.17 = (f32[1,768,768]{2,1,0:T(8,128)S(1)}, f32[1,768,768]{2,1,0:T(8,128)}, u32[]{:S(2)}) copy-start(f32[1,768,768]{2,1,0:T(8,128)} %copy-done.16) | copy-start | bytes 7077892
  208.1 19.2 %collective-permute-start.14 = (bf16[2,128,512]{2,1,0:T(8,128)(2,1)S(1)}, bf16[2,128,512]{2,1,0:T(8,128)(2,1)S(1)}, u32[]{:S(2)}, u32[]{:S(2)}) collective-permute-start(bf16[2,128,512]{2,1,0:T(8,128)(2,1)S(1)} %slice.146), channel_id=1, source_target_pairs={{8,0},{12,4},{16,8},{20,12},{24,16},{28,20},{9,1},{13,5},{17,9},{2... | collective-permute-start | bytes 786440 | tf_op jit(solution)/shard_map/ppermute | solution.py:644
  209.6 21.0 %collective-permute-start.16 = (bf16[128,512]{1,0:T(8,128)(2,1)S(1)}, bf16[128,512]{1,0:T(8,128)(2,1)}, u32[]{:S(2)}, u32[]{:S(2)}) collective-permute-start(bf16[128,512]{1,0:T(8,128)(2,1)S(1)} %slice_bitcast_fusion.6), channel_id=1, source_target_pairs={{16,0},{20,4},{24,8},{28,12},{17,1},{21,5},{25,9},{29,13},{18,2},{... | collective-permute-start | bytes 393224 | tf_op jit(solution)/shard_map/ppermute | solution.py:644
  214.0 22.0 %collective-permute-start.17 = (bf16[2,96,768]{2,1,0:T(8,128)(2,1)}, bf16[2,96,768]{2,1,0:T(8,128)(2,1)}, u32[]{:S(2)}, u32[]{:S(2)}) collective-permute-start(bf16[2,96,768]{2,1,0:T(8,128)(2,1)} %fusion.22), channel_id=1, source_target_pairs={{0,4},{4,0},{8,12},{12,8},{16,20},{20,16},{24,28},{28,24},{1,5},{5... | collective-permute-start | bytes 884744 | tf_op jit(solution)/shard_map/ppermute | solution.py:34
  214.1 13.2 %copy-start.27 = (f32[128,512]{1,0:T(8,128)S(1)}, f32[128,512]{1,0:T(8,128)}, u32[]{:S(2)}) copy-start(f32[128,512]{1,0:T(8,128)} %get-tuple-element.117) | copy-start | bytes 786436
  227.4 7.0 %collective-permute-start.15 = (bf16[1,128,512]{2,1,0:T(8,128)(2,1)S(1)}, bf16[1,128,512]{2,1,0:T(8,128)(2,1)S(1)}, u32[]{:S(2)}, u32[]{:S(2)}) collective-permute-start(bf16[1,128,512]{2,1,0:T(8,128)(2,1)S(1)} %slice.255), channel_id=1, source_target_pairs={{4,0},{8,4},{12,8},{16,12},{20,16},{24,20},{28,24},{5,1},{9,5},{13... | collective-permute-start | bytes 393224 | tf_op jit(solution)/shard_map/ppermute | solution.py:644
  229.9 13.4 %copy-start.13 = (f32[768,768]{0,1:T(8,128)}, f32[768,768]{0,1:T(8,128)S(1)}, u32[]{:S(2)}) copy-start(f32[768,768]{0,1:T(8,128)S(1)} %fusion.83) | copy-start | bytes 7077892
  229.9 8.1 %collective-permute-start.18 = (bf16[2,96,768]{2,1,0:T(8,128)(2,1)S(1)}, bf16[2,96,768]{2,1,0:T(8,128)(2,1)S(1)}, u32[]{:S(2)}, u32[]{:S(2)}) collective-permute-start(bf16[2,96,768]{2,1,0:T(8,128)(2,1)S(1)} %fusion.23), channel_id=1, source_target_pairs={{0,2},{1,3},{2,0},{3,1},{4,6},{5,7},{6,4},{7,5},{8,10},{9,11},{10,... | collective-permute-start | bytes 884744 | tf_op jit(solution)/shard_map/ppermute | solution.py:34
  243.3 3.3 copy-start.32
  246.0 4.5 %collective-permute-start.19 = (bf16[4,2,2,56,768]{4,3,2,1,0:T(8,128)(2,1)}, bf16[4,2,2,56,768]{4,3,2,1,0:T(8,128)(2,1)}, u32[]{:S(2)}, u32[]{:S(2)}) collective-permute-start(bf16[4,2,2,56,768]{4,3,2,1,0:T(8,128)(2,1)} %fusion.5), channel_id=1, source_target_pairs={{0,1},{1,0},{2,3},{3,2},{4,5},{5,4},{6,7},{7,6},{8,9},{9,8},{10,11... | collective-permute-start | bytes 4128776 | tf_op jit(solution)/shard_map/ppermute | solution.py:34
  246.1 21.6 %collective-permute-start.22 = (bf16[2,768,768]{2,1,0:T(8,128)(2,1)}, bf16[2,768,768]{2,1,0:T(8,128)(2,1)}, u32[]{:S(2)}, u32[]{:S(2)}) collective-permute-start(bf16[2,768,768]{2,1,0:T(8,128)(2,1)} %get-tuple-element.130), channel_id=1, source_target_pairs={{0,1},{1,0},{2,3},{3,2},{4,5},{5,4},{6,7},{7,6},{8,9},{9,8},{10,11... | collective-permute-start | bytes 7077896 | tf_op jit(solution)/shard_map/ppermute | solution.py:34
  247.2 3.4 copy-start.14
  250.6 17.1 %slice-start.3 = ((s8[4718592]{0:T(1024)(128)(4,1)}), s8[4194304]{0:T(1024)(128)(4,1)S(1)}, s32[]{:S(2)}) async-start(s8[4718592]{0:T(1024)(128)(4,1)} %bitcast.178), calls=%async_computation.4 | async-start | bytes 8388608
  252.9 14.8 %slice-start.4 = ((s8[4718592]{0:T(1024)(128)(4,1)}), s8[524288]{0:T(1024)(128)(4,1)S(1)}, s32[]{:S(2)}) async-start(s8[4718592]{0:T(1024)(128)(4,1)} %bitcast.178), calls=%async_computation.5 | async-start | bytes 1048576
  253.3 10.4 %collective-permute-start.23 = (bf16[4,2,24,768]{3,2,1,0:T(8,128)(2,1)S(1)}, bf16[4,2,24,768]{3,2,1,0:T(8,128)(2,1)S(1)}, u32[]{:S(2)}, u32[]{:S(2)}) collective-permute-start(bf16[4,2,24,768]{3,2,1,0:T(8,128)(2,1)S(1)} %fusion.21), channel_id=1, source_target_pairs={{0,4},{4,0},{8,12},{12,8},{16,20},{20,16},{24,28},{28,24},{1,5},{5... | collective-permute-start | bytes 884744 | tf_op jit(solution)/shard_map/ppermute | solution.py:34
  255.7 11.7 %collective-permute-start.20 = (bf16[4,2,32,768]{3,2,1,0:T(8,128)(2,1)S(1)}, bf16[4,2,32,768]{3,2,1,0:T(8,128)(2,1)S(1)}, u32[]{:S(2)}, u32[]{:S(2)}) collective-permute-start(bf16[4,2,32,768]{3,2,1,0:T(8,128)(2,1)S(1)} %fusion.20), channel_id=1, source_target_pairs={{0,2},{1,3},{2,0},{3,1},{4,6},{5,7},{6,4},{7,5},{8,10},{9,11},{10,... | collective-permute-start | bytes 1179656 | tf_op jit(solution)/shard_map/ppermute | solution.py:34
  257.2 70.4 %collective-permute-start.30 = (bf16[192,768]{1,0:T(8,128)(2,1)}, bf16[192,768]{1,0:T(8,128)(2,1)}, u32[]{:S(2)}, u32[]{:S(2)}) collective-permute-start(bf16[192,768]{1,0:T(8,128)(2,1)} %get-tuple-element.186), channel_id=1, source_target_pairs={{0,16},{4,20},{8,24},{12,28},{16,0},{20,4},{24,8},{28,12},{1,17},{... | collective-permute-start | bytes 884744 | tf_op jit(solution)/shard_map/ppermute | solution.py:48
  262.1 65.5 %collective-permute-start.31 = (bf16[192,768]{1,0:T(8,128)(2,1)}, bf16[192,768]{1,0:T(8,128)(2,1)}, u32[]{:S(2)}, u32[]{:S(2)}) collective-permute-start(bf16[192,768]{1,0:T(8,128)(2,1)} %get-tuple-element.187), channel_id=1, source_target_pairs={{0,24},{4,28},{8,16},{12,20},{16,8},{20,12},{24,0},{28,4},{1,25},{... | collective-permute-start | bytes 884744 | tf_op jit(solution)/shard_map/ppermute | solution.py:48
  263.7 8.3 %collective-permute-start.24 = (bf16[4,24,768]{2,1,0:T(8,128)(2,1)S(1)}, bf16[4,24,768]{2,1,0:T(8,128)(2,1)S(1)}, u32[]{:S(2)}, u32[]{:S(2)}) collective-permute-start(bf16[4,24,768]{2,1,0:T(8,128)(2,1)S(1)} %fusion.42), channel_id=1, source_target_pairs={{0,2},{1,3},{2,0},{3,1},{4,6},{5,7},{6,4},{7,5},{8,10},{9,11},{10,... | collective-permute-start | bytes 442376 | tf_op jit(solution)/shard_map/ppermute | solution.py:34
  267.6 5.7 %collective-permute-start.21 = (bf16[4,32,768]{2,1,0:T(8,128)(2,1)S(1)}, bf16[4,32,768]{2,1,0:T(8,128)(2,1)S(1)}, u32[]{:S(2)}, u32[]{:S(2)}) collective-permute-start(bf16[4,32,768]{2,1,0:T(8,128)(2,1)S(1)} %fusion.29), channel_id=1, source_target_pairs={{0,4},{4,0},{8,12},{12,8},{16,20},{20,16},{24,28},{28,24},{1,5},{5... | collective-permute-start | bytes 589832 | tf_op jit(solution)/shard_map/ppermute | solution.py:34
  274.1 12.0 %collective-permute-start.25 = (bf16[56,768]{1,0:T(8,128)(2,1)}, bf16[56,768]{1,0:T(8,128)(2,1)}, u32[]{:S(2)}, u32[]{:S(2)}) collective-permute-start(bf16[56,768]{1,0:T(8,128)(2,1)} %get-tuple-element.181), channel_id=1, source_target_pairs={{0,8},{4,12},{8,0},{12,4},{16,24},{20,28},{24,16},{28,20},{1,9},{5... | collective-permute-start | bytes 258056 | tf_op jit(solution)/shard_map/ppermute | solution.py:48
  277.5 17.0 %collective-permute-start.26 = (bf16[56,768]{1,0:T(8,128)(2,1)}, bf16[56,768]{1,0:T(8,128)(2,1)}, u32[]{:S(2)}, u32[]{:S(2)}) collective-permute-start(bf16[56,768]{1,0:T(8,128)(2,1)} %get-tuple-element.182), channel_id=1, source_target_pairs={{0,16},{4,20},{8,24},{12,28},{16,0},{20,4},{24,8},{28,12},{1,17},{... | collective-permute-start | bytes 258056 | tf_op jit(solution)/shard_map/ppermute | solution.py:48
  281.1 14.9 %collective-permute-start.27 = (bf16[56,768]{1,0:T(8,128)(2,1)}, bf16[56,768]{1,0:T(8,128)(2,1)}, u32[]{:S(2)}, u32[]{:S(2)}) collective-permute-start(bf16[56,768]{1,0:T(8,128)(2,1)} %get-tuple-element.183), channel_id=1, source_target_pairs={{0,24},{4,28},{8,16},{12,20},{16,8},{20,12},{24,0},{28,4},{1,25},{... | collective-permute-start | bytes 258056 | tf_op jit(solution)/shard_map/ppermute | solution.py:48
  281.1 16.5 %copy-start.22 = (f32[512,768]{1,0:T(8,128)S(1)}, f32[512,768]{1,0:T(8,128)}, u32[]{:S(2)}) copy-start(f32[512,768]{1,0:T(8,128)} %get-tuple-element.133) | copy-start | bytes 4718596
  281.1 40.6 %slice-start = ((s8[9437184]{0:T(1024)(128)(4,1)}), s8[1048576]{0:T(1024)(128)(4,1)S(1)}, s32[]{:S(2)}) async-start(s8[9437184]{0:T(1024)(128)(4,1)} %bitcast.160), calls=%async_computation.1 | async-start | bytes 2097152
  286.1 11.5 %copy-start.20 = (bf16[4,128,768]{2,1,0:T(8,128)(2,1)S(1)}, bf16[4,128,768]{2,1,0:T(8,128)(2,1)}, u32[]{:S(2)}) copy-start(bf16[4,128,768]{2,1,0:T(8,128)(2,1)} %param.19) | copy-start | bytes 2359300
  286.1 23.7 %collective-permute-start.34 = (bf16[2,2,96,768]{3,2,1,0:T(8,128)(2,1)}, bf16[2,2,96,768]{3,2,1,0:T(8,128)(2,1)S(1)}, u32[]{:S(2)}, u32[]{:S(2)}) collective-permute-start(bf16[2,2,96,768]{3,2,1,0:T(8,128)(2,1)} %fusion.13), channel_id=1, source_target_pairs={{0,4},{4,0},{8,12},{12,8},{16,20},{20,16},{24,28},{28,24},{1,5},{5... | collective-permute-start | bytes 1769480 | tf_op jit(solution)/shard_map/ppermute | solution.py:34
  294.5 17.1 %collective-permute-start.32 = (bf16[2,2,96,768]{3,2,1,0:T(8,128)(2,1)}, bf16[2,2,96,768]{3,2,1,0:T(8,128)(2,1)S(1)}, u32[]{:S(2)}, u32[]{:S(2)}) collective-permute-start(bf16[2,2,96,768]{3,2,1,0:T(8,128)(2,1)} %bitcast.195), channel_id=1, source_target_pairs={{0,2},{1,3},{2,0},{3,1},{4,6},{5,7},{6,4},{7,5},{8,10},{9,11},{10,... | collective-permute-start | bytes 1769480 | tf_op jit(solution)/shard_map/ppermute | solution.py:34
  297.0 12.7 %collective-permute-start.28 = (bf16[56,768]{1,0:T(8,128)(2,1)S(1)}, bf16[56,768]{1,0:T(8,128)(2,1)S(1)}, u32[]{:S(2)}, u32[]{:S(2)}) collective-permute-start(bf16[56,768]{1,0:T(8,128)(2,1)S(1)} %fusion.37), channel_id=1, source_target_pairs={{0,2},{1,3},{2,0},{3,1},{4,6},{5,7},{6,4},{7,5},{8,10},{9,11},{10,... | collective-permute-start | bytes 258056 | tf_op jit(solution)/shard_map/ppermute | solution.py:34
  297.6 24.1 %slice-start.1 = ((s8[9437184]{0:T(1024)(128)(4,1)}), s8[4194304]{0:T(1024)(128)(4,1)S(1)}, s32[]{:S(2)}) async-start(s8[9437184]{0:T(1024)(128)(4,1)} %bitcast.160), calls=%async_computation.2 | async-start | bytes 8388608
  310.0 6.8 %collective-permute-start.35 = (bf16[2,96,768]{2,1,0:T(8,128)(2,1)S(1)}, bf16[2,96,768]{2,1,0:T(8,128)(2,1)S(1)}, u32[]{:S(2)}, u32[]{:S(2)}) collective-permute-start(bf16[2,96,768]{2,1,0:T(8,128)(2,1)S(1)} %fusion.25), channel_id=1, source_target_pairs={{0,2},{1,3},{2,0},{3,1},{4,6},{5,7},{6,4},{7,5},{8,10},{9,11},{10,... | collective-permute-start | bytes 884744 | tf_op jit(solution)/shard_map/ppermute | solution.py:34
  311.6 10.1 %slice-start.2 = ((s8[9437184]{0:T(1024)(128)(4,1)}), s8[4194304]{0:T(1024)(128)(4,1)S(1)}, s32[]{:S(2)}) async-start(s8[9437184]{0:T(1024)(128)(4,1)} %bitcast.160), calls=%async_computation.3 | async-start | bytes 8388608
  311.7 6.8 %collective-permute-start.33 = (bf16[2,96,768]{2,1,0:T(8,128)(2,1)S(1)}, bf16[2,96,768]{2,1,0:T(8,128)(2,1)S(1)}, u32[]{:S(2)}, u32[]{:S(2)}) collective-permute-start(bf16[2,96,768]{2,1,0:T(8,128)(2,1)S(1)} %fusion.24), channel_id=1, source_target_pairs={{0,4},{4,0},{8,12},{12,8},{16,20},{20,16},{24,28},{28,24},{1,5},{5... | collective-permute-start | bytes 884744 | tf_op jit(solution)/shard_map/ppermute | solution.py:34
  312.6 8.9 %collective-permute-start.29 = (bf16[2,56,768]{2,1,0:T(8,128)(2,1)S(1)}, bf16[2,56,768]{2,1,0:T(8,128)(2,1)S(1)}, u32[]{:S(2)}, u32[]{:S(2)}) collective-permute-start(bf16[2,56,768]{2,1,0:T(8,128)(2,1)S(1)} %pad_maximum_fusion.14), channel_id=1, source_target_pairs={{0,1},{1,0},{2,3},{3,2},{4,5},{5,4},{6,7},{7,6},{8,9},{9,8},{10,11... | collective-permute-start | bytes 516104 | tf_op jit(solution)/shard_map/ppermute | solution.py:34
  318.7 8.9 %collective-permute-start.36 = (bf16[192,768]{1,0:T(8,128)(2,1)S(1)}, bf16[192,768]{1,0:T(8,128)(2,1)S(1)}, u32[]{:S(2)}, u32[]{:S(2)}) collective-permute-start(bf16[192,768]{1,0:T(8,128)(2,1)S(1)} %fusion.26), channel_id=1, source_target_pairs={{0,8},{4,12},{8,0},{12,4},{16,24},{20,28},{24,16},{28,20},{1,9},{5... | collective-permute-start | bytes 884744 | tf_op jit(solution)/shard_map/ppermute | solution.py:48
  328.8 6.8 %collective-permute-start.37 = (bf16[192,768]{1,0:T(8,128)(2,1)S(1)}, bf16[192,768]{1,0:T(8,128)(2,1)S(1)}, u32[]{:S(2)}, u32[]{:S(2)}) collective-permute-start(bf16[192,768]{1,0:T(8,128)(2,1)S(1)} %fusion.11), channel_id=1, source_target_pairs={{0,2},{1,3},{2,0},{3,1},{4,6},{5,7},{6,4},{7,5},{8,10},{9,11},{10,... | collective-permute-start | bytes 884744 | tf_op jit(solution)/shard_map/ppermute | solution.py:34
  335.7 2.1 collective-permute-start.38
  340.0 3.7 copy-start
  343.7 4.9 %copy-start.6 = (f32[768,384]{1,0:T(8,128)S(1)}, f32[768,384]{1,0:T(8,128)}, u32[]{:S(2)}) copy-start(f32[768,384]{1,0:T(8,128)} %refs_1_.7) | copy-start | bytes 3538948
  343.7 4.9 %copy-start.7 = (f32[768,384]{1,0:T(8,128)S(1)}, f32[768,384]{1,0:T(8,128)}, u32[]{:S(2)}) copy-start(f32[768,384]{1,0:T(8,128)} %refs_2_.7) | copy-start | bytes 3538948
  348.6 36.6 %copy-start.29 = (f32[1072]{0:T(1024)S(1)}, f32[1072]{0:T(1024)}, u32[]{:S(2)}) copy-start(f32[1072]{0:T(1024)} %param.26) | copy-start | bytes 12868
  348.6 36.6 %copy-start.30 = (f32[1072]{0:T(1024)S(1)}, f32[1072]{0:T(1024)}, u32[]{:S(2)}) copy-start(f32[1072]{0:T(1024)} %param.37) | copy-start | bytes 12868
  348.6 36.6 %copy-start.31 = (f32[1072]{0:T(1024)S(1)}, f32[1072]{0:T(1024)}, u32[]{:S(2)}) copy-start(f32[1072]{0:T(1024)} %param.32) | copy-start | bytes 12868
  (15 other events, 33.2 us)
Sparse Core Ops, SparseCore 0:
  329.6 54.2 all-gather.2
where the time goes:
time: 399 us; the launch traced here: 393 us
  waiting for transfers between devices  155 us (39%)
  Pallas kernels  76.7 us (19%)
  starting transfers between devices  67.2 us (17%)
  other arithmetic  40.6 us (10%)
  local copies, waits for them, and re-layouts  30.3 us (8%)
  between operations  15.4 us (4%)
  matrix products  7.36 us (2%)
    ppermute x24, waiting for transfers between devices, swap(): lax.ppermute(value, axis, [(i, i ^ step) for i in range(lax.axis_size(axi...  83.4 us
    ppermute x9, waiting for transfers between devices, swap_z(): return lax.ppermute(value, 'seq', [(i, i ^ 2 * step) for i in range(size)])  32.4 us
    all_gather x1, waiting for transfers between devices, shards(): vector_parts = lax.all_gather(vector_part[0], ('seq', 'batch'))  30 us
    pallas_call x2, Pallas kernels, feed(): pl.pallas_call(functools.partial(feed_kernel, depths), in_specs=[vmem, vm...  26 us
    ppermute x24, starting transfers between devices, swap(): lax.ppermute(value, axis, [(i, i ^ step) for i in range(lax.axis_size(axi...  23.7 us
    ppermute x9, starting transfers between devices, swap_z(): return lax.ppermute(value, 'seq', [(i, i ^ 2 * step) for i in range(size)])  21.9 us
    ppermute x6, starting transfers between devices, shifted(): lax.ppermute(value, 'seq', [(b, a) for a, b in pairs] if back else pairs)  21.5 us
    pallas_call x1, Pallas kernels, attention(): pl.pallas_call(functools.partial(attention_kernel, blocks, HEADS), grid=(...  18.3 us
  transfers between devices with their start and end apart: 40, of which 19 were waited for; matrix products, arithmetic and copies ran while one was open for 10% of the time, Pallas kernels for 13%

commit v1 on v0

--- a/solution.py
+++ b/solution.py
@@ -25,6 +25,7 @@
 low = jnp.bfloat16
 f32 = jnp.float32
 VMEM_LIMIT = 56 * 1024 * 1024
+GROUPS = 2
 FEED_VMEM = 56 * 1024 * 1024
 UPDATE_VMEM = 28 * 1024 * 1024
 
@@ -39,8 +40,8 @@
     return lax.rem(lax.axis_index(axis) // step, 2)
 
 
-def flow(first, *others):
-    return lax.optimization_barrier((first, *others))[0]
+def hold(*values):
+    return lax.optimization_barrier(values)
 
 
 def swap_z(value, step):
@@ -48,50 +49,20 @@
     return lax.ppermute(value, "seq", [(i, i ^ (2 * step)) for i in range(size)])
 
 
-def z_index():
-    return lax.axis_index("seq") // 2
-
-
 def gather_z(piece):
     return [piece] + [swap_z(piece, k) for k in range(1, lax.axis_size("seq") // 2)]
 
 
-def gather_bit(value, bit, axis, absolute=False, after=()):
+def gather_bit(value, bit, axis, absolute=False):
     got = swap(value, bit)
-    if after:
-        got = flow(got, *after)
     if absolute:
         upper = mine(bit) == 1
         return jnp.stack([jnp.where(upper, got, value), jnp.where(upper, value, got)], axis=axis)
     return jnp.stack([value, got], axis=axis)
 
 
-def split_bit(value, bit, axis, absolute=False):
-    if absolute:
-        own = mine(bit)
-        return (
-            lax.dynamic_index_in_dim(value, own, axis, keepdims=False),
-            lax.dynamic_index_in_dim(value, 1 - own, axis, keepdims=False).astype(low),
-        )
+def split_bit(value, bit, axis):
     return lax.index_in_dim(value, 0, axis, keepdims=False), lax.index_in_dim(value, 1, axis, keepdims=False).astype(low)
-
-
-def sum_bit(value, bit, axis, absolute=False, after=()):
-    kept, sent = split_bit(value, bit, axis, absolute)
-    got = swap(sent, bit)
-    if after:
-        got = flow(got, *after)
-    return kept.astype(f32) + got.astype(f32)
-
-
-def sum_z(value, absolute=False):
-    count = value.shape[0]
-    own = z_index() if absolute else 0
-    pick = lambda k: lax.dynamic_index_in_dim(value, own ^ k, 0, keepdims=False) if absolute else value[k]
-    total = pick(0).astype(f32)
-    for k in range(1, count):
-        total = total + swap_z(pick(k).astype(low), k).astype(f32)
-    return total
 
 
 def bit_names(axis, size):
@@ -193,23 +164,31 @@
     )(q_t, do_t, start, cosine, sine, kv)
 
 
-def feed_kernel(depths, n_ref, dy_ref, far_ref, near_ref, bias_far_ref, bias_near_ref, *refs):
+def gathered_parts(plane, refs, offset, rows):
+    half = plane // 2
+    out = []
+    for end, ref in enumerate(refs):
+        for j in range(half):
+            out.append((0, end * half + j, ref.at[0, j, :, pl.ds(offset, rows)]))
+            out.append((1, 2 * j + end, ref.at[1, j, :, pl.ds(offset, rows)]))
+    return out
+
+
+def feed_kernel(n_ref, dy_ref, first_far, last_far, first_near, last_near, bias_far_ref, bias_near_ref, *refs):
+    far_refs, near_refs = (first_far, last_far), (first_near, last_near)
     before = refs[: len(refs) - 11]
     out_ref, dn_ref, far_grad_ref, near_grad_ref, bias_far_grad_ref, bias_near_grad_ref = refs[-11:-5]
     weights, far_sum, near_sum, held, sems = refs[-5:]
     plane = weights.shape[2]
     last = (((1,), (1,)), ((), ()))
     first = (((0,), (0,)), ((), ()))
-    loads = []
-    for side, ref in enumerate((far_ref, near_ref)):
-        loads.append(
-            [
-                pltpu.make_async_copy(
-                    ref.at[:, k, pl.ds(depths[0], len(depths)), pl.ds(0, weights.shape[4])], weights.at[side, :, k], sems.at[side, k]
-                )
-                for k in range(plane)
-            ]
-        )
+    loads = [
+        [
+            pltpu.make_async_copy(source, weights.at[side, kind, k], sems.at[side, 2 * k + kind])
+            for kind, k, source in gathered_parts(plane, refs_of, 0, weights.shape[4])
+        ]
+        for side, refs_of in enumerate((far_refs, near_refs))
+    ]
     fetches = [pltpu.make_async_copy(ref, held.at[k], sems.at[2, k]) for k, ref in enumerate(before)]
     for copy in loads[0] + loads[1] + fetches:
         copy.start()
@@ -253,15 +232,15 @@
         copy.wait()
 
 
-def feed(normed, d_out, far, near, bias_far, bias_near, depths, rows, before):
+def feed(normed, d_out, far, near, bias_far, bias_near, rows, before):
     tokens = normed.shape[0]
-    plane = far.shape[1]
-    units = plane * len(depths) * rows
+    plane, depth = 2 * far[0].shape[1], far[0].shape[2]
+    units = plane * depth * rows
     before = before or []
     vmem, hbm = pl.BlockSpec(memory_space=pltpu.VMEM), pl.BlockSpec(memory_space=pl.ANY)
     return pl.pallas_call(
-        functools.partial(feed_kernel, depths),
-        in_specs=[vmem, vmem, hbm, hbm, vmem, vmem] + [hbm] * len(before),
+        feed_kernel,
+        in_specs=[vmem, vmem, hbm, hbm, hbm, hbm, vmem, vmem] + [hbm] * len(before),
         out_specs=[vmem, vmem, hbm, hbm, vmem, vmem],
         out_shape=[
             jax.ShapeDtypeStruct((tokens, D), f32),
@@ -272,27 +251,28 @@
             jax.ShapeDtypeStruct((1, units), f32),
         ],
         scratch_shapes=[
-            pltpu.VMEM((2, 2, plane, len(depths), rows, D), low),
+            pltpu.VMEM((2, 2, plane, depth, rows, D), low),
             pltpu.VMEM((2, units, D), low),
             pltpu.VMEM((2, units, D), f32),
             pltpu.VMEM((2, tokens, D), f32),
-            pltpu.SemaphoreType.DMA((4, max(plane, 4))),
+            pltpu.SemaphoreType.DMA((4, 2 * plane)),
         ],
         compiler_params=pltpu.CompilerParams(vmem_limit_bytes=FEED_VMEM),
         cost_estimate=pl.CostEstimate(flops=4 * 24 * tokens * units * D, bytes_accessed=8 << 20, transcendentals=0),
         name="feed",
-    )(normed, d_out, far, near, bias_far, bias_near, *before)
+    )(normed, d_out, *far, *near, bias_far, bias_near, *before)
 
 
 def head_kernel(
-    vec_len, group_pieces, offset, out_rows, device_ref, x_ref, near_ref, far_ref, cos_ref, sin_ref, n_one_ref, n_two_ref,
-    q_ref, kv_ref, w_ref, gain_ref, bias_ref, *refs
+    vec_len, offset, out_rows, device_ref, x_ref, first_near, last_near, first_far, last_far, cos_ref, sin_ref, n_one_ref,
+    n_two_ref, q_ref, kv_ref, w_ref, gain_ref, bias_ref, *refs
 ):
     *bias_refs, out_ref, flat, units, held, pieces_of, outs_of, sems = refs if out_rows else (*refs[:-6], None, *refs[-6:])
     _, _, plane, depth, size, _ = held.shape
     copies = [
-        pltpu.make_async_copy(ref.at[:, :, :, pl.ds(offset, size)], held.at[side], sems.at[side])
-        for side, ref in enumerate((near_ref, far_ref))
+        pltpu.make_async_copy(source, held.at[side, kind, k], sems.at[side, 2 * k + kind])
+        for side, refs_of in enumerate(((first_near, last_near), (first_far, last_far)))
+        for kind, k, source in gathered_parts(plane, refs_of, offset, size)
     ]
     for copy in copies:
         copy.start()
@@ -326,16 +306,18 @@
     gain_ref[0:1] = gain_one
     gain_ref[1:2] = gain_two
     qkv_bias = vector(4 * D, D + 2 * HEAD)
-    offset = 4 * D + D + 2 * HEAD
-    bias_ref[...] = vector(offset, D) + vector(offset + D + FF, D)
-    count, size = units.shape
+    start = 4 * D + D + 2 * HEAD
+    bias_ref[...] = vector(start, D) + vector(start + D + FF, D)
+    count, size_of = units.shape
     for k in range(count):
-        units[k : k + 1, :] = vector(offset + D + k * size, size)
-    sides = len(bias_refs) // len(group_pieces)
+        units[k : k + 1, :] = vector(start + D + k * size_of, size_of)
+    groups = len(bias_refs) // 2
     for k, ref in enumerate(bias_refs):
-        side, pieces = k // len(group_pieces), group_pieces[k % len(group_pieces)]
-        for i, piece in enumerate(pieces):
-            ref[:, i * size : (i + 1) * size] = units[pl.ds(device_ref[side * (count // sides) + piece], 1), :]
+        side, g = k // groups, k % groups
+        width = size_of // groups
+        for i in range(count // 2):
+            row = units[pl.ds(device_ref[side * (count // 2) + i], 1), :]
+            ref[:, i * width : (i + 1) * width] = row[:, g * width : (g + 1) * width]
     n_one = (xhat * gain_one + shift_one).astype(low)
     n_one_ref[...] = n_one
     n_two_ref[...] = (xhat * gain_two + shift_two).astype(low)
@@ -357,16 +339,14 @@
     kv_ref[HEAD:, :] = projected[D + HEAD :].astype(low)
 
 
-def head(device, x, near, far, offset, size, out_rows, cosine, sine, group_pieces, vec_len, shards_of):
+def head(device, x, near, far, offset, size, out_rows, cosine, sine, groups, vec_len, shards_of):
     tokens = x.shape[0]
     count = device.shape[0]
-    _, plane, depth = near.shape[:3]
-    width = FF // count
+    plane, depth = 2 * near[0].shape[1], near[0].shape[2]
     vmem, hbm = pl.BlockSpec(memory_space=pltpu.VMEM), pl.BlockSpec(memory_space=pl.ANY)
-    bias_rows = [jax.ShapeDtypeStruct((1, len(pieces) * width), f32) for pieces in group_pieces] * 2
     return pl.pallas_call(
-        functools.partial(head_kernel, vec_len, group_pieces, offset, out_rows),
-        in_specs=[pl.BlockSpec(memory_space=pltpu.SMEM), vmem, hbm, hbm, vmem, vmem],
+        functools.partial(head_kernel, vec_len, offset, out_rows),
+        in_specs=[pl.BlockSpec(memory_space=pltpu.SMEM), vmem, hbm, hbm, hbm, hbm, vmem, vmem],
         out_shape=[
             jax.ShapeDtypeStruct((tokens, D), low),
             jax.ShapeDtypeStruct((tokens, D), low),
@@ -375,60 +355,37 @@
             jax.ShapeDtypeStruct((D + 2 * HEAD, D), low),
             jax.ShapeDtypeStruct((2, D), f32),
             jax.ShapeDtypeStruct((1, D), f32),
-            *bias_rows,
         ]
+        + [jax.ShapeDtypeStruct((1, FF // 2 // groups), f32)] * (2 * groups)
         + [jax.ShapeDtypeStruct((D, D), low)] * (out_rows > 0),
         scratch_shapes=[
             pltpu.VMEM((1, shards_of * vec_len), f32),
-            pltpu.VMEM((count, width), f32),
+            pltpu.VMEM((count, FF // count), f32),
             pltpu.VMEM((2, 2, plane, depth, size, D), low),
             pltpu.VMEM((count, size, D), f32),
             pltpu.VMEM((count, max(out_rows, 8), D), f32),
-            pltpu.SemaphoreType.DMA((2,)),
+            pltpu.SemaphoreType.DMA((2, 2 * plane)),
         ],
         compiler_params=pltpu.CompilerParams(vmem_limit_bytes=FEED_VMEM),
         cost_estimate=pl.CostEstimate(flops=4 * 2 * tokens * 896 * D, bytes_accessed=8 << 20, transcendentals=0),
         name="head",
-    )(device, x, near, far, cosine, sine)
-
-
-def back_kernel(dq_ref, dkv_ref, cos_ref, sin_ref, w_ref, n_ref, grad_ref, dn_ref, sum_ref):
-    shards_of = grad_ref.shape[0]
-    rows = (D + 2 * HEAD) // shards_of
+    )(device, x, *near, *far, cosine, sine)
+
+
+def tail_kernel(
+    shards_of, entry_ref, x_ref, dy_ref, dq_ref, dkv_ref, cos_ref, sin_ref, w_ref, n_ref, context_ref, d_two_ref, gain_ref, *refs
+):
+    bias_refs, (in_grad_ref, qkv_ref, out_ref, flat, units) = refs[:-5], refs[-5:]
     d_kv = dkv_ref[...]
     a, b = d_kv[: ROT // 2], d_kv[ROT // 2 : ROT]
     cosine, sine = cos_ref[...], sin_ref[...]
     d_kv = jnp.concatenate([a * cosine + b * sine, b * cosine - a * sine, d_kv[ROT:]], axis=0).astype(low)
     d_proj = jnp.concatenate([dq_ref[...], d_kv], axis=0)
-    weight = w_ref[...]
-    grad = jnp.dot(d_proj, n_ref[...], preferred_element_type=f32)
-    grad_ref[...] = jnp.zeros_like(grad_ref)
-    for s in range(shards_of):
-        grad_ref[s, :rows, :] = grad[s * rows : (s + 1) * rows]
-    dn_ref[...] = lax.dot_general(d_proj, weight, (((0,), (0,)), ((), ())), preferred_element_type=f32)
-    ones = jnp.ones((8, d_proj.shape[1]), low)
-    sum_ref[...] = lax.dot_general(ones, d_proj, (((1,), (1,)), ((), ())), preferred_element_type=f32)[0:1]
-
-
-def back(dq_t, dkv, cosine, sine, weight, normed, shards_of, padded):
-    tokens = normed.shape[0]
-    width = D + 2 * HEAD
-    return pl.pallas_call(
-        back_kernel,
-        out_shape=[
-            jax.ShapeDtypeStruct((shards_of, padded, D), f32),
-            jax.ShapeDtypeStruct((tokens, D), f32),
-            jax.ShapeDtypeStruct((1, width), f32),
-        ],
-        compiler_params=pltpu.CompilerParams(vmem_limit_bytes=VMEM_LIMIT),
-        cost_estimate=pl.CostEstimate(flops=4 * 4 * tokens * 896 * D, bytes_accessed=8 << 20, transcendentals=0),
-        name="back",
-    )(dq_t, dkv, cosine, sine, weight, normed)
-
-
-def tail_kernel(group_pieces, entry_ref, x_ref, dy_ref, d_one_ref, d_two_ref, gain_ref, sum_ref, *refs):
-    bias_refs, (in_grad_ref, flat, units) = refs[:-3], refs[-3:]
-    d_one, d_two = d_one_ref[...], d_two_ref[...]
+    first = (((0,), (0,)), ((), ()))
+    qkv_grad = jnp.dot(d_proj, n_ref[...], preferred_element_type=f32)
+    out_grad = lax.dot_general(dy_ref[...], context_ref[...], first, preferred_element_type=f32)
+    d_one = lax.dot_general(d_proj, w_ref[...], first, preferred_element_type=f32)
+    d_two = d_two_ref[...]
     x = x_ref[...].astype(f32)
     dy = dy_ref[...].astype(f32)
     center = x - jnp.mean(x, axis=-1, keepdims=True)
@@ -441,15 +398,18 @@
     in_grad_ref[...] = (dy + d_in).astype(low)
     columns = lambda v: jnp.sum(v, axis=0, keepdims=True)
     dy_column = columns(dy)
+    ones = jnp.ones((8, d_proj.shape[1]), low)
+    proj_sum = lax.dot_general(ones, d_proj, (((1,), (1,)), ((), ())), preferred_element_type=f32)[0:1]
     pieces = [columns(d_one * xhat), columns(d_one), columns(d_two * xhat), columns(d_two)]
-    pieces += [sum_ref[...], dy_column, None, dy_column]
+    pieces += [proj_sum, dy_column, None, dy_column]
     count, size = units.shape
-    sides = len(bias_refs) // len(group_pieces)
+    groups = len(bias_refs) // 2
+    width = size // groups
     for k, ref in enumerate(bias_refs):
-        side, members = k // len(group_pieces), group_pieces[k % len(group_pieces)]
-        for i, member in enumerate(members):
-            place = side * (count // sides) + member
-            units[place : place + 1, :] = ref[:, i * size : (i + 1) * size]
+        side, g = k // groups, k % groups
+        for i in range(count // 2):
+            place = side * (count // 2) + i
+            units[place : place + 1, g * width : (g + 1) * width] = ref[:, i * width : (i + 1) * width]
     offset = 0
     for piece in pieces:
         if piece is None:
@@ -459,19 +419,39 @@
         else:
             flat[:, offset : offset + piece.shape[1]] = piece
             offset += piece.shape[1]
-
-
-def tail(entry, x, dy, d_one, d_two, gains, proj_sum, bias_grads, group_pieces, total):
+    qkv_rows, vec_len = qkv_grad.shape[0] // shards_of, flat.shape[1] // shards_of
+    to_shard = count // shards_of
+    share = lambda k, total: [k // to_shard * total + min(-(-total // to_shard) * j, total) for j in (k % to_shard, k % to_shard + 1)]
+    out_own = D // count
+    vec_row = qkv_ref.shape[1] - 4
+    for k in range(count):
+        to = entry_ref[k]
+        begin, end = share(k, qkv_rows)
+        qkv_ref[to] = jnp.zeros(qkv_ref.shape[1:], f32)
+        if end > begin:
+            qkv_ref[to, : end - begin, :] = qkv_grad[begin:end]
+        begin, end = share(k, vec_len)
+        if end > begin:
+            qkv_ref[to, vec_row : vec_row + 1, : end - begin] = flat[:, begin:end]
+        out_ref[to] = jnp.zeros(out_ref.shape[1:], f32)
+        out_ref[to, :out_own, :] = out_grad[k * out_own : (k + 1) * out_own]
+
+
+def tail(entry, x, dy, dq_t, dkv, cosine, sine, weight, normed, context, d_two, gains, bias_grads, rows, shards_of, vec_len):
     tokens = x.shape[0]
     count = entry.shape[0]
-    operands = (entry, x, dy, d_one, d_two, gains, proj_sum, *sum(bias_grads, []))
+    operands = (entry, x, dy, dq_t, dkv, cosine, sine, weight, normed, context, d_two, gains, *sum(bias_grads, []))
     return pl.pallas_call(
-        functools.partial(tail_kernel, group_pieces),
+        functools.partial(tail_kernel, shards_of),
         in_specs=[pl.BlockSpec(memory_space=pltpu.SMEM)] + [pl.BlockSpec(memory_space=pltpu.VMEM)] * (len(operands) - 1),
-        out_shape=[jax.ShapeDtypeStruct((tokens, D), low), jax.ShapeDtypeStruct((1, total), f32)],
-        scratch_shapes=[pltpu.VMEM((count, FF // count), f32)],
+        out_shape=[
+            jax.ShapeDtypeStruct((tokens, D), low),
+            jax.ShapeDtypeStruct((count, rows, D), f32),
+            jax.ShapeDtypeStruct((count, rows, D), f32),
+        ],
+        scratch_shapes=[pltpu.VMEM((1, shards_of * vec_len), f32), pltpu.VMEM((count, FF // count), f32)],
         compiler_params=pltpu.CompilerParams(vmem_limit_bytes=VMEM_LIMIT),
-        cost_estimate=pl.CostEstimate(flops=4 * tokens * 896 * D, bytes_accessed=8 << 20, transcendentals=0),
+        cost_estimate=pl.CostEstimate(flops=4 * 6 * tokens * 896 * D, bytes_accessed=8 << 20, transcendentals=0),
         name="tail",
     )(*operands)
 
@@ -551,8 +531,6 @@
     near = [core_bit] + x_bits[::-1] + [y_bit] + z_bits[::-1]
     depth = seq_count // 2
     plane = 2 ** (len(x_bits) + 1)
-    group_depths = (range(depth // 2, depth), range(depth // 2))
-    group_pieces = [[k * depth + z for k in range(plane) for z in depths] for depths in group_depths]
     x_low = inputs.reshape(tokens, D)
     dy = cotangent.reshape(tokens, D)
 
@@ -596,167 +574,200 @@
         [qkv_weight, jnp.pad(vectors, (0, vec_pad)).reshape(vec_rows, D), jnp.zeros((head_rows - used, D), f32)], axis=0
     ).astype(low)
     head_part_rows = head_rows // batch_count
-    unit_rows = up_rows // batch_count
+    unit_rows = up_rows // batch_count // GROUPS
     out_own = out_rows // batch_count
-    part = jnp.concatenate(
-        [
-            own_part(up_weight.astype(low)),
-            own_part(head_shard),
-            own_part(down_weight.T.astype(low)),
-            own_part(out_weight.astype(low)),
-            jnp.zeros((head_part_rows - out_own, D), low),
-        ],
-        axis=0,
-    )
-    parts, cosine, sine, start_here, entry, device = lax.optimization_barrier(
-        (jnp.stack(gather_z(part)), cosine, sine, start_here, entry, device)
-    )
-    half = part.shape[0] // 2
-    up_near, down_near = parts[:, :half], parts[:, half:]
-    up_near = gather_bit(up_near, y_bit, 0)
-    for bit in x_bits:
-        down_near = gather_bit(down_near, bit, 0)
-    for bit in x_bits:
-        up_near = gather_bit(up_near, bit, 0)
-    down_near = gather_bit(down_near, y_bit, len(x_bits))
-    near_all = jnp.stack([up_near, down_near]).reshape(2, plane, depth, half, D)
-    far_all = swap(near_all, core_bit)
+    up_low, down_low = own_part(up_weight.astype(low)), own_part(down_weight.T.astype(low))
+    outer = [
+        own_part(head_shard),
+        jnp.concatenate([own_part(out_weight.astype(low)), jnp.zeros((head_part_rows - out_own, D), low)], axis=0),
+    ]
+    parts_of = []
+    for g in range(GROUPS):
+        rows = slice(g * unit_rows, (g + 1) * unit_rows)
+        pieces = [up_low[rows], outer[0], down_low[rows], outer[1]] if g == 0 else [up_low[rows], down_low[rows]]
+        parts_of.append(jnp.concatenate(pieces, axis=0))
+
+    def gather_first(parts):
+        half = parts.shape[1] // 2
+        up, down = parts[:, :half], parts[:, half:]
+        for bit in x_bits[:-1]:
+            down = gather_bit(down, bit, 0)
+        return up, down, swap(up, y_bit), swap(down, x_bits[-1])
+
+    def gather_second(up, down, up_got, down_got):
+        up, down = jnp.stack([up, up_got]), jnp.stack([down, down_got])
+        for bit in x_bits[:-1]:
+            up = gather_bit(up, bit, 0)
+        shape = (1, plane // 2, depth) + up.shape[-2:]
+        return up, down, jnp.concatenate([up.reshape(shape), down.reshape(shape)], axis=0)
+
+    def gather_last(up, down):
+        return swap(up, x_bits[-1]), swap(down, y_bit)
+
+    def joined(up, down):
+        shape = (1, plane // 2, depth) + up.shape[-2:]
+        return jnp.concatenate([up.reshape(shape), down.reshape(shape)], axis=0)
+
+    z_zero = gather_z(parts_of[0])
+    *z_zero, cosine, sine, start_here, entry, device, part_one = hold(
+        *z_zero, cosine, sine, start_here, entry, device, parts_of[1]
+    )
+    up, down, up_got, down_got = gather_first(jnp.stack(z_zero))
+    z_one = gather_z(part_one)
+    up_got, down_got, *z_one = hold(up_got, down_got, *z_one)
+    up, down, first_zero = gather_second(up, down, up_got, down_got)
+    up_got, down_got = gather_last(up, down)
+    first_far_zero = swap(first_zero, core_bit)
+    up_got, down_got, first_far_zero = hold(up_got, down_got, first_far_zero)
+    last_zero = joined(up_got, down_got)
+    last_far_zero = swap(last_zero, core_bit)
+
     aligned = unit_rows % 16 == 0 and head_part_rows % 16 == 0
-    trim = lambda value, begin, end: value if aligned else value[..., begin:end, :]
-    near_weight, far_weight = trim(near_all, 0, unit_rows), trim(far_all, 0, unit_rows)
+    trim = lambda values, begin, end: values if aligned else tuple(v[..., begin:end, :] for v in values)
+    near_zero, far_zero = (first_zero, last_zero), (first_far_zero, last_far_zero)
+    end = unit_rows + head_part_rows
 
     inside = out_own % 8 == 0
     normed_one, normed_two, q_t, kv_own, qkv_full, gains, out_bias, *bias_rows = head(
-        device, x_low, trim(near_all, unit_rows, half), trim(far_all, unit_rows, half), unit_rows if aligned else 0,
-        head_part_rows, out_own if inside else 0, cosine, sine, group_pieces, vec_len, seq_count,
+        device, x_low, trim(near_zero, unit_rows, end), trim(far_zero, unit_rows, end), unit_rows if aligned else 0,
+        head_part_rows, out_own if inside else 0, cosine, sine, GROUPS, vec_len, seq_count,
     )
     if inside:
         out_full = bias_rows.pop()
     else:
-        out_full = jnp.concatenate([v[1, ..., unit_rows : unit_rows + out_own, :] for v in (near_all, far_all)], axis=0)
         chosen = (entry[:, None] == number[None, :]).astype(low)
-        out_full = jnp.dot(chosen, out_full.reshape(-1, out_own * D), preferred_element_type=f32).astype(low).reshape(D, D)
-    bias_rows = [bias_rows[: len(group_pieces)], bias_rows[len(group_pieces) :]]
+        sides = []
+        for pair in (near_zero, far_zero):
+            along = [v[1, :, :, unit_rows : unit_rows + out_own] for v in pair]
+            sides.append(jnp.stack(along, axis=1).reshape(-1, out_own * D))
+        out_full = jnp.dot(chosen, jnp.concatenate(sides, axis=0), preferred_element_type=f32).astype(low).reshape(D, D)
+    bias_rows = [bias_rows[:GROUPS], bias_rows[GROUPS:]]
     reach = seq_count // 2
 
     def shifted(value, step, back=False):
         pairs = [(j, j + step) for j in range(seq_count - step)]
         return lax.ppermute(value, "seq", [(b, a) for a, b in pairs] if back else pairs)
 
-    kv = kv_own[None]
-    farthest = shifted(kv_own, reach)
-    pair = shifted(kv, 1)
-    kv = jnp.concatenate([kv, pair], axis=0)
+    farthest, pair = shifted(kv_own, reach), shifted(kv_own[None], 1)
+    up, down, up_got, down_got = gather_first(jnp.stack(z_one))
+    farthest, pair, up_got, down_got, normed_two = hold(farthest, pair, up_got, down_got, normed_two)
+    kv = jnp.concatenate([kv_own[None], pair], axis=0)
     while kv.shape[0] < reach:
-        kv = jnp.concatenate([kv, shifted(kv, kv.shape[0])], axis=0)
-    kv = jnp.concatenate([kv, farthest[None]], axis=0)
+        kv_got = shifted(kv, kv.shape[0])
+        if 2 * kv.shape[0] < reach:
+            kv = jnp.concatenate([kv, kv_got], axis=0)
+        else:
+            break
+    up, down, first_one = gather_second(up, down, up_got, down_got)
+    up_got, down_got = gather_last(up, down)
+    first_far_one = swap(first_one, core_bit)
 
     last = (((1,), (1,)), ((), ()))
-    bias_grads, halves_of = [[], []], []
-
-    def feed_group(g, sums, *earlier):
-        depths = group_depths[g]
+    bias_grads = [[], []]
+
+    def feed_group(g, sums, normed, near, far, *beside):
         *sums, far_grad, near_grad, bias_far, bias_here = feed(
-            flow(normed_two, *earlier), dy, far_weight, near_weight, bias_rows[1][g], bias_rows[0][g], depths, unit_rows, sums
+            normed, dy, trim(far, 0, unit_rows), trim(near, 0, unit_rows), bias_rows[1][g], bias_rows[0][g], unit_rows, sums
         )
         bias_grads[0].append(bias_here)
         bias_grads[1].append(bias_far)
-        grad_sum = near_grad + swap(far_grad, core_bit).astype(f32)
-        half_shape = (2,) * len(x_bits) + (2, len(depths), unit_rows, D)
-        halves_of.append(
-            [
-                split_bit(grad_sum[0].reshape(half_shape), x_bits[-1], 0),
-                split_bit(grad_sum[1].reshape(half_shape), y_bit, len(x_bits)),
-            ]
-        )
-        return sums
-
-    def feed_first(halves):
-        (up_kept, up_sent), (down_kept, down_sent) = halves
-        up_sum = up_kept + swap(up_sent, x_bits[-1]).astype(f32)
+        far_grad, *beside = hold(far_grad, *beside)
+        shape = (2,) + (2,) * len(x_bits) + (2, depth, unit_rows, D)
+        grad_sum = (near_grad + swap(far_grad, core_bit).astype(f32)).reshape(shape)
+        return sums, grad_sum[0], grad_sum[1], *beside
+
+    def sum_first(up, down):
+        (up_kept, up_sent), (down_kept, down_sent) = split_bit(up, x_bits[-1], 0), split_bit(down, y_bit, len(x_bits))
+        return up_kept, up_sent, down_kept, down_sent
+
+    def sum_second(up_kept, up_sent, down_kept, down_sent):
+        up = up_kept + swap(up_sent, x_bits[-1]).astype(f32)
         for bit in x_bits[-2::-1]:
-            up_sum = sum_bit(up_sum, bit, 0)
-        return up_sum, down_kept + swap(down_sent, y_bit).astype(f32)
-
-    def feed_halves(up_sum, down_sum):
-        return split_bit(up_sum, y_bit, 0), split_bit(down_sum, x_bits[-1], 0)
-
-    def feed_second(halves, after):
-        (up_kept, up_sent), (down_kept, down_sent) = halves
-        up_sum = up_kept + flow(swap(up_sent, y_bit), *after).astype(f32)
-        down_sum = down_kept + flow(swap(down_sent, x_bits[-1]), *after).astype(f32)
+            kept, sent = split_bit(up, bit, 0)
+            up = kept + swap(sent, bit).astype(f32)
+        down = down_kept + swap(down_sent, y_bit).astype(f32)
+        (up_kept, up_sent), (down_kept, down_sent) = split_bit(up, y_bit, 0), split_bit(down, x_bits[-1], 0)
+        return up_kept, up_sent, down_kept, down_sent
+
+    def sum_third(up_kept, up_got, down_kept, down_got):
+        up = up_kept + up_got.astype(f32)
+        down = down_kept + down_got.astype(f32)
         for bit in x_bits[-2::-1]:
-            down_sum = sum_bit(down_sum, bit, 0, after=after)
-        return jnp.concatenate([up_sum, down_sum], axis=1)
-
-    sums = feed_group(0, None, pair, farthest)
-    first_sent = (halves_of[0][0][1], halves_of[0][1][1])
-
-    do_t = lax.dot_general(out_full, dy, (((0,), (1,)), ((), ())), preferred_element_type=f32).astype(low)
-    context, dq_t, dkv_own, dkv_sent = attention(flow(q_t, *first_sent), do_t, start_here, cosine, sine, kv)
-    first_halves = feed_halves(*feed_first(halves_of[0]))
-    mlp_out, d_normed_two = feed_group(1, sums, dq_t, first_halves[0][1], first_halves[1][1])
-
-    dkv_far = flow(shifted(dkv_sent[reach - 1], reach, True), d_normed_two)
-    dkv = jnp.concatenate([dkv_own[None], dkv_sent[: reach - 1].astype(f32)], axis=0)
-    while dkv.shape[0] > 1:
-        both = dkv.shape[0] // 2
-        dkv = dkv[:both] + flow(shifted(dkv[both:].astype(low), both, True), d_normed_two).astype(f32)
-    dkv = dkv[0] + dkv_far.astype(f32)
-
-    last_step = feed_second(first_halves, (d_normed_two,))
-    dkv, last_step = lax.optimization_barrier((dkv, last_step))
-    last_steps = [last_step]
-
-    shape = (depth, 2) + (2,) * len(x_bits) + (2, -1, D)
-    qkv_own = -(-qkv_rows // (8 * batch_count)) * 8
-    qkv_part, d_normed_one, proj_sum = back(
-        dq_t, dkv, cosine, sine, qkv_full, normed_one, seq_count, qkv_own * batch_count
-    )
-    out_part = lax.dot_general(dy, context, (((0,), (0,)), ((), ())), preferred_element_type=f32)
-    both = jnp.concatenate([qkv_part.reshape(shape), out_part.reshape(shape)], axis=len(shape) - 2)
-    both = sum_bit(both, core_bit, len(shape) - 3, True)
+            kept, sent = split_bit(down, bit, 0)
+            down = kept + swap(sent, bit).astype(f32)
+        return jnp.concatenate([up, down], axis=1)
+
+    def sum_z(value):
+        got = [swap_z(value[k].astype(low), k) for k in range(1, depth)]
+        total = value[0]
+        for part in got:
+            total = total + part.astype(f32)
+        return total
 
     def spread(part):
         value = part.astype(low)
-        for k, bit in enumerate(x_bits):
+        for bit in x_bits:
             value = gather_bit(value, bit, 0, True)
-        value = gather_bit(value, core_bit, len(x_bits), True)
-        return value.reshape(batch_count, -1, D)
-
-    qkv_sum, out_sum = both[..., :qkv_own, :], both[..., qkv_own:, :]
-    for bit in x_bits[::-1]:
-        qkv_sum = sum_bit(qkv_sum, bit, 2, True)
-    out_sum = sum_bit(out_sum, y_bit, 1, True)
-    sent = (halves_of[1][0][1], halves_of[1][1][1])
-    input_grad, vector_part = tail(
-        entry, x_low, dy, d_normed_one, flow(d_normed_two, *sent), gains, proj_sum, bias_grads, group_pieces,
-        seq_count * vec_len,
-    )
-    vector_parts = lax.all_gather(vector_part[0], ("seq", "batch"))
-    qkv_sum = sum_bit(qkv_sum, y_bit, 1, True, after=sent)
-    for bit in x_bits[::-1]:
-        out_sum = sum_bit(out_sum, bit, 1, True, after=sent)
-    both = sum_z(jnp.concatenate([qkv_sum, out_sum], axis=1), True)
-    second_halves = feed_halves(*feed_first(halves_of[1]))
-    last_steps.append(feed_second(second_halves, (both, vector_part)))
-    feed_sum = 0.0
-    for depths, last_step in zip(group_depths, last_steps):
-        for k, z in enumerate(depths):
-            feed_sum = feed_sum + (last_step[k] if z == 0 else swap_z(last_step[k].astype(low), z).astype(f32))
-    others = spread(both)
-    qkv_low = others[:, :qkv_own].reshape(-1, D)[:qkv_rows]
-    out_low = others[:, qkv_own:].reshape(-1, D)
-    out_grad, *out_states = update(out_low, bases, 1, out_weight, out_first, out_second)
-    qkv_grad, *qkv_states = update(qkv_low, bases, 0, qkv_weight, qkv_first, qkv_second)
+        return gather_bit(value, core_bit, len(x_bits), True).reshape(batch_count, -1, D)
+
+    sums, up_sum, down_sum, up_got, down_got, kv_got = feed_group(
+        0, None, normed_two, near_zero, far_zero, up_got, down_got, kv_got
+    )
+    kv = jnp.concatenate([kv, kv_got, farthest[None]], axis=0)
+    sum_zero = sum_first(up_sum, down_sum)
+    *sum_zero, first_far_one, q_t = hold(*sum_zero, first_far_one, q_t)
+    last_one = joined(up_got, down_got)
+    last_far_one = swap(last_one, core_bit)
+
+    do_t = lax.dot_general(out_full, dy, (((0,), (1,)), ((), ())), preferred_element_type=f32).astype(low)
+    context, dq_t, dkv_own, dkv_sent = attention(q_t, do_t, start_here, cosine, sine, kv)
+    sum_zero = sum_second(*sum_zero)
+    last_far_one, dq_t, normed_late, *sum_zero = hold(last_far_one, dq_t, normed_two, *sum_zero)
+    dkv_far = shifted(dkv_sent[reach - 1], reach, True)
+    dkv = jnp.concatenate([dkv_own[None], dkv_sent[: reach - 1].astype(f32)], axis=0)
+    middle = reach // 2
+    got = shifted(dkv[middle:].astype(low), middle, True)
+    up_got, down_got = swap(sum_zero[1], y_bit), swap(sum_zero[3], x_bits[-1])
+    (mlp_out, d_normed_two), up_sum, down_sum, up_got, down_got, dkv_far, got = feed_group(
+        1, sums, normed_late, (first_one, last_one), (first_far_one, last_far_one), up_got, down_got, dkv_far, got
+    )
+    sum_zero = sum_third(sum_zero[0], up_got, sum_zero[2], down_got)
+    dkv = dkv[:middle] + got.astype(f32)
+    while dkv.shape[0] > 1:
+        middle = dkv.shape[0] // 2
+        got = shifted(dkv[middle:].astype(low), middle, True)
+        dkv = dkv[:middle] + got.astype(f32)
+    dkv = dkv[0] + dkv_far.astype(f32)
+    qkv_share, vec_share = -(-qkv_rows // batch_count), -(-vec_len // batch_count)
+    input_grad, qkv_part, out_part = tail(
+        entry, x_low, dy, dq_t, dkv, cosine, sine, qkv_full, normed_one, context, d_normed_two, gains, bias_grads,
+        head_part_rows, seq_count, vec_len,
+    )
+    outer = jnp.stack([qkv_part, out_part]).reshape((2, 2) + (2,) * len(x_bits) + (2, depth, head_part_rows, D))
+    outer = outer[:, 0] + swap(outer[:, 1].astype(low), core_bit).astype(f32)
+    sum_one = sum_first(
+        jnp.concatenate([up_sum, outer[0]], axis=-2), jnp.concatenate([down_sum, outer[1]], axis=-2)
+    )
+    feed_zero = sum_z(sum_zero)
+    sum_one = sum_second(*sum_one)
+    *sum_one, feed_zero = hold(*sum_one, feed_zero)
+    grads_zero = spread(feed_zero)
     attn_out = lax.dot_general(context, out_full, last, preferred_element_type=f32)
-    outputs = (x_low.astype(f32) + attn_out + flow(mlp_out, both) + out_bias).astype(low)
-    feed_grads = spread(flow(feed_sum, out_grad, qkv_grad, outputs))
-    up_low = feed_grads[:, :unit_rows].reshape(-1, D)
-    down_low = feed_grads[:, unit_rows:].reshape(-1, D)
-    up_grad, *up_states = update(up_low, bases, 2, up_weight, up_first, up_second)
-    down_grad, *down_states = update(down_low, bases, 3, down_weight, down_first, down_second, True)
-    vector_grad = jnp.sum(lax.dynamic_slice_in_dim(vector_parts, seq_index * vec_len, vec_len, axis=1), axis=0)
+    outputs = (x_low.astype(f32) + attn_out + mlp_out + out_bias).astype(low)
+    sum_one = sum_third(sum_one[0], swap(sum_one[1], y_bit), sum_one[2], swap(sum_one[3], x_bits[-1]))
+    sum_one, grads_zero, outputs = hold(sum_one, grads_zero, outputs)
+    grads_one = spread(sum_z(sum_one))
+
+    end = unit_rows + head_part_rows
+    up_all = jnp.concatenate([grads_zero[:, :unit_rows], grads_one[:, :unit_rows]], axis=1).reshape(-1, D)
+    down_all = jnp.concatenate([grads_zero[:, unit_rows:], grads_one[:, end : end + unit_rows]], axis=1).reshape(-1, D)
+    qkv_all = grads_one[:, unit_rows : unit_rows + qkv_share].reshape(-1, D)[:qkv_rows]
+    out_all = grads_one[:, end + unit_rows : end + unit_rows + out_own].reshape(-1, D)
+    vector_grad = grads_one[:, end - 4, :vec_share].astype(f32).reshape(-1)[:vec_len]
+    out_grad, *out_states = update(out_all, bases, 1, out_weight, out_first, out_second)
+    qkv_grad, *qkv_states = update(qkv_all, bases, 0, qkv_weight, qkv_first, qkv_second)
+    up_grad, *up_states = update(up_all, bases, 2, up_weight, up_first, up_second)
+    down_grad, *down_states = update(down_all, bases, 3, down_weight, down_first, down_second, True)
     vector_new, *vector_states = adam_step(vectors, vector_grad, vector_first, vector_second)
     states = (qkv_states, out_states, up_states, down_states, (*vector_states, vector_new))
     return (

time: 399 us -> 315 us (0.79)
  waiting for transfers between devices: 155 us -> 129 us
  other arithmetic: 40.6 us -> 18.9 us
  between operations: 15.4 us -> 2.17 us
  local copies, waits for them, and re-layouts: 30.3 us -> 21 us
  starting transfers between devices: 67.2 us -> 59.9 us
  matrix products: 7.36 us -> 2.52 us
    all_gather x1 -> x0, waiting for transfers between devices: 30 us -> none  [shards(): vector_parts = lax.all_gather(vector_part[0], ('seq', 'batch'))]
    ppermute x9 -> x12, waiting for transfers between devices: 32.4 us -> 54.2 us  [swap_z(): return lax.ppermute(value, 'seq', [(i, i ^ 2 * step) for i in range(size)])]
    ppermute x24 -> x27, waiting for transfers between devices: 83.4 us -> 66.5 us  [swap(): lax.ppermute(value, axis, [(i, i ^ step) for i in range(lax.axis_size(axi...]
    another operation x8, other arithmetic: 12.3 us -> 0.64 us  [the longest x2 0.26 us: gather_second(): up, down = (jnp.stack([up, up_got]), jnp.stack([down, down_got]))]
    add x18 -> x13, other arithmetic: 13.3 us -> 3.86 us  [the longest x2 1.53 us: sum_second(): up = up_kept + swap(up_sent, x_bits[-1]).astype(f32)]
    another operation x3, local copies, waits for them, and re-layouts: 9.99 us -> 1.52 us  [gather_bit(): return jnp.stack([value, got], axis=axis)]
    ppermute x6, starting transfers between devices: 21.5 us -> 14.9 us  [shifted(): lax.ppermute(value, 'seq', [(b, a) for a, b in pairs] if back else pairs)]
    ppermute x24 -> x27, starting transfers between devices: 23.7 us -> 21.3 us  [swap(): lax.ppermute(value, axis, [(i, i ^ step) for i in range(lax.axis_size(axi...]
  transfers between devices with their start and end apart: 40 -> 45, of which waited for: 19 -> 24; matrix products, arithmetic and copies ran while one was open for 10% -> 7% of each run, Pallas kernels for 13% -> 20%
where the time goes in v1:
time: 315 us; the launch traced here: 310 us
  waiting for transfers between devices  129 us (41%)
  Pallas kernels  76.5 us (24%)
  starting transfers between devices  59.9 us (19%)
  local copies, waits for them, and re-layouts  21 us (7%)
  other arithmetic  18.9 us (6%)
    ppermute x27, waiting for transfers between devices, swap(): lax.ppermute(value, axis, [(i, i ^ step) for i in range(lax.axis_size(axi...  66.5 us
    ppermute x12, waiting for transfers between devices, swap_z(): return lax.ppermute(value, 'seq', [(i, i ^ 2 * step) for i in range(size)])  54.2 us
    pallas_call x2, Pallas kernels, feed(): pl.pallas_call(feed_kernel, in_specs=[vmem, vmem, hbm, hbm, hbm, hbm, vme...  26.3 us
    ppermute x12, starting transfers between devices, swap_z(): return lax.ppermute(value, 'seq', [(i, i ^ 2 * step) for i in range(size)])  23.7 us
    ppermute x27, starting transfers between devices, swap(): lax.ppermute(value, axis, [(i, i ^ step) for i in range(lax.axis_size(axi...  21.3 us
    pallas_call x1, Pallas kernels, attention(): pl.pallas_call(functools.partial(attention_kernel, blocks, HEADS), grid=(...  18.5 us
    pallas_call x4, Pallas kernels, update(): pl.pallas_call(functools.partial(update_kernel, across, number), in_specs...  15.7 us
    ppermute x6, starting transfers between devices, shifted(): lax.ppermute(value, 'seq', [(b, a) for a, b in pairs] if back else pairs)  14.9 us
  transfers between devices with their start and end apart: 45, of which 24 were waited for; matrix products, arithmetic and copies ran while one was open for 7% of the time, Pallas kernels for 20%

profile of v1, /device:TPU:0, one launch (start us, length us, event | category | flops | bytes accessed | tf_op | source)
XLA Modules:
  0.0 309.7 jit_solution(15258377931353792415)
XLA Ops:
  0.7 1.3 constant_dynamic-slice_fusion
  3.5 3.1 collective-permute-start
  6.6 2.6 collective-permute-start.1
  11.4 5.7 %collective-permute-done = bf16[160,768]{1,0:T(8,128)(2,1)S(1)} collective-permute-done((bf16[160,768]{1,0:T(8,128)(2,1)S(1)}, bf16[160,768]{1,0:T(8,128)(2,1)S(1)}, u32[]{:S(2)}, u32[]{:S(2)}) %collective-permute-start) | collective-permute-done | bytes 245792 | tf_op jit(solution)/shard_map/ppermute | solution.py:49
  17.0 9.9 %collective-permute-done.1 = bf16[160,768]{1,0:T(8,128)(2,1)S(1)} collective-permute-done((bf16[160,768]{1,0:T(8,128)(2,1)S(1)}, bf16[160,768]{1,0:T(8,128)(2,1)S(1)}, u32[]{:S(2)}, u32[]{:S(2)}) %collective-permute-start.1) | collective-permute-done | bytes 245792 | tf_op jit(solution)/shard_map/ppermute | solution.py:49
  27.2 1.6 collective-permute-start.3
  28.8 1.5 collective-permute-start.4
  30.3 4.3 %collective-permute-start.5 = (bf16[96,768]{1,0:T(8,128)(2,1)S(1)}, bf16[96,768]{1,0:T(8,128)(2,1)S(1)}, u32[]{:S(2)}, u32[]{:S(2)}) collective-permute-start(bf16[96,768]{1,0:T(8,128)(2,1)S(1)} %pad_maximum_fusion.24), channel_id=1, source_target_pairs={{0,8},{4,12},{8,0},{12,4},{16,24},{20,28},{24,16},{28,20},{1,9},{5... | collective-permute-start | bytes 442376 | tf_op jit(solution)/shard_map/ppermute | solution.py:49
  35.5 1.5 collective-permute-start.7
  37.0 1.9 collective-permute-done.5
  38.9 7.9 %collective-permute-done.6 = bf16[96,768]{1,0:T(8,128)(2,1)S(1)} collective-permute-done((bf16[96,768]{1,0:T(8,128)(2,1)S(1)}, bf16[96,768]{1,0:T(8,128)(2,1)S(1)}, u32[]{:S(2)}, u32[]{:S(2)}) %collective-permute-start.6) | collective-permute-done | bytes 147488 | tf_op jit(solution)/shard_map/ppermute | solution.py:49
  48.7 22.8 %collective-permute-done.8 = bf16[2,4,80,768]{3,2,1,0:T(8,128)(2,1)S(1)} collective-permute-done((bf16[2,4,80,768]{3,2,1,0:T(8,128)(2,1)S(1)}, bf16[2,4,80,768]{3,2,1,0:T(8,128)(2,1)S(1)}, u32[]{:S(2)}, u32[]{:S(2)}) %collective-permute-start.8) | collective-permute-done | bytes 983072 | tf_op jit(solution)/shard_map/ppermute | solution.py:35
  72.3 1.1 copy-done.42
  74.1 1.2 collective-permute-start.15
  75.3 2.0 collective-permute-done.11.last_far
  77.3 1.3 copy-done.43
  78.6 6.6 %head.1 = (bf16[512,768]{1,0:T(8,128)(2,1)}, bf16[512,768]{1,0:T(8,128)(2,1)}, bf16[768,512]{1,0:T(8,128)(2,1)}, bf16[128,512]{1,0:T(8,128)(2,1)}, bf16[896,768]...) custom-call(s32[32]{0:T(128)} %get-tuple-element.123.device_ref, ...), custom_call_target="tpu_custom_call" | custom-call | flops 2818572288 | bytes 8388608 | tf_op jit(solution)/shard_map/head/pallas_call | solution.py:347
  85.2 5.1 %collective-permute-start.12 = (bf16[128,512]{1,0:T(8,128)(2,1)}, bf16[128,512]{1,0:T(8,128)(2,1)S(1)}, u32[]{:S(2)}, u32[]{:S(2)}) collective-permute-start(bf16[128,512]{1,0:T(8,128)(2,1)} %get-tuple-element.136), channel_id=1, source_target_pairs={{0,16},{4,20},{8,24},{12,28},{1,17},{5,21},{9,25},{13,29},{2,18},{... | collective-permute-start | bytes 393224 | tf_op jit(solution)/shard_map/ppermute | solution.py:649
  90.2 2.4 collective-permute-start.13
  93.6 2.1 collective-permute-done.13
  95.8 1.3 collective-permute-start.16
  97.2 2.4 collective-permute-start.17
  99.6 3.2 %collective-permute-start.18 = (bf16[2,128,512]{2,1,0:T(8,128)(2,1)S(1)}, bf16[2,128,512]{2,1,0:T(8,128)(2,1)S(1)}, u32[]{:S(2)}, u32[]{:S(2)}) collective-permute-start(bf16[2,128,512]{2,1,0:T(8,128)(2,1)S(1)} %pad_maximum_fusion.23), channel_id=1, source_target_pairs={{0,8},{4,12},{8,16},{12,20},{16,24},{20,28},{1,9},{5,13},{9,17},{1... | collective-permute-start | bytes 786440 | tf_op jit(solution)/shard_map/ppermute | solution.py:649
  102.8 13.0 %feed.2 = (f32[512,768]{1,0:T(8,128)}, f32[512,768]{1,0:T(8,128)}, bf16[2,768,768]{2,1,0:T(8,128)(2,1)}, f32[2,768,768]{2,1,0:T(8,128)}, f32[1,768]{1,0:T(1,128)}, /*index=5*/f32[1,768]{1,0:T(1,128)}) custom-call(bf16[512,768]{1,0:T(8,128)(2,1)} %get-tuple-element.164.n_ref, bf16[512,768]{1,0:T(8,128)(2,1)} %bitcast.208, ...), custom_call_target="tpu_custom_call" | custom-call | flops 28991029248 | bytes 8388608 | tf_op jit(solution)/shard_map/feed/pallas_call | solution.py:241
  116.0 1.7 convolution_convert_fusion.do_ref
  119.5 1.2 collective-permute-done.20
  122.1 1.8 collective-permute-done.21.first_far
  124.9 1.6 collective-permute-start.23
  126.5 18.5 %attention.1 = (bf16[512,768]{1,0:T(8,128)(2,1)}, bf16[768,512]{1,0:T(8,128)(2,1)}, f32[128,512]{1,0:T(8,128)}, bf16[4,128,512]{2,1,0:T(8,128)(2,1)}) custom-call(bf16[768,512]{1,0:T(8,128)(2,1)} %get-tuple-element.154.q_ref, bf16[768,512]{1,0:T(8,128)(2,1)} %convolution_convert_fusion.do_ref, s32[4,1,128]{2,1,0:T(1,128)} %bitcast.207, ...), custom_call_target="tpu_custom_call" | custom-call | flops 14092861440 | bytes 8388608 | tf_op jit(solution)/shard_map/attention/pallas_call | solution.py:142
  145.0 1.1 slice_convert_fusion.6
  147.8 1.3 collective-permute-start.26
  149.1 1.3 collective-permute-start.27
  152.4 13.3 %feed.3 = (f32[512,768]{1,0:T(8,128)}, f32[512,768]{1,0:T(8,128)}, bf16[2,768,768]{2,1,0:T(8,128)(2,1)}, f32[2,768,768]{2,1,0:T(8,128)}, f32[1,768]{1,0:T(1,128)}, /*index=5*/f32[1,768]{1,0:T(1,128)}) custom-call(bf16[512,768]{1,0:T(8,128)(2,1)} %get-tuple-element.164.n_ref, bf16[512,768]{1,0:T(8,128)(2,1)} %bitcast.209, ...), custom_call_target="tpu_custom_call" | custom-call | flops 28991029248 | bytes 8388608 | tf_op jit(solution)/shard_map/feed/pallas_call | solution.py:241
  165.8 1.7 collective-permute-start.29
  167.6 5.1 %collective-permute-done.29 = bf16[1,128,512]{2,1,0:T(8,128)(2,1)S(1)} collective-permute-done((bf16[1,128,512]{2,1,0:T(8,128)(2,1)S(1)}, bf16[1,128,512]{2,1,0:T(8,128)(2,1)S(1)}, u32[]{:S(2)}, u32[]{:S(2)}) %collective-permute-start.29) | collective-permute-done | bytes 131104 | tf_op jit(solution)/shard_map/ppermute | solution.py:649
  172.7 1.6 fusion.31.dkv_ref
  174.3 9.4 %tail.1 = (bf16[512,768]{1,0:T(8,128)(2,1)}, f32[32,32,768]{2,1,0:T(8,128)}, f32[32,32,768]{2,1,0:T(8,128)}) custom-call(s32[32]{0:T(128)} %get-tuple-element.177.entry_ref, bf16[512,768]{1,0:T(8,128)(2,1)} %bitcast.184, bf16[512,768]{1,0:T(8,128)(2,1)} %bitcast.210, bf16[768,512]{1,0:T(8,128)(2,1)} %get-tuple-element.178.dq_ref, ...), custom_call_target="tpu_custom_call" | custom-call | flops 8455716864 | bytes 8388608 | tf_op jit(solution)/shard_map/tail/pallas_call | solution.py:444
  183.7 2.3 fusion.12
  186.2 3.3 %collective-permute-done.30 = bf16[2,2,2,4,32,768]{5,4,3,2,1,0:T(8,128)(2,1)S(1)} collective-permute-done((bf16[2,2,2,4,32,768]{5,4,3,2,1,0:T(8,128)(2,1)S(1)}, bf16[2,2,2,4,32,768]{5,4,3,2,1,0:T(8,128)(2,1)S(1)}, u32[]{:S(2)}, u32[]{:S(2)}) %collective-permute-start.30) | collective-permute-done | bytes 1572896 | tf_op jit(solution)/shard_map/ppermute | solution.py:35
  189.9 1.5 slice_bitcast_fusion
  192.7 1.3 fusion.14
  196.8 6.3 %collective-permute-start.35 = (bf16[96,768]{1,0:T(8,128)(2,1)}, bf16[96,768]{1,0:T(8,128)(2,1)S(1)}, u32[]{:S(2)}, u32[]{:S(2)}) collective-permute-start(bf16[96,768]{1,0:T(8,128)(2,1)} %get-tuple-element.251), channel_id=1, source_target_pairs={{0,24},{4,28},{8,16},{12,20},{16,8},{20,12},{24,0},{28,4},{1,25},{... | collective-permute-start | bytes 442376 | tf_op jit(solution)/shard_map/ppermute | solution.py:49
  203.7 1.4 fusion.15
  205.1 1.1 collective-permute-start.32
  206.2 1.9 collective-permute-done.35
  208.1 7.1 %collective-permute-done.34 = bf16[96,768]{1,0:T(8,128)(2,1)S(1)} collective-permute-done((bf16[96,768]{1,0:T(8,128)(2,1)}, bf16[96,768]{1,0:T(8,128)(2,1)S(1)}, u32[]{:S(2)}, u32[]{:S(2)}) %collective-permute-start.34) | collective-permute-done | bytes 147488 | tf_op jit(solution)/shard_map/ppermute | solution.py:49
  215.2 3.0 collective-permute-done.31
  218.3 1.4 fusion.9
  219.8 8.3 %collective-permute-done.32 = bf16[2,4,80,768]{3,2,1,0:T(8,128)(2,1)S(1)} collective-permute-done((bf16[2,4,80,768]{3,2,1,0:T(8,128)(2,1)S(1)}, bf16[2,4,80,768]{3,2,1,0:T(8,128)(2,1)S(1)}, u32[]{:S(2)}, u32[]{:S(2)}) %collective-permute-start.32) | collective-permute-done | bytes 983072 | tf_op jit(solution)/shard_map/ppermute | solution.py:35
  231.7 3.5 %collective-permute-done.38 = bf16[96,768]{1,0:T(8,128)(2,1)S(1)} collective-permute-done((bf16[96,768]{1,0:T(8,128)(2,1)S(1)}, bf16[96,768]{1,0:T(8,128)(2,1)S(1)}, u32[]{:S(2)}, u32[]{:S(2)}) %collective-permute-start.38) | collective-permute-done | bytes 147488 | tf_op jit(solution)/shard_map/ppermute | solution.py:35
  235.4 1.3 add_convert_fusion
  237.9 5.9 %collective-permute-done.37 = bf16[4,80,768]{2,1,0:T(8,128)(2,1)S(1)} collective-permute-done((bf16[4,80,768]{2,1,0:T(8,128)(2,1)S(1)}, bf16[4,80,768]{2,1,0:T(8,128)(2,1)S(1)}, u32[]{:S(2)}, u32[]{:S(2)}) %collective-permute-start.37) | collective-permute-done | bytes 491552 | tf_op jit(solution)/shard_map/ppermute | solution.py:35
  243.9 6.4 %collective-permute-done.36 = bf16[4,80,768]{2,1,0:T(8,128)(2,1)S(1)} collective-permute-done((bf16[4,80,768]{2,1,0:T(8,128)(2,1)S(1)}, bf16[4,80,768]{2,1,0:T(8,128)(2,1)S(1)}, u32[]{:S(2)}, u32[]{:S(2)}) %collective-permute-start.36) | collective-permute-done | bytes 491552 | tf_op jit(solution)/shard_map/ppermute | solution.py:35
  250.8 3.6 %collective-permute-start.42 = (bf16[160,768]{1,0:T(8,128)(2,1)S(1)}, bf16[160,768]{1,0:T(8,128)(2,1)S(1)}, u32[]{:S(2)}, u32[]{:S(2)}) collective-permute-start(bf16[160,768]{1,0:T(8,128)(2,1)S(1)} %get-tuple-element.236), channel_id=1, source_target_pairs={{0,24},{4,28},{8,16},{12,20},{16,8},{20,12},{24,0},{28,4},{1,25},{... | collective-permute-start | bytes 737288 | tf_op jit(solution)/shard_map/ppermute | solution.py:49
  255.2 6.4 %collective-permute-done.42 = bf16[160,768]{1,0:T(8,128)(2,1)S(1)} collective-permute-done((bf16[160,768]{1,0:T(8,128)(2,1)S(1)}, bf16[160,768]{1,0:T(8,128)(2,1)S(1)}, u32[]{:S(2)}, u32[]{:S(2)}) %collective-permute-start.42) | collective-permute-done | bytes 245792 | tf_op jit(solution)/shard_map/ppermute | solution.py:49
  261.6 13.5 %collective-permute-done.41 = bf16[160,768]{1,0:T(8,128)(2,1)S(1)} collective-permute-done((bf16[160,768]{1,0:T(8,128)(2,1)S(1)}, bf16[160,768]{1,0:T(8,128)(2,1)S(1)}, u32[]{:S(2)}, u32[]{:S(2)}) %collective-permute-start.41) | collective-permute-done | bytes 245792 | tf_op jit(solution)/shard_map/ppermute | solution.py:49
  276.3 5.9 %collective-permute-done.43 = bf16[160,768]{1,0:T(8,128)(2,1)S(1)} collective-permute-done((bf16[160,768]{1,0:T(8,128)(2,1)S(1)}, bf16[160,768]{1,0:T(8,128)(2,1)S(1)}, u32[]{:S(2)}, u32[]{:S(2)}) %collective-permute-start.43) | collective-permute-done | bytes 245792 | tf_op jit(solution)/shard_map/ppermute | solution.py:35
  282.4 1.8 collective-permute-done.44
  285.6 3.7 %copy-done = f32[4,768,768]{2,1,0:T(8,128)S(1)} copy-done((f32[4,768,768]{2,1,0:T(8,128)S(1)}, f32[4,768,768]{2,1,0:T(8,128)}, u32[]{:S(2)}) %copy-start) | copy-done | bytes 9437208
  289.3 2.9 update.4
  292.3 3.7 %copy-done.1 = f32[4,768,768]{2,1,0:T(8,128)S(1)} copy-done((f32[4,768,768]{2,1,0:T(8,128)S(1)}, f32[4,768,768]{2,1,0:T(8,128)}, u32[]{:S(2)}) %copy-start.1) | copy-done | bytes 9437208
  296.0 2.7 update.5
  298.8 4.9 %update.6 = (f32[384,768]{1,0:T(8,128)}, f32[384,768]{1,0:T(8,128)}, f32[384,768]{1,0:T(8,128)}, f32[384,768]{1,0:T(8,128)}) custom-call(bf16[384,768]{1,0:T(8,128)(2,1)S(1)} %bitcast.161, f32[4,768,768]{2,1,0:T(8,128)S(1)} %copy-done.1, f32[384,768]{1,0:T(8,128)S(1)} %copy-done.3, f32[384,768]{1,0:T(8,128)S(1)} %copy-done.5, f32[384,768]{1,0:T(8,128)S(1)} %copy-done.6), custom_call_target="tpu_custom_call" | custom-call | flops 2264924160 | bytes 8388608 | tf_op jit(solution)/shard_map/update/pallas_call | solution.py:493
  303.7 5.2 %update.7 = (f32[768,384]{1,0:T(8,128)}, f32[768,384]{1,0:T(8,128)}, f32[768,384]{1,0:T(8,128)}, f32[768,384]{1,0:T(8,128)}) custom-call(bf16[384,768]{1,0:T(8,128)(2,1)S(1)} %bitcast.160, f32[4,768,768]{2,1,0:T(8,128)S(1)} %copy-done.1, f32[768,384]{1,0:T(8,128)S(1)} %copy-done.2, f32[768,384]{1,0:T(8,128)S(1)} %copy-done.7, f32[768,384]{1,0:T(8,128)S(1)} %copy-done.8), custom_call_target="tpu_custom_call" | custom-call | flops 2264924160 | bytes 8388608 | tf_op jit(solution)/shard_map/update/pallas_call | solution.py:493
  (241 shorter events, 32.3 us)
Async XLA Ops:
  0.7 9.1 %copy-start.41 = (s32[4,8]{1,0:T(4,128)S(1)}, s32[4,8]{1,0:T(4,128)}, u32[]{:S(2)}) copy-start(s32[4,8]{1,0:T(4,128)} %param.21) | copy-start | bytes 388
  3.5 13.5 %collective-permute-start = (bf16[160,768]{1,0:T(8,128)(2,1)S(1)}, bf16[160,768]{1,0:T(8,128)(2,1)S(1)}, u32[]{:S(2)}, u32[]{:S(2)}) collective-permute-start(bf16[160,768]{1,0:T(8,128)(2,1)S(1)} %constant_dynamic-update-slice_fusion), channel_id=1, source_target_pairs={{0,8},{4,12},{8,0},{12,4},{16,24},{20,28},{24,16},{28,20},{1,9},{5... | collective-permute-start | bytes 737288 | tf_op jit(solution)/shard_map/ppermute | solution.py:49
  6.6 20.3 %collective-permute-start.1 = (bf16[160,768]{1,0:T(8,128)(2,1)S(1)}, bf16[160,768]{1,0:T(8,128)(2,1)S(1)}, u32[]{:S(2)}, u32[]{:S(2)}) collective-permute-start(bf16[160,768]{1,0:T(8,128)(2,1)S(1)} %constant_dynamic-update-slice_fusion), channel_id=1, source_target_pairs={{0,16},{4,20},{8,24},{12,28},{16,0},{20,4},{24,8},{28,12},{1,17},{... | collective-permute-start | bytes 737288 | tf_op jit(solution)/shard_map/ppermute | solution.py:49
  9.2 17.7 %collective-permute-start.2 = (bf16[160,768]{1,0:T(8,128)(2,1)S(1)}, bf16[160,768]{1,0:T(8,128)(2,1)S(1)}, u32[]{:S(2)}, u32[]{:S(2)}) collective-permute-start(bf16[160,768]{1,0:T(8,128)(2,1)S(1)} %constant_dynamic-update-slice_fusion), channel_id=1, source_target_pairs={{0,24},{4,28},{8,16},{12,20},{16,8},{20,12},{24,0},{28,4},{1,25},{... | collective-permute-start | bytes 737288 | tf_op jit(solution)/shard_map/ppermute | solution.py:49
  27.2 19.6 %collective-permute-start.3 = (bf16[4,80,768]{2,1,0:T(8,128)(2,1)S(1)}, bf16[4,80,768]{2,1,0:T(8,128)(2,1)S(1)}, u32[]{:S(2)}, u32[]{:S(2)}) collective-permute-start(bf16[4,80,768]{2,1,0:T(8,128)(2,1)S(1)} %get-tuple-element.245), channel_id=1, source_target_pairs={{0,4},{4,0},{8,12},{12,8},{16,20},{20,16},{24,28},{28,24},{1,5},{5... | collective-permute-start | bytes 1474568 | tf_op jit(solution)/shard_map/ppermute | solution.py:35
  28.8 18.0 %collective-permute-start.4 = (bf16[4,80,768]{2,1,0:T(8,128)(2,1)S(1)}, bf16[4,80,768]{2,1,0:T(8,128)(2,1)S(1)}, u32[]{:S(2)}, u32[]{:S(2)}) collective-permute-start(bf16[4,80,768]{2,1,0:T(8,128)(2,1)S(1)} %get-tuple-element.244), channel_id=1, source_target_pairs={{0,2},{1,3},{2,0},{3,1},{4,6},{5,7},{6,4},{7,5},{8,10},{9,11},{10,... | collective-permute-start | bytes 1474568 | tf_op jit(solution)/shard_map/ppermute | solution.py:35
  30.3 8.6 %collective-permute-start.5 = (bf16[96,768]{1,0:T(8,128)(2,1)S(1)}, bf16[96,768]{1,0:T(8,128)(2,1)S(1)}, u32[]{:S(2)}, u32[]{:S(2)}) collective-permute-start(bf16[96,768]{1,0:T(8,128)(2,1)S(1)} %pad_maximum_fusion.24), channel_id=1, source_target_pairs={{0,8},{4,12},{8,0},{12,4},{16,24},{20,28},{24,16},{28,20},{1,9},{5... | collective-permute-start | bytes 442376 | tf_op jit(solution)/shard_map/ppermute | solution.py:49
  34.5 12.3 %collective-permute-start.6 = (bf16[96,768]{1,0:T(8,128)(2,1)S(1)}, bf16[96,768]{1,0:T(8,128)(2,1)S(1)}, u32[]{:S(2)}, u32[]{:S(2)}) collective-permute-start(bf16[96,768]{1,0:T(8,128)(2,1)S(1)} %pad_maximum_fusion.24), channel_id=1, source_target_pairs={{0,16},{4,20},{8,24},{12,28},{16,0},{20,4},{24,8},{28,12},{1,17},{... | collective-permute-start | bytes 442376 | tf_op jit(solution)/shard_map/ppermute | solution.py:49
  35.5 11.2 %collective-permute-start.7 = (bf16[96,768]{1,0:T(8,128)(2,1)S(1)}, bf16[96,768]{1,0:T(8,128)(2,1)S(1)}, u32[]{:S(2)}, u32[]{:S(2)}) collective-permute-start(bf16[96,768]{1,0:T(8,128)(2,1)S(1)} %pad_maximum_fusion.24), channel_id=1, source_target_pairs={{0,24},{4,28},{8,16},{12,20},{16,8},{20,12},{24,0},{28,4},{1,25},{... | collective-permute-start | bytes 442376 | tf_op jit(solution)/shard_map/ppermute | solution.py:49
  47.3 25.0 %copy-start.26 = (bf16[2,2,4,80,768]{4,3,2,1,0:T(8,128)(2,1)}, bf16[2,2,4,80,768]{4,3,2,1,0:T(8,128)(2,1)S(1)}, u32[]{:S(2)}) copy-start(bf16[2,2,4,80,768]{4,3,2,1,0:T(8,128)(2,1)S(1)} %pad_maximum_fusion.3.first_near) | copy-start | bytes 5898244
  47.3 24.8 %collective-permute-start.10 = (bf16[2,2,4,80,768]{4,3,2,1,0:T(8,128)(2,1)S(1)}, bf16[2,2,4,80,768]{4,3,2,1,0:T(8,128)(2,1)S(1)}, u32[]{:S(2)}, u32[]{:S(2)}) collective-permute-start(bf16[2,2,4,80,768]{4,3,2,1,0:T(8,128)(2,1)S(1)} %pad_maximum_fusion.3.first_near), channel_id=1, source_target_pairs={{0,1},{1,0},{2,3},{3,2},{4,5},{5,4},{6,7},{7,6},{8,9},{9,8},{10,11... | collective-permute-start | bytes 5898248 | tf_op jit(solution)/shard_map/ppermute | solution.py:35
  47.3 24.2 %collective-permute-start.8 = (bf16[2,4,80,768]{3,2,1,0:T(8,128)(2,1)S(1)}, bf16[2,4,80,768]{3,2,1,0:T(8,128)(2,1)S(1)}, u32[]{:S(2)}, u32[]{:S(2)}) collective-permute-start(bf16[2,4,80,768]{3,2,1,0:T(8,128)(2,1)S(1)} %get-tuple-element.240), channel_id=1, source_target_pairs={{0,2},{1,3},{2,0},{3,1},{4,6},{5,7},{6,4},{7,5},{8,10},{9,11},{10,... | collective-permute-start | bytes 2949128 | tf_op jit(solution)/shard_map/ppermute | solution.py:35
  48.2 23.8 %collective-permute-start.9 = (bf16[2,4,80,768]{3,2,1,0:T(8,128)(2,1)S(1)}, bf16[2,4,80,768]{3,2,1,0:T(8,128)(2,1)S(1)}, u32[]{:S(2)}, u32[]{:S(2)}) collective-permute-start(bf16[2,4,80,768]{3,2,1,0:T(8,128)(2,1)S(1)} %get-tuple-element.238), channel_id=1, source_target_pairs={{0,4},{4,0},{8,12},{12,8},{16,20},{20,16},{24,28},{28,24},{1,5},{5... | collective-permute-start | bytes 2949128 | tf_op jit(solution)/shard_map/ppermute | solution.py:35
  73.4 4.0 %collective-permute-start.11 = (bf16[2,2,4,80,768]{4,3,2,1,0:T(8,128)(2,1)S(1)}, bf16[2,2,4,80,768]{4,3,2,1,0:T(8,128)(2,1)S(1)}, u32[]{:S(2)}, u32[]{:S(2)}) collective-permute-start(bf16[2,2,4,80,768]{4,3,2,1,0:T(8,128)(2,1)S(1)} %pad_maximum_fusion.4.last_near), channel_id=1, source_target_pairs={{0,1},{1,0},{2,3},{3,2},{4,5},{5,4},{6,7},{7,6},{8,9},{9,8},{10,11... | collective-permute-start | bytes 5898248 | tf_op jit(solution)/shard_map/ppermute | solution.py:35
  73.5 19.2 %collective-permute-start.14 = (bf16[4,48,768]{2,1,0:T(8,128)(2,1)S(1)}, bf16[4,48,768]{2,1,0:T(8,128)(2,1)S(1)}, u32[]{:S(2)}, u32[]{:S(2)}) collective-permute-start(bf16[4,48,768]{2,1,0:T(8,128)(2,1)S(1)} %get-tuple-element.260), channel_id=1, source_target_pairs={{0,4},{4,0},{8,12},{12,8},{16,20},{20,16},{24,28},{28,24},{1,5},{5... | collective-permute-start | bytes 884744 | tf_op jit(solution)/shard_map/ppermute | solution.py:35
  74.1 18.6 %collective-permute-start.15 = (bf16[4,48,768]{2,1,0:T(8,128)(2,1)S(1)}, bf16[4,48,768]{2,1,0:T(8,128)(2,1)S(1)}, u32[]{:S(2)}, u32[]{:S(2)}) collective-permute-start(bf16[4,48,768]{2,1,0:T(8,128)(2,1)S(1)} %get-tuple-element.259), channel_id=1, source_target_pairs={{0,2},{1,3},{2,0},{3,1},{4,6},{5,7},{6,4},{7,5},{8,10},{9,11},{10,... | collective-permute-start | bytes 884744 | tf_op jit(solution)/shard_map/ppermute | solution.py:35
  85.2 8.5 %collective-permute-start.12 = (bf16[128,512]{1,0:T(8,128)(2,1)}, bf16[128,512]{1,0:T(8,128)(2,1)S(1)}, u32[]{:S(2)}, u32[]{:S(2)}) collective-permute-start(bf16[128,512]{1,0:T(8,128)(2,1)} %get-tuple-element.136), channel_id=1, source_target_pairs={{0,16},{4,20},{8,24},{12,28},{1,17},{5,21},{9,25},{13,29},{2,18},{... | collective-permute-start | bytes 393224 | tf_op jit(solution)/shard_map/ppermute | solution.py:649
  90.2 5.5 %collective-permute-start.13 = (bf16[1,128,512]{2,1,0:T(8,128)(2,1)}, bf16[1,128,512]{2,1,0:T(8,128)(2,1)S(1)}, u32[]{:S(2)}, u32[]{:S(2)}) collective-permute-start(bf16[1,128,512]{2,1,0:T(8,128)(2,1)} %bitcast.191), channel_id=1, source_target_pairs={{0,4},{4,8},{8,12},{12,16},{16,20},{20,24},{24,28},{1,5},{5,9},{9,... | collective-permute-start | bytes 393224 | tf_op jit(solution)/shard_map/ppermute | solution.py:649
  95.8 20.1 %collective-permute-start.16 = (bf16[2,4,48,768]{3,2,1,0:T(8,128)(2,1)S(1)}, bf16[2,4,48,768]{3,2,1,0:T(8,128)(2,1)S(1)}, u32[]{:S(2)}, u32[]{:S(2)}) collective-permute-start(bf16[2,4,48,768]{3,2,1,0:T(8,128)(2,1)S(1)} %get-tuple-element.254), channel_id=1, source_target_pairs={{0,2},{1,3},{2,0},{3,1},{4,6},{5,7},{6,4},{7,5},{8,10},{9,11},{10,... | collective-permute-start | bytes 1769480 | tf_op jit(solution)/shard_map/ppermute | solution.py:35
  97.2 18.7 %collective-permute-start.17 = (bf16[2,4,48,768]{3,2,1,0:T(8,128)(2,1)S(1)}, bf16[2,4,48,768]{3,2,1,0:T(8,128)(2,1)S(1)}, u32[]{:S(2)}, u32[]{:S(2)}) collective-permute-start(bf16[2,4,48,768]{3,2,1,0:T(8,128)(2,1)S(1)} %get-tuple-element.256), channel_id=1, source_target_pairs={{0,4},{4,0},{8,12},{12,8},{16,20},{20,16},{24,28},{28,24},{1,5},{5... | collective-permute-start | bytes 1769480 | tf_op jit(solution)/shard_map/ppermute | solution.py:35
  99.6 16.2 %collective-permute-start.18 = (bf16[2,128,512]{2,1,0:T(8,128)(2,1)S(1)}, bf16[2,128,512]{2,1,0:T(8,128)(2,1)S(1)}, u32[]{:S(2)}, u32[]{:S(2)}) collective-permute-start(bf16[2,128,512]{2,1,0:T(8,128)(2,1)S(1)} %pad_maximum_fusion.23), channel_id=1, source_target_pairs={{0,8},{4,12},{8,16},{12,20},{16,24},{20,28},{1,9},{5,13},{9,17},{1... | collective-permute-start | bytes 786440 | tf_op jit(solution)/shard_map/ppermute | solution.py:649
  102.8 13.2 %copy-start.45 = (bf16[4,128,768]{2,1,0:T(8,128)(2,1)S(1)}, bf16[4,128,768]{2,1,0:T(8,128)(2,1)}, u32[]{:S(2)}) copy-start(bf16[4,128,768]{2,1,0:T(8,128)(2,1)} %param.20) | copy-start | bytes 2359300
  102.8 13.2 %copy-start.46 = (bf16[768,768]{1,0:T(8,128)(2,1)S(1)}, bf16[768,768]{1,0:T(8,128)(2,1)}, u32[]{:S(2)}) copy-start(bf16[768,768]{1,0:T(8,128)(2,1)} %get-tuple-element.155) | copy-start | bytes 3538948
  115.9 4.8 %collective-permute-start.20 = (bf16[2,768,768]{2,1,0:T(8,128)(2,1)}, bf16[2,768,768]{2,1,0:T(8,128)(2,1)S(1)}, u32[]{:S(2)}, u32[]{:S(2)}) collective-permute-start(bf16[2,768,768]{2,1,0:T(8,128)(2,1)} %get-tuple-element.152), channel_id=1, source_target_pairs={{0,1},{1,0},{2,3},{3,2},{4,5},{5,4},{6,7},{7,6},{8,9},{9,8},{10,11... | collective-permute-start | bytes 7077896 | tf_op jit(solution)/shard_map/ppermute | solution.py:35
  117.8 6.0 %collective-permute-start.21 = (bf16[2,2,4,48,768]{4,3,2,1,0:T(8,128)(2,1)S(1)}, bf16[2,2,4,48,768]{4,3,2,1,0:T(8,128)(2,1)S(1)}, u32[]{:S(2)}, u32[]{:S(2)}) collective-permute-start(bf16[2,2,4,48,768]{4,3,2,1,0:T(8,128)(2,1)S(1)} %pad_maximum_fusion.8.first_near), channel_id=1, source_target_pairs={{0,1},{1,0},{2,3},{3,2},{4,5},{5,4},{6,7},{7,6},{8,9},{9,8},{10,11... | collective-permute-start | bytes 3538952 | tf_op jit(solution)/shard_map/ppermute | solution.py:35
  118.5 32.3 %collective-permute-start.19 = (bf16[2,2,4,48,768]{4,3,2,1,0:T(8,128)(2,1)S(1)}, bf16[2,2,4,48,768]{4,3,2,1,0:T(8,128)(2,1)}, u32[]{:S(2)}, u32[]{:S(2)}) collective-permute-start(bf16[2,2,4,48,768]{4,3,2,1,0:T(8,128)(2,1)S(1)} %pad_maximum_fusion.7.last_near), channel_id=1, source_target_pairs={{0,1},{1,0},{2,3},{3,2},{4,5},{5,4},{6,7},{7,6},{8,9},{9,8},{10,11... | collective-permute-start | bytes 3538952 | tf_op jit(solution)/shard_map/ppermute | solution.py:35
  123.9 26.5 %collective-permute-start.22 = (bf16[2,4,48,768]{3,2,1,0:T(8,128)(2,1)S(1)}, bf16[2,4,48,768]{3,2,1,0:T(8,128)(2,1)S(1)}, u32[]{:S(2)}, u32[]{:S(2)}) collective-permute-start(bf16[2,4,48,768]{3,2,1,0:T(8,128)(2,1)S(1)} %bitcast.187), channel_id=1, source_target_pairs={{0,2},{1,3},{2,0},{3,1},{4,6},{5,7},{6,4},{7,5},{8,10},{9,11},{10,... | collective-permute-start | bytes 1769480 | tf_op jit(solution)/shard_map/ppermute | solution.py:35
  124.9 25.7 %collective-permute-start.23 = (bf16[2,4,48,768]{3,2,1,0:T(8,128)(2,1)S(1)}, bf16[2,4,48,768]{3,2,1,0:T(8,128)(2,1)S(1)}, u32[]{:S(2)}, u32[]{:S(2)}) collective-permute-start(bf16[2,4,48,768]{3,2,1,0:T(8,128)(2,1)S(1)} %fusion.16), channel_id=1, source_target_pairs={{0,4},{4,0},{8,12},{12,8},{16,20},{20,16},{24,28},{28,24},{1,5},{5... | collective-permute-start | bytes 1769480 | tf_op jit(solution)/shard_map/ppermute | solution.py:35
  147.8 17.8 %collective-permute-start.26 = (bf16[128,512]{1,0:T(8,128)(2,1)S(1)}, bf16[128,512]{1,0:T(8,128)(2,1)}, u32[]{:S(2)}, u32[]{:S(2)}) collective-permute-start(bf16[128,512]{1,0:T(8,128)(2,1)S(1)} %slice_bitcast_fusion.13), channel_id=1, source_target_pairs={{16,0},{20,4},{24,8},{28,12},{17,1},{21,5},{25,9},{29,13},{18,2},{... | collective-permute-start | bytes 393224 | tf_op jit(solution)/shard_map/ppermute | solution.py:649
  149.1 16.6 %collective-permute-start.27 = (bf16[2,128,512]{2,1,0:T(8,128)(2,1)}, bf16[2,128,512]{2,1,0:T(8,128)(2,1)S(1)}, u32[]{:S(2)}, u32[]{:S(2)}) collective-permute-start(bf16[2,128,512]{2,1,0:T(8,128)(2,1)} %slice.201), channel_id=1, source_target_pairs={{8,0},{12,4},{16,8},{20,12},{24,16},{28,20},{9,1},{13,5},{17,9},{2... | collective-permute-start | bytes 786440 | tf_op jit(solution)/shard_map/ppermute | solution.py:649
  150.9 14.8 %collective-permute-start.24 = (bf16[4,48,768]{2,1,0:T(8,128)(2,1)S(1)}, bf16[4,48,768]{2,1,0:T(8,128)(2,1)S(1)}, u32[]{:S(2)}, u32[]{:S(2)}) collective-permute-start(bf16[4,48,768]{2,1,0:T(8,128)(2,1)S(1)} %fusion.23), channel_id=1, source_target_pairs={{0,4},{4,0},{8,12},{12,8},{16,20},{20,16},{24,28},{28,24},{1,5},{5... | collective-permute-start | bytes 884744 | tf_op jit(solution)/shard_map/ppermute | solution.py:35
  151.3 14.3 %collective-permute-start.25 = (bf16[4,48,768]{2,1,0:T(8,128)(2,1)S(1)}, bf16[4,48,768]{2,1,0:T(8,128)(2,1)S(1)}, u32[]{:S(2)}, u32[]{:S(2)}) collective-permute-start(bf16[4,48,768]{2,1,0:T(8,128)(2,1)S(1)} %fusion.24), channel_id=1, source_target_pairs={{0,2},{1,3},{2,0},{3,1},{4,6},{5,7},{6,4},{7,5},{8,10},{9,11},{10,... | collective-permute-start | bytes 884744 | tf_op jit(solution)/shard_map/ppermute | solution.py:35
  152.4 13.3 %copy-start.34 = (f32[128,512]{1,0:T(8,128)S(1)}, f32[128,512]{1,0:T(8,128)}, u32[]{:S(2)}) copy-start(f32[128,512]{1,0:T(8,128)} %get-tuple-element.179) | copy-start | bytes 786436
  165.8 6.9 %collective-permute-start.29 = (bf16[1,128,512]{2,1,0:T(8,128)(2,1)S(1)}, bf16[1,128,512]{2,1,0:T(8,128)(2,1)S(1)}, u32[]{:S(2)}, u32[]{:S(2)}) collective-permute-start(bf16[1,128,512]{2,1,0:T(8,128)(2,1)S(1)} %slice.373), channel_id=1, source_target_pairs={{4,0},{8,4},{12,8},{16,12},{20,16},{24,20},{28,24},{5,1},{9,5},{13... | collective-permute-start | bytes 393224 | tf_op jit(solution)/shard_map/ppermute | solution.py:649
  167.5 23.9 %collective-permute-start.28 = (bf16[2,768,768]{2,1,0:T(8,128)(2,1)}, bf16[2,768,768]{2,1,0:T(8,128)(2,1)S(1)}, u32[]{:S(2)}, u32[]{:S(2)}) collective-permute-start(bf16[2,768,768]{2,1,0:T(8,128)(2,1)} %get-tuple-element.176), channel_id=1, source_target_pairs={{0,1},{1,0},{2,3},{3,2},{4,5},{5,4},{6,7},{7,6},{8,9},{9,8},{10,11... | collective-permute-start | bytes 7077896 | tf_op jit(solution)/shard_map/ppermute | solution.py:35
  183.7 5.8 %copy-start.19 = (f32[32,32,768]{2,1,0:T(8,128)S(1)}, f32[32,32,768]{2,1,0:T(8,128)}, u32[]{:S(2)}) copy-start(f32[32,32,768]{2,1,0:T(8,128)} %get-tuple-element.191) | copy-start | bytes 9437188
  183.7 5.8 %copy-start.20 = (f32[32,32,768]{2,1,0:T(8,128)S(1)}, f32[32,32,768]{2,1,0:T(8,128)}, u32[]{:S(2)}) copy-start(f32[32,32,768]{2,1,0:T(8,128)} %get-tuple-element.192) | copy-start | bytes 9437188
  186.0 3.5 %collective-permute-start.30 = (bf16[2,2,2,4,32,768]{5,4,3,2,1,0:T(8,128)(2,1)S(1)}, bf16[2,2,2,4,32,768]{5,4,3,2,1,0:T(8,128)(2,1)S(1)}, u32[]{:S(2)}, u32[]{:S(2)}) collective-permute-start(bf16[2,2,2,4,32,768]{5,4,3,2,1,0:T(8,128)(2,1)S(1)} %fusion.12), channel_id=1, source_target_pairs={{0,1},{1,0},{2,3},{3,2},{4,5},{5,4},{6,7},{7,6},{8,9},{9,8},{10,11... | collective-permute-start | bytes 4718600 | tf_op jit(solution)/shard_map/ppermute | solution.py:35
  186.1 5.3 %slice-start = ((s8[4718592]{0:T(1024)(128)(4,1)}), s8[4194304]{0:T(1024)(128)(4,1)S(1)}, s32[]{:S(2)}) async-start(s8[4718592]{0:T(1024)(128)(4,1)} %bitcast.174), calls=%async_computation | async-start | bytes 8388608
  186.1 9.1 %copy-start.21 = (f32[4,48,768]{2,1,0:T(8,128)}, f32[4,48,768]{2,1,0:T(8,128)S(1)}, u32[]{:S(2)}) copy-start(f32[4,48,768]{2,1,0:T(8,128)S(1)} %convert_add_fusion.7) | copy-start | bytes 1769476
  186.2 5.3 %slice-start.1 = ((s8[4718592]{0:T(1024)(128)(4,1)}), s8[524288]{0:T(1024)(128)(4,1)S(1)}, s32[]{:S(2)}) async-start(s8[4718592]{0:T(1024)(128)(4,1)} %bitcast.174), calls=%async_computation.1 | async-start | bytes 1048576
  194.1 24.1 %collective-permute-start.31 = (bf16[2,4,80,768]{3,2,1,0:T(8,128)(2,1)}, bf16[2,4,80,768]{3,2,1,0:T(8,128)(2,1)}, u32[]{:S(2)}, u32[]{:S(2)}) collective-permute-start(bf16[2,4,80,768]{3,2,1,0:T(8,128)(2,1)} %fusion.14), channel_id=1, source_target_pairs={{0,2},{1,3},{2,0},{3,1},{4,6},{5,7},{6,4},{7,5},{8,10},{9,11},{10,... | collective-permute-start | bytes 2949128 | tf_op jit(solution)/shard_map/ppermute | solution.py:35
  195.2 8.4 %copy-start.40 = (f32[1,768]{1,0:T(1,128)S(1)}, f32[1,768]{1,0:T(1,128)}, u32[]{:S(2)}) copy-start(f32[1,768]{1,0:T(1,128)} %get-tuple-element.203) | copy-start | bytes 9220
  196.8 11.3 %collective-permute-start.35 = (bf16[96,768]{1,0:T(8,128)(2,1)}, bf16[96,768]{1,0:T(8,128)(2,1)S(1)}, u32[]{:S(2)}, u32[]{:S(2)}) collective-permute-start(bf16[96,768]{1,0:T(8,128)(2,1)} %get-tuple-element.251), channel_id=1, source_target_pairs={{0,24},{4,28},{8,16},{12,20},{16,8},{20,12},{24,0},{28,4},{1,25},{... | collective-permute-start | bytes 442376 | tf_op jit(solution)/shard_map/ppermute | solution.py:49
  203.1 12.1 %collective-permute-start.34 = (bf16[96,768]{1,0:T(8,128)(2,1)}, bf16[96,768]{1,0:T(8,128)(2,1)S(1)}, u32[]{:S(2)}, u32[]{:S(2)}) collective-permute-start(bf16[96,768]{1,0:T(8,128)(2,1)} %get-tuple-element.252), channel_id=1, source_target_pairs={{0,16},{4,20},{8,24},{12,28},{16,0},{20,4},{24,8},{28,12},{1,17},{... | collective-permute-start | bytes 442376 | tf_op jit(solution)/shard_map/ppermute | solution.py:49
  203.1 12.1 %collective-permute-start.33 = (bf16[96,768]{1,0:T(8,128)(2,1)}, bf16[96,768]{1,0:T(8,128)(2,1)S(1)}, u32[]{:S(2)}, u32[]{:S(2)}) collective-permute-start(bf16[96,768]{1,0:T(8,128)(2,1)} %get-tuple-element.250), channel_id=1, source_target_pairs={{0,8},{4,12},{8,0},{12,4},{16,24},{20,28},{24,16},{28,20},{1,9},{5... | collective-permute-start | bytes 442376 | tf_op jit(solution)/shard_map/ppermute | solution.py:49
  203.7 11.5 %copy-start.22 = (f32[4,48,768]{2,1,0:T(8,128)S(1)}, f32[4,48,768]{2,1,0:T(8,128)}, u32[]{:S(2)}) copy-start(f32[4,48,768]{2,1,0:T(8,128)} %copy-done.21) | copy-start | bytes 1769476
  203.7 11.5 %copy-start.24 = (f32[4,48,768]{2,1,0:T(8,128)S(1)}, f32[4,48,768]{2,1,0:T(8,128)}, u32[]{:S(2)}) copy-start(f32[4,48,768]{2,1,0:T(8,128)} %copy-done.23) | copy-start | bytes 1769476
  203.7 14.6 %copy-start.15 = (f32[1,768,768]{2,1,0:T(8,128)S(1)}, f32[1,768,768]{2,1,0:T(8,128)}, u32[]{:S(2)}) copy-start(f32[1,768,768]{2,1,0:T(8,128)} %copy-done.14) | copy-start | bytes 7077892
  205.1 13.2 %copy-start.18 = (f32[2,2,4,32,768]{4,3,2,1,0:T(8,128)S(1)}, f32[2,2,4,32,768]{4,3,2,1,0:T(8,128)}, u32[]{:S(2)}) copy-start(f32[2,2,4,32,768]{4,3,2,1,0:T(8,128)} %copy-done.17) | copy-start | bytes 4718596
  205.1 23.0 %collective-permute-start.32 = (bf16[2,4,80,768]{3,2,1,0:T(8,128)(2,1)S(1)}, bf16[2,4,80,768]{3,2,1,0:T(8,128)(2,1)S(1)}, u32[]{:S(2)}, u32[]{:S(2)}) collective-permute-start(bf16[2,4,80,768]{3,2,1,0:T(8,128)(2,1)S(1)} %fusion.15), channel_id=1, source_target_pairs={{0,4},{4,0},{8,12},{12,8},{16,20},{20,16},{24,28},{28,24},{1,5},{5... | collective-permute-start | bytes 2949128 | tf_op jit(solution)/shard_map/ppermute | solution.py:35
  219.7 8.5 %copy-start.16 = (f32[2,2,4,32,768]{4,3,2,1,0:T(8,128)S(1)}, f32[2,2,4,32,768]{4,3,2,1,0:T(8,128)}, u32[]{:S(2)}) copy-start(f32[2,2,4,32,768]{4,3,2,1,0:T(8,128)} %get-tuple-element.229) | copy-start | bytes 4718596
  228.5 6.9 %copy-start.28 = (f32[512,768]{1,0:T(8,128)S(1)}, f32[512,768]{1,0:T(8,128)}, u32[]{:S(2)}) copy-start(f32[512,768]{1,0:T(8,128)} %get-tuple-element.202) | copy-start | bytes 4718596
  228.5 6.9 %copy-start.32 = (bf16[4,128,768]{2,1,0:T(8,128)(2,1)S(1)}, bf16[4,128,768]{2,1,0:T(8,128)(2,1)}, u32[]{:S(2)}) copy-start(bf16[4,128,768]{2,1,0:T(8,128)(2,1)} %param.19) | copy-start | bytes 2359300
  228.5 6.7 %collective-permute-start.38 = (bf16[96,768]{1,0:T(8,128)(2,1)S(1)}, bf16[96,768]{1,0:T(8,128)(2,1)S(1)}, u32[]{:S(2)}, u32[]{:S(2)}) collective-permute-start(bf16[96,768]{1,0:T(8,128)(2,1)S(1)} %fusion.29), channel_id=1, source_target_pairs={{0,2},{1,3},{2,0},{3,1},{4,6},{5,7},{6,4},{7,5},{8,10},{9,11},{10,... | collective-permute-start | bytes 442376 | tf_op jit(solution)/shard_map/ppermute | solution.py:35
  230.7 13.1 %collective-permute-start.37 = (bf16[4,80,768]{2,1,0:T(8,128)(2,1)S(1)}, bf16[4,80,768]{2,1,0:T(8,128)(2,1)S(1)}, u32[]{:S(2)}, u32[]{:S(2)}) collective-permute-start(bf16[4,80,768]{2,1,0:T(8,128)(2,1)S(1)} %fusion.19), channel_id=1, source_target_pairs={{0,2},{1,3},{2,0},{3,1},{4,6},{5,7},{6,4},{7,5},{8,10},{9,11},{10,... | collective-permute-start | bytes 1474568 | tf_op jit(solution)/shard_map/ppermute | solution.py:35
  235.3 2.4 collective-permute-start.39
  236.7 13.6 %collective-permute-start.36 = (bf16[4,80,768]{2,1,0:T(8,128)(2,1)S(1)}, bf16[4,80,768]{2,1,0:T(8,128)(2,1)S(1)}, u32[]{:S(2)}, u32[]{:S(2)}) collective-permute-start(bf16[4,80,768]{2,1,0:T(8,128)(2,1)S(1)} %fusion.18), channel_id=1, source_target_pairs={{0,4},{4,0},{8,12},{12,8},{16,20},{20,16},{24,28},{28,24},{1,5},{5... | collective-permute-start | bytes 1474568 | tf_op jit(solution)/shard_map/ppermute | solution.py:35
  250.8 10.8 %collective-permute-start.42 = (bf16[160,768]{1,0:T(8,128)(2,1)S(1)}, bf16[160,768]{1,0:T(8,128)(2,1)S(1)}, u32[]{:S(2)}, u32[]{:S(2)}) collective-permute-start(bf16[160,768]{1,0:T(8,128)(2,1)S(1)} %get-tuple-element.236), channel_id=1, source_target_pairs={{0,24},{4,28},{8,16},{12,20},{16,8},{20,12},{24,0},{28,4},{1,25},{... | collective-permute-start | bytes 737288 | tf_op jit(solution)/shard_map/ppermute | solution.py:49
  254.4 20.7 %collective-permute-start.41 = (bf16[160,768]{1,0:T(8,128)(2,1)S(1)}, bf16[160,768]{1,0:T(8,128)(2,1)S(1)}, u32[]{:S(2)}, u32[]{:S(2)}) collective-permute-start(bf16[160,768]{1,0:T(8,128)(2,1)S(1)} %get-tuple-element.237), channel_id=1, source_target_pairs={{0,16},{4,20},{8,24},{12,28},{16,0},{20,4},{24,8},{28,12},{1,17},{... | collective-permute-start | bytes 737288 | tf_op jit(solution)/shard_map/ppermute | solution.py:49
  254.4 20.7 %collective-permute-start.40 = (bf16[160,768]{1,0:T(8,128)(2,1)S(1)}, bf16[160,768]{1,0:T(8,128)(2,1)S(1)}, u32[]{:S(2)}, u32[]{:S(2)}) collective-permute-start(bf16[160,768]{1,0:T(8,128)(2,1)S(1)} %get-tuple-element.235), channel_id=1, source_target_pairs={{0,8},{4,12},{8,0},{12,4},{16,24},{20,28},{24,16},{28,20},{1,9},{5... | collective-permute-start | bytes 737288 | tf_op jit(solution)/shard_map/ppermute | solution.py:49
  275.2 7.0 %collective-permute-start.43 = (bf16[160,768]{1,0:T(8,128)(2,1)S(1)}, bf16[160,768]{1,0:T(8,128)(2,1)S(1)}, u32[]{:S(2)}, u32[]{:S(2)}) collective-permute-start(bf16[160,768]{1,0:T(8,128)(2,1)S(1)} %fusion.22), channel_id=1, source_target_pairs={{0,2},{1,3},{2,0},{3,1},{4,6},{5,7},{6,4},{7,5},{8,10},{9,11},{10,... | collective-permute-start | bytes 737288 | tf_op jit(solution)/shard_map/ppermute | solution.py:35
  282.3 1.9 collective-permute-start.44
  284.7 24.2 %copy-start.35 = (f32[1072]{0:T(1024)}, f32[1072]{0:T(1024)S(1)}, u32[]{:S(2)}) copy-start(f32[1072]{0:T(1024)S(1)} %reshape.213) | copy-start | bytes 12868
  (32 other events, 91.4 us)

commit v2 on v1

--- a/solution.py
+++ b/solution.py
@@ -479,26 +479,18 @@
     w_new_ref[...] = w_ref[...] - matrix_rate * unrotated
 
 
-def update_kernel(across, number, grad_ref, bases_ref, *refs):
-    *refs, basis, sem = refs
-    copy = pltpu.make_async_copy(bases_ref.at[number], basis, sem)
-    copy.start()
-    copy.wait()
-    high, rest = split_low(basis[...])
-    update_step(across, grad_ref[...], high, rest, *refs)
-
-
-def update(grad, bases, number, weight, first, second, across=False):
-    vmem = pl.BlockSpec(memory_space=pltpu.VMEM)
+def update_kernel(across, grad_ref, high_ref, rest_ref, *refs):
+    update_step(across, grad_ref[...], high_ref[...], rest_ref[...], *refs)
+
+
+def update(grad, basis, weight, first, second, across=False):
     return pl.pallas_call(
-        functools.partial(update_kernel, across, number),
-        in_specs=[vmem, pl.BlockSpec(memory_space=pl.ANY), vmem, vmem, vmem],
+        functools.partial(update_kernel, across),
         out_shape=[jax.ShapeDtypeStruct(weight.shape, f32)] * 4,
-        scratch_shapes=[pltpu.VMEM((D, D), f32), pltpu.SemaphoreType.DMA(())],
         compiler_params=pltpu.CompilerParams(vmem_limit_bytes=UPDATE_VMEM),
         cost_estimate=pl.CostEstimate(flops=10 * grad.shape[0] * D * D, bytes_accessed=8 << 20, transcendentals=0),
         name="update",
-    )(grad, bases, weight, first, second)
+    )(grad, *basis, weight, first, second)
 
 
 def shards(
@@ -614,11 +606,15 @@
     )
     up, down, up_got, down_got = gather_first(jnp.stack(z_zero))
     z_one = gather_z(part_one)
-    up_got, down_got, *z_one = hold(up_got, down_got, *z_one)
+    up_got, down_got, z_one[1] = hold(up_got, down_got, z_one[1])
     up, down, first_zero = gather_second(up, down, up_got, down_got)
     up_got, down_got = gather_last(up, down)
     first_far_zero = swap(first_zero, core_bit)
-    up_got, down_got, first_far_zero = hold(up_got, down_got, first_far_zero)
+    late_bases, up, down = hold(bases, up, down)
+    split_bases = [part for k in range(4) for part in split_low(late_bases[k])]
+    up_got, down_got, first_far_zero, *rest = hold(up_got, down_got, first_far_zero, *z_one[2:], *split_bases)
+    z_one[2:], split_bases = rest[: len(z_one) - 2], rest[len(z_one) - 2 :]
+    split_bases = [split_bases[2 * k : 2 * k + 2] for k in range(4)]
     last_zero = joined(up_got, down_got)
     last_far_zero = swap(last_zero, core_bit)
 
@@ -650,14 +646,7 @@
 
     farthest, pair = shifted(kv_own, reach), shifted(kv_own[None], 1)
     up, down, up_got, down_got = gather_first(jnp.stack(z_one))
-    farthest, pair, up_got, down_got, normed_two = hold(farthest, pair, up_got, down_got, normed_two)
-    kv = jnp.concatenate([kv_own[None], pair], axis=0)
-    while kv.shape[0] < reach:
-        kv_got = shifted(kv, kv.shape[0])
-        if 2 * kv.shape[0] < reach:
-            kv = jnp.concatenate([kv, kv_got], axis=0)
-        else:
-            break
+    up_got, down_got, normed_two = hold(up_got, down_got, normed_two)
     up, down, first_one = gather_second(up, down, up_got, down_got)
     up_got, down_got = gather_last(up, down)
     first_far_one = swap(first_one, core_bit)
@@ -710,10 +699,13 @@
             value = gather_bit(value, bit, 0, True)
         return gather_bit(value, core_bit, len(x_bits), True).reshape(batch_count, -1, D)
 
-    sums, up_sum, down_sum, up_got, down_got, kv_got = feed_group(
-        0, None, normed_two, near_zero, far_zero, up_got, down_got, kv_got
-    )
-    kv = jnp.concatenate([kv, kv_got, farthest[None]], axis=0)
+    sums, up_sum, down_sum, up_got, down_got, farthest, pair = feed_group(
+        0, None, normed_two, near_zero, far_zero, up_got, down_got, farthest, pair
+    )
+    kv = jnp.concatenate([kv_own[None], pair], axis=0)
+    while kv.shape[0] < reach:
+        kv = jnp.concatenate([kv, shifted(kv, kv.shape[0])], axis=0)
+    kv = jnp.concatenate([kv, farthest[None]], axis=0)
     sum_zero = sum_first(up_sum, down_sum)
     *sum_zero, first_far_one, q_t = hold(*sum_zero, first_far_one, q_t)
     last_one = joined(up_got, down_got)
@@ -743,19 +735,21 @@
         entry, x_low, dy, dq_t, dkv, cosine, sine, qkv_full, normed_one, context, d_normed_two, gains, bias_grads,
         head_part_rows, seq_count, vec_len,
     )
+    z_got = [swap_z(sum_zero[k].astype(low), k) for k in range(1, depth)]
+    qkv_part, *z_got = hold(qkv_part, *z_got)
+    feed_zero = sum_zero[0] + sum(part.astype(f32) for part in z_got)
     outer = jnp.stack([qkv_part, out_part]).reshape((2, 2) + (2,) * len(x_bits) + (2, depth, head_part_rows, D))
     outer = outer[:, 0] + swap(outer[:, 1].astype(low), core_bit).astype(f32)
     sum_one = sum_first(
         jnp.concatenate([up_sum, outer[0]], axis=-2), jnp.concatenate([down_sum, outer[1]], axis=-2)
     )
-    feed_zero = sum_z(sum_zero)
+    grads_zero = spread(feed_zero)
     sum_one = sum_second(*sum_one)
-    *sum_one, feed_zero = hold(*sum_one, feed_zero)
-    grads_zero = spread(feed_zero)
+    *sum_one, grads_zero = hold(*sum_one, grads_zero)
     attn_out = lax.dot_general(context, out_full, last, preferred_element_type=f32)
     outputs = (x_low.astype(f32) + attn_out + mlp_out + out_bias).astype(low)
     sum_one = sum_third(sum_one[0], swap(sum_one[1], y_bit), sum_one[2], swap(sum_one[3], x_bits[-1]))
-    sum_one, grads_zero, outputs = hold(sum_one, grads_zero, outputs)
+    sum_one, outputs = hold(sum_one, outputs)
     grads_one = spread(sum_z(sum_one))
 
     end = unit_rows + head_part_rows
@@ -764,10 +758,10 @@
     qkv_all = grads_one[:, unit_rows : unit_rows + qkv_share].reshape(-1, D)[:qkv_rows]
     out_all = grads_one[:, end + unit_rows : end + unit_rows + out_own].reshape(-1, D)
     vector_grad = grads_one[:, end - 4, :vec_share].astype(f32).reshape(-1)[:vec_len]
-    out_grad, *out_states = update(out_all, bases, 1, out_weight, out_first, out_second)
-    qkv_grad, *qkv_states = update(qkv_all, bases, 0, qkv_weight, qkv_first, qkv_second)
-    up_grad, *up_states = update(up_all, bases, 2, up_weight, up_first, up_second)
-    down_grad, *down_states = update(down_all, bases, 3, down_weight, down_first, down_second, True)
+    out_grad, *out_states = update(out_all, split_bases[1], out_weight, out_first, out_second)
+    qkv_grad, *qkv_states = update(qkv_all, split_bases[0], qkv_weight, qkv_first, qkv_second)
+    up_grad, *up_states = update(up_all, split_bases[2], up_weight, up_first, up_second)
+    down_grad, *down_states = update(down_all, split_bases[3], down_weight, down_first, down_second, True)
     vector_new, *vector_states = adam_step(vectors, vector_grad, vector_first, vector_second)
     states = (qkv_states, out_states, up_states, down_states, (*vector_states, vector_new))
     return (

time: 315 us -> 311 us (0.987)
  waiting for transfers between devices: 129 us -> 97.7 us
  other arithmetic: 18.9 us -> 35.1 us
  starting transfers between devices: 59.9 us -> 68.2 us
    ppermute x27, waiting for transfers between devices: 66.5 us -> 48.6 us  [swap(): lax.ppermute(value, axis, [(i, i ^ step) for i in range(lax.axis_size(axi...]
    ppermute x12, waiting for transfers between devices: 54.2 us -> 46.3 us  [swap_z(): return lax.ppermute(value, 'seq', [(i, i ^ 2 * step) for i in range(size)])]
    ppermute x12, starting transfers between devices: 23.7 us -> 30 us  [swap_z(): return lax.ppermute(value, 'seq', [(i, i ^ 2 * step) for i in range(size)])]
    ppermute x6, waiting for transfers between devices: 8.12 us -> 2.84 us  [shifted(): lax.ppermute(value, 'seq', [(b, a) for a, b in pairs] if back else pairs)]
    unnamed x104 -> x122, local copies, waits for them, and re-layouts: 12.9 us -> 7.88 us
    ppermute x6, starting transfers between devices: 14.9 us -> 18.5 us  [shifted(): lax.ppermute(value, 'seq', [(b, a) for a, b in pairs] if back else pairs)]
  transfers between devices with their start and end apart: 45 -> 45, of which waited for: 24 -> 20; matrix products, arithmetic and copies ran while one was open for 7% -> 13% of each run, Pallas kernels for 20% -> 20%
where the time goes in v2:
time: 311 us; the launch traced here: 305 us
  waiting for transfers between devices  97.7 us (31%)
  Pallas kernels  75.6 us (24%)
  starting transfers between devices  68.2 us (22%)
  other arithmetic  35.1 us (11%)
  local copies, waits for them, and re-layouts  23.4 us (8%)
    ppermute x27, waiting for transfers between devices, swap(): lax.ppermute(value, axis, [(i, i ^ step) for i in range(lax.axis_size(axi...  48.6 us
    ppermute x12, waiting for transfers between devices, swap_z(): return lax.ppermute(value, 'seq', [(i, i ^ 2 * step) for i in range(size)])  46.3 us
    ppermute x12, starting transfers between devices, swap_z(): return lax.ppermute(value, 'seq', [(i, i ^ 2 * step) for i in range(size)])  30 us
    pallas_call x2, Pallas kernels, feed(): pl.pallas_call(feed_kernel, in_specs=[vmem, vmem, hbm, hbm, hbm, hbm, vme...  26.3 us
    ppermute x27, starting transfers between devices, swap(): lax.ppermute(value, axis, [(i, i ^ step) for i in range(lax.axis_size(axi...  19.7 us
    ppermute x6, starting transfers between devices, shifted(): lax.ppermute(value, 'seq', [(b, a) for a, b in pairs] if back else pairs)  18.5 us
    pallas_call x1, Pallas kernels, attention(): pl.pallas_call(functools.partial(attention_kernel, blocks, HEADS), grid=(...  18.3 us
    pallas_call x4, Pallas kernels, update(): pl.pallas_call(functools.partial(update_kernel, across), out_shape=[jax.S...  15 us
  transfers between devices with their start and end apart: 45, of which 20 were waited for; matrix products, arithmetic and copies ran while one was open for 13% of the time, Pallas kernels for 20%

profile of v2, /device:TPU:0, one launch (start us, length us, event | category | flops | bytes accessed | tf_op | source)
XLA Modules:
  0.0 304.7 jit_solution(16956074327553181041)
XLA Ops:
  0.7 1.3 constant_dynamic-slice_fusion
  4.3 3.0 collective-permute-start
  7.4 2.6 collective-permute-start.1
  12.1 5.7 %collective-permute-done = bf16[160,768]{1,0:T(8,128)(2,1)S(1)} collective-permute-done((bf16[160,768]{1,0:T(8,128)(2,1)S(1)}, bf16[160,768]{1,0:T(8,128)(2,1)S(1)}, u32[]{:S(2)}, u32[]{:S(2)}) %collective-permute-start) | collective-permute-done | bytes 245792 | tf_op jit(solution)/shard_map/ppermute | solution.py:49
  17.8 9.9 %collective-permute-done.1 = bf16[160,768]{1,0:T(8,128)(2,1)S(1)} collective-permute-done((bf16[160,768]{1,0:T(8,128)(2,1)S(1)}, bf16[160,768]{1,0:T(8,128)(2,1)S(1)}, u32[]{:S(2)}, u32[]{:S(2)}) %collective-permute-start.1) | collective-permute-done | bytes 245792 | tf_op jit(solution)/shard_map/ppermute | solution.py:49
  27.9 1.6 collective-permute-start.3
  29.5 1.5 collective-permute-start.4
  31.0 4.3 %collective-permute-start.5 = (bf16[96,768]{1,0:T(8,128)(2,1)S(1)}, bf16[96,768]{1,0:T(8,128)(2,1)S(1)}, u32[]{:S(2)}, u32[]{:S(2)}) collective-permute-start(bf16[96,768]{1,0:T(8,128)(2,1)S(1)} %pad_maximum_fusion.24), channel_id=1, source_target_pairs={{0,8},{4,12},{8,0},{12,4},{16,24},{20,28},{24,16},{28,20},{1,9},{5... | collective-permute-start | bytes 442376 | tf_op jit(solution)/shard_map/ppermute | solution.py:49
  35.3 3.1 %collective-permute-done.5 = bf16[96,768]{1,0:T(8,128)(2,1)S(1)} collective-permute-done((bf16[96,768]{1,0:T(8,128)(2,1)S(1)}, bf16[96,768]{1,0:T(8,128)(2,1)S(1)}, u32[]{:S(2)}, u32[]{:S(2)}) %collective-permute-start.5) | collective-permute-done | bytes 147488 | tf_op jit(solution)/shard_map/ppermute | solution.py:49
  38.5 1.2 collective-permute-done.4
  40.3 1.3 collective-permute-start.6
  42.1 6.7 %collective-permute-start.9 = (bf16[96,768]{1,0:T(8,128)(2,1)S(1)}, bf16[96,768]{1,0:T(8,128)(2,1)S(1)}, u32[]{:S(2)}, u32[]{:S(2)}) collective-permute-start(bf16[96,768]{1,0:T(8,128)(2,1)S(1)} %pad_maximum_fusion.24), channel_id=1, source_target_pairs={{0,16},{4,20},{8,24},{12,28},{16,0},{20,4},{24,8},{28,12},{1,17},{... | collective-permute-start | bytes 442376 | tf_op jit(solution)/shard_map/ppermute | solution.py:49
  48.8 1.4 collective-permute-start.10
  50.2 2.7 fusion.4
  52.9 6.9 %collective-permute-done.9 = bf16[96,768]{1,0:T(8,128)(2,1)S(1)} collective-permute-done((bf16[96,768]{1,0:T(8,128)(2,1)S(1)}, bf16[96,768]{1,0:T(8,128)(2,1)S(1)}, u32[]{:S(2)}, u32[]{:S(2)}) %collective-permute-start.9) | collective-permute-done | bytes 147488 | tf_op jit(solution)/shard_map/ppermute | solution.py:49
  59.8 4.7 %collective-permute-done.6 = bf16[2,4,80,768]{3,2,1,0:T(8,128)(2,1)S(1)} collective-permute-done((bf16[2,4,80,768]{3,2,1,0:T(8,128)(2,1)S(1)}, bf16[2,4,80,768]{3,2,1,0:T(8,128)(2,1)S(1)}, u32[]{:S(2)}, u32[]{:S(2)}) %collective-permute-start.6) | collective-permute-done | bytes 983072 | tf_op jit(solution)/shard_map/ppermute | solution.py:35
  68.3 2.4 collective-permute-done.13.last_far
  70.7 1.3 copy-done.52
  72.0 6.6 %head.1 = (bf16[512,768]{1,0:T(8,128)(2,1)}, bf16[512,768]{1,0:T(8,128)(2,1)}, bf16[768,512]{1,0:T(8,128)(2,1)}, bf16[128,512]{1,0:T(8,128)(2,1)}, bf16[896,768]...) custom-call(s32[32]{0:T(128)} %get-tuple-element.144.device_ref, ...), custom_call_target="tpu_custom_call" | custom-call | flops 2818572288 | bytes 8388608 | tf_op jit(solution)/shard_map/head/pallas_call | solution.py:347
  80.3 8.6 %collective-permute-start.16 = (bf16[128,512]{1,0:T(8,128)(2,1)S(1)}, bf16[128,512]{1,0:T(8,128)(2,1)S(1)}, u32[]{:S(2)}, u32[]{:S(2)}) collective-permute-start(bf16[128,512]{1,0:T(8,128)(2,1)S(1)} %copy-done.42), channel_id=1, source_target_pairs={{0,16},{4,20},{8,24},{12,28},{1,17},{5,21},{9,25},{13,29},{2,18},{... | collective-permute-start | bytes 393224 | tf_op jit(solution)/shard_map/ppermute | solution.py:645
  88.9 3.6 %collective-permute-start.17 = (bf16[1,128,512]{2,1,0:T(8,128)(2,1)S(1)}, bf16[1,128,512]{2,1,0:T(8,128)(2,1)S(1)}, u32[]{:S(2)}, u32[]{:S(2)}) collective-permute-start(bf16[1,128,512]{2,1,0:T(8,128)(2,1)S(1)} %bitcast.212), channel_id=1, source_target_pairs={{0,4},{4,8},{8,12},{12,16},{16,20},{20,24},{24,28},{1,5},{5,9},{9,... | collective-permute-start | bytes 393224 | tf_op jit(solution)/shard_map/ppermute | solution.py:645
  92.6 13.0 %feed.2 = (f32[512,768]{1,0:T(8,128)}, f32[512,768]{1,0:T(8,128)}, bf16[2,768,768]{2,1,0:T(8,128)(2,1)}, f32[2,768,768]{2,1,0:T(8,128)}, f32[1,768]{1,0:T(1,128)}, /*index=5*/f32[1,768]{1,0:T(1,128)}) custom-call(bf16[512,768]{1,0:T(8,128)(2,1)} %get-tuple-element.173.n_ref, bf16[512,768]{1,0:T(8,128)(2,1)} %bitcast.229, ...), custom_call_target="tpu_custom_call" | custom-call | flops 28991029248 | bytes 8388608 | tf_op jit(solution)/shard_map/feed/pallas_call | solution.py:241
  106.7 1.7 collective-permute-start.21
  108.5 1.7 convolution_convert_fusion.do_ref
  111.8 2.8 collective-permute-done.21
  119.1 1.2 collective-permute-start.22
  120.6 18.3 %attention.1 = (bf16[512,768]{1,0:T(8,128)(2,1)}, bf16[768,512]{1,0:T(8,128)(2,1)}, f32[128,512]{1,0:T(8,128)}, bf16[4,128,512]{2,1,0:T(8,128)(2,1)}) custom-call(bf16[768,512]{1,0:T(8,128)(2,1)} %get-tuple-element.163.q_ref, bf16[768,512]{1,0:T(8,128)(2,1)} %convolution_convert_fusion.do_ref, s32[4,1,128]{2,1,0:T(1,128)} %bitcast.228, ...), custom_call_target="tpu_custom_call" | custom-call | flops 14092861440 | bytes 8388608 | tf_op jit(solution)/shard_map/attention/pallas_call | solution.py:142
  141.6 1.3 collective-permute-start.26
  142.9 1.8 collective-permute-start.27
  145.1 1.9 collective-permute-start.24
  147.9 13.3 %feed.3 = (f32[512,768]{1,0:T(8,128)}, f32[512,768]{1,0:T(8,128)}, bf16[2,768,768]{2,1,0:T(8,128)(2,1)}, f32[2,768,768]{2,1,0:T(8,128)}, f32[1,768]{1,0:T(1,128)}, /*index=5*/f32[1,768]{1,0:T(1,128)}) custom-call(bf16[512,768]{1,0:T(8,128)(2,1)} %get-tuple-element.173.n_ref, bf16[512,768]{1,0:T(8,128)(2,1)} %bitcast.230, ...), custom_call_target="tpu_custom_call" | custom-call | flops 28991029248 | bytes 8388608 | tf_op jit(solution)/shard_map/feed/pallas_call | solution.py:241
  161.4 1.5 collective-permute-start.29
  163.7 3.8 %collective-permute-start.30 = (bf16[96,768]{1,0:T(8,128)(2,1)S(1)}, bf16[96,768]{1,0:T(8,128)(2,1)S(1)}, u32[]{:S(2)}, u32[]{:S(2)}) collective-permute-start(bf16[96,768]{1,0:T(8,128)(2,1)S(1)} %get-tuple-element.286), channel_id=1, source_target_pairs={{0,8},{4,12},{8,0},{12,4},{16,24},{20,28},{24,16},{28,20},{1,9},{5... | collective-permute-start | bytes 442376 | tf_op jit(solution)/shard_map/ppermute | solution.py:49
  167.6 3.7 %collective-permute-start.31 = (bf16[96,768]{1,0:T(8,128)(2,1)S(1)}, bf16[96,768]{1,0:T(8,128)(2,1)S(1)}, u32[]{:S(2)}, u32[]{:S(2)}) collective-permute-start(bf16[96,768]{1,0:T(8,128)(2,1)S(1)} %get-tuple-element.285), channel_id=1, source_target_pairs={{0,16},{4,20},{8,24},{12,28},{16,0},{20,4},{24,8},{28,12},{1,17},{... | collective-permute-start | bytes 442376 | tf_op jit(solution)/shard_map/ppermute | solution.py:49
  171.3 1.6 fusion.34.dkv_ref
  173.0 9.5 %tail.1 = (bf16[512,768]{1,0:T(8,128)(2,1)}, f32[32,32,768]{2,1,0:T(8,128)}, f32[32,32,768]{2,1,0:T(8,128)}) custom-call(s32[32]{0:T(128)} %get-tuple-element.186.entry_ref, bf16[512,768]{1,0:T(8,128)(2,1)} %bitcast.206, bf16[512,768]{1,0:T(8,128)(2,1)} %bitcast.231, bf16[768,512]{1,0:T(8,128)(2,1)} %get-tuple-element.187.dq_ref, ...), custom_call_target="tpu_custom_call" | custom-call | flops 8455716864 | bytes 8388608 | tf_op jit(solution)/shard_map/tail/pallas_call | solution.py:444
  183.3 3.3 %fusion.16 = bf16[2,2,2,4,32,768]{5,4,3,2,1,0:T(8,128)(2,1)} fusion(f32[1,2,2,2,4,32,768]{6,5,4,3,2,1,0:T(8,128)} %bitcast.191, f32[1,2,2,2,4,32,768]{6,5,4,3,2,1,0:T(8,128)} %bitcast.189), kind=kLoop, calls=%fused_computation.38 | loop fusion | flops 786432 | bytes 7864320 | tf_op jit(solution)/shard_map/convert_element_type | solution.py:742
  186.8 1.4 fusion.32
  188.2 1.3 collective-permute-start.36
  190.5 2.8 fusion.2
  193.2 1.4 slice_bitcast_fusion
  194.6 2.9 convert_add_fusion
  197.5 1.8 fusion.75
  201.1 1.2 collective-permute-start.34
  203.8 1.7 fusion.19
  205.6 1.4 collective-permute-start.35
  208.0 17.1 %collective-permute-done.34 = bf16[2,4,80,768]{3,2,1,0:T(8,128)(2,1)} collective-permute-done((bf16[2,4,80,768]{3,2,1,0:T(8,128)(2,1)}, bf16[2,4,80,768]{3,2,1,0:T(8,128)(2,1)}, u32[]{:S(2)}, u32[]{:S(2)}) %collective-permute-start.34) | collective-permute-done | bytes 983072 | tf_op jit(solution)/shard_map/ppermute | solution.py:35
  225.2 1.5 fusion.13
  226.9 2.9 collective-permute-done.35
  232.3 1.4 collective-permute-start.38
  233.7 1.3 add_convert_fusion
  234.9 8.2 %collective-permute-done.39 = bf16[4,80,768]{2,1,0:T(8,128)(2,1)S(1)} collective-permute-done((bf16[4,80,768]{2,1,0:T(8,128)(2,1)S(1)}, bf16[4,80,768]{2,1,0:T(8,128)(2,1)S(1)}, u32[]{:S(2)}, u32[]{:S(2)}) %collective-permute-start.39) | collective-permute-done | bytes 491552 | tf_op jit(solution)/shard_map/ppermute | solution.py:35
  243.2 2.0 collective-permute-done.38
  245.7 3.5 %collective-permute-start.42 = (bf16[160,768]{1,0:T(8,128)(2,1)S(1)}, bf16[160,768]{1,0:T(8,128)(2,1)S(1)}, u32[]{:S(2)}, u32[]{:S(2)}) collective-permute-start(bf16[160,768]{1,0:T(8,128)(2,1)S(1)} %get-tuple-element.270), channel_id=1, source_target_pairs={{0,24},{4,28},{8,16},{12,20},{16,8},{20,12},{24,0},{28,4},{1,25},{... | collective-permute-start | bytes 737288 | tf_op jit(solution)/shard_map/ppermute | solution.py:49
  250.1 6.4 %collective-permute-done.42 = bf16[160,768]{1,0:T(8,128)(2,1)S(1)} collective-permute-done((bf16[160,768]{1,0:T(8,128)(2,1)S(1)}, bf16[160,768]{1,0:T(8,128)(2,1)S(1)}, u32[]{:S(2)}, u32[]{:S(2)}) %collective-permute-start.42) | collective-permute-done | bytes 245792 | tf_op jit(solution)/shard_map/ppermute | solution.py:49
  256.5 13.5 %collective-permute-done.41 = bf16[160,768]{1,0:T(8,128)(2,1)S(1)} collective-permute-done((bf16[160,768]{1,0:T(8,128)(2,1)S(1)}, bf16[160,768]{1,0:T(8,128)(2,1)S(1)}, u32[]{:S(2)}, u32[]{:S(2)}) %collective-permute-start.41) | collective-permute-done | bytes 245792 | tf_op jit(solution)/shard_map/ppermute | solution.py:49
  271.0 7.0 %collective-permute-done.43 = bf16[160,768]{1,0:T(8,128)(2,1)S(1)} collective-permute-done((bf16[160,768]{1,0:T(8,128)(2,1)S(1)}, bf16[160,768]{1,0:T(8,128)(2,1)S(1)}, u32[]{:S(2)}, u32[]{:S(2)}) %collective-permute-start.43) | collective-permute-done | bytes 245792 | tf_op jit(solution)/shard_map/ppermute | solution.py:35
  283.1 1.6 reshape.209.grad_ref
  285.5 1.2 pad_maximum_fusion.18
  287.9 1.3 multiply_subtract_fusion
  289.3 2.6 update.4
  292.0 2.7 update.5
  294.8 4.8 %update.6 = (f32[384,768]{1,0:T(8,128)}, f32[384,768]{1,0:T(8,128)}, f32[384,768]{1,0:T(8,128)}, f32[384,768]{1,0:T(8,128)}) custom-call(bf16[384,768]{1,0:T(8,128)(2,1)S(1)} %bitcast.184, bf16[768,768]{1,0:T(8,128)(2,1)S(1)} %copy-done.6, bf16[768,768]{1,0:T(8,128)(2,1)S(1)} %copy-done.5, f32[384,768]{1,0:T(8,128)S(1)} %copy-done.15, ...), custom_call_target="tpu_custom_call" | custom-call | flops 2264924160 | bytes 8388608 | tf_op jit(solution)/shard_map/update/pallas_call | solution.py:487
  299.6 5.0 %update.7 = (f32[768,384]{1,0:T(8,128)}, f32[768,384]{1,0:T(8,128)}, f32[768,384]{1,0:T(8,128)}, f32[768,384]{1,0:T(8,128)}) custom-call(bf16[384,768]{1,0:T(8,128)(2,1)S(1)} %bitcast.183, bf16[768,768]{1,0:T(8,128)(2,1)S(1)} %copy-done.4, bf16[768,768]{1,0:T(8,128)(2,1)S(1)} %copy-done.3, f32[768,384]{1,0:T(8,128)S(1)} %copy-done.14, ...), custom_call_target="tpu_custom_call" | custom-call | flops 2264924160 | bytes 8388608 | tf_op jit(solution)/shard_map/update/pallas_call | solution.py:487
  (260 shorter events, 41.9 us)
Async XLA Ops:
  0.7 9.9 %copy-start.50 = (s32[4,8]{1,0:T(4,128)S(1)}, s32[4,8]{1,0:T(4,128)}, u32[]{:S(2)}) copy-start(s32[4,8]{1,0:T(4,128)} %param.21) | copy-start | bytes 388
  4.3 13.5 %collective-permute-start = (bf16[160,768]{1,0:T(8,128)(2,1)S(1)}, bf16[160,768]{1,0:T(8,128)(2,1)S(1)}, u32[]{:S(2)}, u32[]{:S(2)}) collective-permute-start(bf16[160,768]{1,0:T(8,128)(2,1)S(1)} %constant_dynamic-update-slice_fusion), channel_id=1, source_target_pairs={{0,8},{4,12},{8,0},{12,4},{16,24},{20,28},{24,16},{28,20},{1,9},{5... | collective-permute-start | bytes 737288 | tf_op jit(solution)/shard_map/ppermute | solution.py:49
  7.4 20.3 %collective-permute-start.1 = (bf16[160,768]{1,0:T(8,128)(2,1)S(1)}, bf16[160,768]{1,0:T(8,128)(2,1)S(1)}, u32[]{:S(2)}, u32[]{:S(2)}) collective-permute-start(bf16[160,768]{1,0:T(8,128)(2,1)S(1)} %constant_dynamic-update-slice_fusion), channel_id=1, source_target_pairs={{0,16},{4,20},{8,24},{12,28},{16,0},{20,4},{24,8},{28,12},{1,17},{... | collective-permute-start | bytes 737288 | tf_op jit(solution)/shard_map/ppermute | solution.py:49
  9.9 17.7 %collective-permute-start.2 = (bf16[160,768]{1,0:T(8,128)(2,1)S(1)}, bf16[160,768]{1,0:T(8,128)(2,1)S(1)}, u32[]{:S(2)}, u32[]{:S(2)}) collective-permute-start(bf16[160,768]{1,0:T(8,128)(2,1)S(1)} %constant_dynamic-update-slice_fusion), channel_id=1, source_target_pairs={{0,24},{4,28},{8,16},{12,20},{16,8},{20,12},{24,0},{28,4},{1,25},{... | collective-permute-start | bytes 737288 | tf_op jit(solution)/shard_map/ppermute | solution.py:49
  27.9 10.6 %collective-permute-start.3 = (bf16[4,80,768]{2,1,0:T(8,128)(2,1)S(1)}, bf16[4,80,768]{2,1,0:T(8,128)(2,1)S(1)}, u32[]{:S(2)}, u32[]{:S(2)}) collective-permute-start(bf16[4,80,768]{2,1,0:T(8,128)(2,1)S(1)} %get-tuple-element.279), channel_id=1, source_target_pairs={{0,4},{4,0},{8,12},{12,8},{16,20},{20,16},{24,28},{28,24},{1,5},{5... | collective-permute-start | bytes 1474568 | tf_op jit(solution)/shard_map/ppermute | solution.py:35
  29.5 10.2 %collective-permute-start.4 = (bf16[4,80,768]{2,1,0:T(8,128)(2,1)S(1)}, bf16[4,80,768]{2,1,0:T(8,128)(2,1)S(1)}, u32[]{:S(2)}, u32[]{:S(2)}) collective-permute-start(bf16[4,80,768]{2,1,0:T(8,128)(2,1)S(1)} %get-tuple-element.278), channel_id=1, source_target_pairs={{0,2},{1,3},{2,0},{3,1},{4,6},{5,7},{6,4},{7,5},{8,10},{9,11},{10,... | collective-permute-start | bytes 1474568 | tf_op jit(solution)/shard_map/ppermute | solution.py:35
  31.0 7.4 %collective-permute-start.5 = (bf16[96,768]{1,0:T(8,128)(2,1)S(1)}, bf16[96,768]{1,0:T(8,128)(2,1)S(1)}, u32[]{:S(2)}, u32[]{:S(2)}) collective-permute-start(bf16[96,768]{1,0:T(8,128)(2,1)S(1)} %pad_maximum_fusion.24), channel_id=1, source_target_pairs={{0,8},{4,12},{8,0},{12,4},{16,24},{20,28},{24,16},{28,20},{1,9},{5... | collective-permute-start | bytes 442376 | tf_op jit(solution)/shard_map/ppermute | solution.py:49
  39.7 10.4 %copy-start.20 = (f32[4,768,768]{2,1,0:T(8,128)S(1)}, f32[4,768,768]{2,1,0:T(8,128)}, u32[]{:S(2)}) copy-start(f32[4,768,768]{2,1,0:T(8,128)} %param.27) | copy-start | bytes 28311556
  40.2 12.7 %copy-start.30 = (bf16[2,2,4,80,768]{4,3,2,1,0:T(8,128)(2,1)}, bf16[2,2,4,80,768]{4,3,2,1,0:T(8,128)(2,1)S(1)}, u32[]{:S(2)}) copy-start(bf16[2,2,4,80,768]{4,3,2,1,0:T(8,128)(2,1)S(1)} %pad_maximum_fusion.3.first_near) | copy-start | bytes 5898244
  40.2 25.2 %collective-permute-start.8 = (bf16[2,2,4,80,768]{4,3,2,1,0:T(8,128)(2,1)S(1)}, bf16[2,2,4,80,768]{4,3,2,1,0:T(8,128)(2,1)S(1)}, u32[]{:S(2)}, u32[]{:S(2)}) collective-permute-start(bf16[2,2,4,80,768]{4,3,2,1,0:T(8,128)(2,1)S(1)} %pad_maximum_fusion.3.first_near), channel_id=1, source_target_pairs={{0,1},{1,0},{2,3},{3,2},{4,5},{5,4},{6,7},{7,6},{8,9},{9,8},{10,11... | collective-permute-start | bytes 5898248 | tf_op jit(solution)/shard_map/ppermute | solution.py:35
  40.3 24.2 %collective-permute-start.6 = (bf16[2,4,80,768]{3,2,1,0:T(8,128)(2,1)S(1)}, bf16[2,4,80,768]{3,2,1,0:T(8,128)(2,1)S(1)}, u32[]{:S(2)}, u32[]{:S(2)}) collective-permute-start(bf16[2,4,80,768]{3,2,1,0:T(8,128)(2,1)S(1)} %get-tuple-element.273), channel_id=1, source_target_pairs={{0,2},{1,3},{2,0},{3,1},{4,6},{5,7},{6,4},{7,5},{8,10},{9,11},{10,... | collective-permute-start | bytes 2949128 | tf_op jit(solution)/shard_map/ppermute | solution.py:35
  41.6 23.8 %collective-permute-start.7 = (bf16[2,4,80,768]{3,2,1,0:T(8,128)(2,1)S(1)}, bf16[2,4,80,768]{3,2,1,0:T(8,128)(2,1)S(1)}, u32[]{:S(2)}, u32[]{:S(2)}) collective-permute-start(bf16[2,4,80,768]{3,2,1,0:T(8,128)(2,1)S(1)} %get-tuple-element.275), channel_id=1, source_target_pairs={{0,4},{4,0},{8,12},{12,8},{16,20},{20,16},{24,28},{28,24},{1,5},{5... | collective-permute-start | bytes 2949128 | tf_op jit(solution)/shard_map/ppermute | solution.py:35
  42.1 17.7 %collective-permute-start.9 = (bf16[96,768]{1,0:T(8,128)(2,1)S(1)}, bf16[96,768]{1,0:T(8,128)(2,1)S(1)}, u32[]{:S(2)}, u32[]{:S(2)}) collective-permute-start(bf16[96,768]{1,0:T(8,128)(2,1)S(1)} %pad_maximum_fusion.24), channel_id=1, source_target_pairs={{0,16},{4,20},{8,24},{12,28},{16,0},{20,4},{24,8},{28,12},{1,17},{... | collective-permute-start | bytes 442376 | tf_op jit(solution)/shard_map/ppermute | solution.py:49
  48.8 11.0 %collective-permute-start.10 = (bf16[96,768]{1,0:T(8,128)(2,1)S(1)}, bf16[96,768]{1,0:T(8,128)(2,1)S(1)}, u32[]{:S(2)}, u32[]{:S(2)}) collective-permute-start(bf16[96,768]{1,0:T(8,128)(2,1)S(1)} %pad_maximum_fusion.24), channel_id=1, source_target_pairs={{0,24},{4,28},{8,16},{12,20},{16,8},{20,12},{24,0},{28,4},{1,25},{... | collective-permute-start | bytes 442376 | tf_op jit(solution)/shard_map/ppermute | solution.py:49
  66.7 5.3 %copy-start.31 = (bf16[2,2,4,80,768]{4,3,2,1,0:T(8,128)(2,1)}, bf16[2,2,4,80,768]{4,3,2,1,0:T(8,128)(2,1)S(1)}, u32[]{:S(2)}) copy-start(bf16[2,2,4,80,768]{4,3,2,1,0:T(8,128)(2,1)S(1)} %pad_maximum_fusion.4.last_near) | copy-start | bytes 5898244
  66.7 4.0 %collective-permute-start.13 = (bf16[2,2,4,80,768]{4,3,2,1,0:T(8,128)(2,1)S(1)}, bf16[2,2,4,80,768]{4,3,2,1,0:T(8,128)(2,1)S(1)}, u32[]{:S(2)}, u32[]{:S(2)}) collective-permute-start(bf16[2,2,4,80,768]{4,3,2,1,0:T(8,128)(2,1)S(1)} %pad_maximum_fusion.4.last_near), channel_id=1, source_target_pairs={{0,1},{1,0},{2,3},{3,2},{4,5},{5,4},{6,7},{7,6},{8,9},{9,8},{10,11... | collective-permute-start | bytes 5898248 | tf_op jit(solution)/shard_map/ppermute | solution.py:35
  66.9 11.7 %collective-permute-start.11 = (bf16[4,48,768]{2,1,0:T(8,128)(2,1)S(1)}, bf16[4,48,768]{2,1,0:T(8,128)(2,1)S(1)}, u32[]{:S(2)}, u32[]{:S(2)}) collective-permute-start(bf16[4,48,768]{2,1,0:T(8,128)(2,1)S(1)} %get-tuple-element.294), channel_id=1, source_target_pairs={{0,4},{4,0},{8,12},{12,8},{16,20},{20,16},{24,28},{28,24},{1,5},{5... | collective-permute-start | bytes 884744 | tf_op jit(solution)/shard_map/ppermute | solution.py:35
  67.4 11.2 %collective-permute-start.12 = (bf16[4,48,768]{2,1,0:T(8,128)(2,1)S(1)}, bf16[4,48,768]{2,1,0:T(8,128)(2,1)S(1)}, u32[]{:S(2)}, u32[]{:S(2)}) collective-permute-start(bf16[4,48,768]{2,1,0:T(8,128)(2,1)S(1)} %get-tuple-element.293), channel_id=1, source_target_pairs={{0,2},{1,3},{2,0},{3,1},{4,6},{5,7},{6,4},{7,5},{8,10},{9,11},{10,... | collective-permute-start | bytes 884744 | tf_op jit(solution)/shard_map/ppermute | solution.py:35
  78.7 26.9 %collective-permute-start.14 = (bf16[2,4,48,768]{3,2,1,0:T(8,128)(2,1)S(1)}, bf16[2,4,48,768]{3,2,1,0:T(8,128)(2,1)S(1)}, u32[]{:S(2)}, u32[]{:S(2)}) collective-permute-start(bf16[2,4,48,768]{3,2,1,0:T(8,128)(2,1)S(1)} %get-tuple-element.288), channel_id=1, source_target_pairs={{0,2},{1,3},{2,0},{3,1},{4,6},{5,7},{6,4},{7,5},{8,10},{9,11},{10,... | collective-permute-start | bytes 1769480 | tf_op jit(solution)/shard_map/ppermute | solution.py:35
  79.7 26.0 %collective-permute-start.15 = (bf16[2,4,48,768]{3,2,1,0:T(8,128)(2,1)S(1)}, bf16[2,4,48,768]{3,2,1,0:T(8,128)(2,1)S(1)}, u32[]{:S(2)}, u32[]{:S(2)}) collective-permute-start(bf16[2,4,48,768]{3,2,1,0:T(8,128)(2,1)S(1)} %get-tuple-element.290), channel_id=1, source_target_pairs={{0,4},{4,0},{8,12},{12,8},{16,20},{20,16},{24,28},{28,24},{1,5},{5... | collective-permute-start | bytes 1769480 | tf_op jit(solution)/shard_map/ppermute | solution.py:35
  80.3 25.4 %collective-permute-start.16 = (bf16[128,512]{1,0:T(8,128)(2,1)S(1)}, bf16[128,512]{1,0:T(8,128)(2,1)S(1)}, u32[]{:S(2)}, u32[]{:S(2)}) collective-permute-start(bf16[128,512]{1,0:T(8,128)(2,1)S(1)} %copy-done.42), channel_id=1, source_target_pairs={{0,16},{4,20},{8,24},{12,28},{1,17},{5,21},{9,25},{13,29},{2,18},{... | collective-permute-start | bytes 393224 | tf_op jit(solution)/shard_map/ppermute | solution.py:645
  88.9 16.7 %collective-permute-start.17 = (bf16[1,128,512]{2,1,0:T(8,128)(2,1)S(1)}, bf16[1,128,512]{2,1,0:T(8,128)(2,1)S(1)}, u32[]{:S(2)}, u32[]{:S(2)}) collective-permute-start(bf16[1,128,512]{2,1,0:T(8,128)(2,1)S(1)} %bitcast.212), channel_id=1, source_target_pairs={{0,4},{4,8},{8,12},{12,16},{16,20},{20,24},{24,28},{1,5},{5,9},{9,... | collective-permute-start | bytes 393224 | tf_op jit(solution)/shard_map/ppermute | solution.py:645
  105.7 9.9 %collective-permute-start.19 = (bf16[2,768,768]{2,1,0:T(8,128)(2,1)}, bf16[2,768,768]{2,1,0:T(8,128)(2,1)S(1)}, u32[]{:S(2)}, u32[]{:S(2)}) collective-permute-start(bf16[2,768,768]{2,1,0:T(8,128)(2,1)} %get-tuple-element.161), channel_id=1, source_target_pairs={{0,1},{1,0},{2,3},{3,2},{4,5},{5,4},{6,7},{7,6},{8,9},{9,8},{10,11... | collective-permute-start | bytes 7077896 | tf_op jit(solution)/shard_map/ppermute | solution.py:35
  106.6 11.5 %collective-permute-start.20 = (bf16[2,2,4,48,768]{4,3,2,1,0:T(8,128)(2,1)S(1)}, bf16[2,2,4,48,768]{4,3,2,1,0:T(8,128)(2,1)S(1)}, u32[]{:S(2)}, u32[]{:S(2)}) collective-permute-start(bf16[2,2,4,48,768]{4,3,2,1,0:T(8,128)(2,1)S(1)} %pad_maximum_fusion.8.first_near), channel_id=1, source_target_pairs={{0,1},{1,0},{2,3},{3,2},{4,5},{5,4},{6,7},{7,6},{8,9},{9,8},{10,11... | collective-permute-start | bytes 3538952 | tf_op jit(solution)/shard_map/ppermute | solution.py:35
  106.7 7.9 %collective-permute-start.21 = (bf16[2,128,512]{2,1,0:T(8,128)(2,1)S(1)}, bf16[2,128,512]{2,1,0:T(8,128)(2,1)S(1)}, u32[]{:S(2)}, u32[]{:S(2)}) collective-permute-start(bf16[2,128,512]{2,1,0:T(8,128)(2,1)S(1)} %pad_maximum_fusion.23), channel_id=1, source_target_pairs={{0,8},{4,12},{8,16},{12,20},{16,24},{20,28},{1,9},{5,13},{9,17},{1... | collective-permute-start | bytes 786440 | tf_op jit(solution)/shard_map/ppermute | solution.py:645
  108.4 7.1 %copy-start.29 = (f32[2,768,768]{2,1,0:T(8,128)S(1)}, f32[2,768,768]{2,1,0:T(8,128)}, u32[]{:S(2)}) copy-start(f32[2,768,768]{2,1,0:T(8,128)} %get-tuple-element.160) | copy-start | bytes 14155780
  111.3 33.8 %collective-permute-start.18 = (bf16[2,2,4,48,768]{4,3,2,1,0:T(8,128)(2,1)}, bf16[2,2,4,48,768]{4,3,2,1,0:T(8,128)(2,1)}, u32[]{:S(2)}, u32[]{:S(2)}) collective-permute-start(bf16[2,2,4,48,768]{4,3,2,1,0:T(8,128)(2,1)} %pad_maximum_fusion.7.last_near), channel_id=1, source_target_pairs={{0,1},{1,0},{2,3},{3,2},{4,5},{5,4},{6,7},{7,6},{8,9},{9,8},{10,11... | collective-permute-start | bytes 3538952 | tf_op jit(solution)/shard_map/ppermute | solution.py:35
  119.1 25.6 %collective-permute-start.22 = (bf16[2,4,48,768]{3,2,1,0:T(8,128)(2,1)}, bf16[2,4,48,768]{3,2,1,0:T(8,128)(2,1)S(1)}, u32[]{:S(2)}, u32[]{:S(2)}) collective-permute-start(bf16[2,4,48,768]{3,2,1,0:T(8,128)(2,1)} %bitcast.33), channel_id=1, source_target_pairs={{0,2},{1,3},{2,0},{3,1},{4,6},{5,7},{6,4},{7,5},{8,10},{9,11},{10,... | collective-permute-start | bytes 1769480 | tf_op jit(solution)/shard_map/ppermute | solution.py:35
  120.3 24.5 %collective-permute-start.23 = (bf16[2,4,48,768]{3,2,1,0:T(8,128)(2,1)}, bf16[2,4,48,768]{3,2,1,0:T(8,128)(2,1)S(1)}, u32[]{:S(2)}, u32[]{:S(2)}) collective-permute-start(bf16[2,4,48,768]{3,2,1,0:T(8,128)(2,1)} %fusion.20), channel_id=1, source_target_pairs={{0,4},{4,0},{8,12},{12,8},{16,20},{20,16},{24,28},{28,24},{1,5},{5... | collective-permute-start | bytes 1769480 | tf_op jit(solution)/shard_map/ppermute | solution.py:35
  141.6 19.5 %collective-permute-start.26 = (bf16[128,512]{1,0:T(8,128)(2,1)S(1)}, bf16[128,512]{1,0:T(8,128)(2,1)}, u32[]{:S(2)}, u32[]{:S(2)}) collective-permute-start(bf16[128,512]{1,0:T(8,128)(2,1)S(1)} %slice_bitcast_fusion.13), channel_id=1, source_target_pairs={{16,0},{20,4},{24,8},{28,12},{17,1},{21,5},{25,9},{29,13},{18,2},{... | collective-permute-start | bytes 393224 | tf_op jit(solution)/shard_map/ppermute | solution.py:645
  142.9 18.2 %collective-permute-start.27 = (bf16[2,128,512]{2,1,0:T(8,128)(2,1)}, bf16[2,128,512]{2,1,0:T(8,128)(2,1)S(1)}, u32[]{:S(2)}, u32[]{:S(2)}) collective-permute-start(bf16[2,128,512]{2,1,0:T(8,128)(2,1)} %slice.217), channel_id=1, source_target_pairs={{8,0},{12,4},{16,8},{20,12},{24,16},{28,20},{9,1},{13,5},{17,9},{2... | collective-permute-start | bytes 786440 | tf_op jit(solution)/shard_map/ppermute | solution.py:645
  145.1 16.0 %collective-permute-start.24 = (bf16[4,48,768]{2,1,0:T(8,128)(2,1)S(1)}, bf16[4,48,768]{2,1,0:T(8,128)(2,1)S(1)}, u32[]{:S(2)}, u32[]{:S(2)}) collective-permute-start(bf16[4,48,768]{2,1,0:T(8,128)(2,1)S(1)} %fusion.27), channel_id=1, source_target_pairs={{0,4},{4,0},{8,12},{12,8},{16,20},{20,16},{24,28},{28,24},{1,5},{5... | collective-permute-start | bytes 884744 | tf_op jit(solution)/shard_map/ppermute | solution.py:35
  147.0 14.1 %collective-permute-start.25 = (bf16[4,48,768]{2,1,0:T(8,128)(2,1)S(1)}, bf16[4,48,768]{2,1,0:T(8,128)(2,1)S(1)}, u32[]{:S(2)}, u32[]{:S(2)}) collective-permute-start(bf16[4,48,768]{2,1,0:T(8,128)(2,1)S(1)} %fusion.28), channel_id=1, source_target_pairs={{0,2},{1,3},{2,0},{3,1},{4,6},{5,7},{6,4},{7,5},{8,10},{9,11},{10,... | collective-permute-start | bytes 884744 | tf_op jit(solution)/shard_map/ppermute | solution.py:35
  147.9 13.4 %copy-start.43 = (f32[128,512]{1,0:T(8,128)S(1)}, f32[128,512]{1,0:T(8,128)}, u32[]{:S(2)}) copy-start(f32[128,512]{1,0:T(8,128)} %get-tuple-element.188) | copy-start | bytes 786436
  161.2 33.4 %collective-permute-start.28 = (bf16[2,768,768]{2,1,0:T(8,128)(2,1)}, bf16[2,768,768]{2,1,0:T(8,128)(2,1)}, u32[]{:S(2)}, u32[]{:S(2)}) collective-permute-start(bf16[2,768,768]{2,1,0:T(8,128)(2,1)} %get-tuple-element.185), channel_id=1, source_target_pairs={{0,1},{1,0},{2,3},{3,2},{4,5},{5,4},{6,7},{7,6},{8,9},{9,8},{10,11... | collective-permute-start | bytes 7077896 | tf_op jit(solution)/shard_map/ppermute | solution.py:35
  161.4 9.9 %collective-permute-start.29 = (bf16[1,128,512]{2,1,0:T(8,128)(2,1)S(1)}, bf16[1,128,512]{2,1,0:T(8,128)(2,1)S(1)}, u32[]{:S(2)}, u32[]{:S(2)}) collective-permute-start(bf16[1,128,512]{2,1,0:T(8,128)(2,1)S(1)} %slice.395), channel_id=1, source_target_pairs={{4,0},{8,4},{12,8},{16,12},{20,16},{24,20},{28,24},{5,1},{9,5},{13... | collective-permute-start | bytes 393224 | tf_op jit(solution)/shard_map/ppermute | solution.py:645
  163.0 10.0 %copy-start.28 = (f32[4,48,768]{2,1,0:T(8,128)}, f32[4,48,768]{2,1,0:T(8,128)S(1)}, u32[]{:S(2)}) copy-start(f32[4,48,768]{2,1,0:T(8,128)S(1)} %convert_add_fusion.7) | copy-start | bytes 1769476
  163.7 18.7 %collective-permute-start.30 = (bf16[96,768]{1,0:T(8,128)(2,1)S(1)}, bf16[96,768]{1,0:T(8,128)(2,1)S(1)}, u32[]{:S(2)}, u32[]{:S(2)}) collective-permute-start(bf16[96,768]{1,0:T(8,128)(2,1)S(1)} %get-tuple-element.286), channel_id=1, source_target_pairs={{0,8},{4,12},{8,0},{12,4},{16,24},{20,28},{24,16},{28,20},{1,9},{5... | collective-permute-start | bytes 442376 | tf_op jit(solution)/shard_map/ppermute | solution.py:49
  167.6 14.9 %collective-permute-start.31 = (bf16[96,768]{1,0:T(8,128)(2,1)S(1)}, bf16[96,768]{1,0:T(8,128)(2,1)S(1)}, u32[]{:S(2)}, u32[]{:S(2)}) collective-permute-start(bf16[96,768]{1,0:T(8,128)(2,1)S(1)} %get-tuple-element.285), channel_id=1, source_target_pairs={{0,16},{4,20},{8,24},{12,28},{16,0},{20,4},{24,8},{28,12},{1,17},{... | collective-permute-start | bytes 442376 | tf_op jit(solution)/shard_map/ppermute | solution.py:49
  171.3 12.0 %collective-permute-start.32 = (bf16[96,768]{1,0:T(8,128)(2,1)S(1)}, bf16[96,768]{1,0:T(8,128)(2,1)S(1)}, u32[]{:S(2)}, u32[]{:S(2)}) collective-permute-start(bf16[96,768]{1,0:T(8,128)(2,1)S(1)} %get-tuple-element.284), channel_id=1, source_target_pairs={{0,24},{4,28},{8,16},{12,20},{16,8},{20,12},{24,0},{28,4},{1,25},{... | collective-permute-start | bytes 442376 | tf_op jit(solution)/shard_map/ppermute | solution.py:49
  186.6 3.8 %collective-permute-start.33 = (bf16[2,2,2,4,32,768]{5,4,3,2,1,0:T(8,128)(2,1)}, bf16[2,2,2,4,32,768]{5,4,3,2,1,0:T(8,128)(2,1)}, u32[]{:S(2)}, u32[]{:S(2)}) collective-permute-start(bf16[2,2,2,4,32,768]{5,4,3,2,1,0:T(8,128)(2,1)} %fusion.16), channel_id=1, source_target_pairs={{0,1},{1,0},{2,3},{3,2},{4,5},{5,4},{6,7},{7,6},{8,9},{9,8},{10,11... | collective-permute-start | bytes 4718600 | tf_op jit(solution)/shard_map/ppermute | solution.py:35
  186.7 7.9 %slice-start = ((s8[4718592]{0:T(1024)(128)(4,1)}), s8[4194304]{0:T(1024)(128)(4,1)S(1)}, s32[]{:S(2)}) async-start(s8[4718592]{0:T(1024)(128)(4,1)} %bitcast.196), calls=%async_computation | async-start | bytes 8388608
  188.2 6.5 %slice-start.1 = ((s8[4718592]{0:T(1024)(128)(4,1)}), s8[524288]{0:T(1024)(128)(4,1)S(1)}, s32[]{:S(2)}) async-start(s8[4718592]{0:T(1024)(128)(4,1)} %bitcast.196), calls=%async_computation.1 | async-start | bytes 1048576
  188.2 14.1 %collective-permute-start.36 = (bf16[96,768]{1,0:T(8,128)(2,1)S(1)}, bf16[96,768]{1,0:T(8,128)(2,1)S(1)}, u32[]{:S(2)}, u32[]{:S(2)}) collective-permute-start(bf16[96,768]{1,0:T(8,128)(2,1)S(1)} %fusion.32), channel_id=1, source_target_pairs={{0,2},{1,3},{2,0},{3,1},{4,6},{5,7},{6,4},{7,5},{8,10},{9,11},{10,... | collective-permute-start | bytes 442376 | tf_op jit(solution)/shard_map/ppermute | solution.py:35
  201.1 24.1 %collective-permute-start.34 = (bf16[2,4,80,768]{3,2,1,0:T(8,128)(2,1)}, bf16[2,4,80,768]{3,2,1,0:T(8,128)(2,1)}, u32[]{:S(2)}, u32[]{:S(2)}) collective-permute-start(bf16[2,4,80,768]{3,2,1,0:T(8,128)(2,1)} %fusion.18), channel_id=1, source_target_pairs={{0,2},{1,3},{2,0},{3,1},{4,6},{5,7},{6,4},{7,5},{8,10},{9,11},{10,... | collective-permute-start | bytes 2949128 | tf_op jit(solution)/shard_map/ppermute | solution.py:35
  203.7 3.2 %collective-permute-start.37 = (bf16[2,96,768]{2,1,0:T(8,128)(2,1)}, bf16[2,96,768]{2,1,0:T(8,128)(2,1)}, u32[]{:S(2)}, u32[]{:S(2)}) collective-permute-start(bf16[2,96,768]{2,1,0:T(8,128)(2,1)} %pad_maximum_fusion.22), channel_id=1, source_target_pairs={{0,1},{1,0},{2,3},{3,2},{4,5},{5,4},{6,7},{7,6},{8,9},{9,8},{10,11... | collective-permute-start | bytes 884744 | tf_op jit(solution)/shard_map/ppermute | solution.py:35
  203.8 21.4 %copy-start.26 = (f32[2,2,4,32,768]{4,3,2,1,0:T(8,128)S(1)}, f32[2,2,4,32,768]{4,3,2,1,0:T(8,128)}, u32[]{:S(2)}) copy-start(f32[2,2,4,32,768]{4,3,2,1,0:T(8,128)} %copy-done.25) | copy-start | bytes 4718596
  205.5 19.7 %copy-start.23 = (f32[1,768,768]{2,1,0:T(8,128)S(1)}, f32[1,768,768]{2,1,0:T(8,128)}, u32[]{:S(2)}) copy-start(f32[1,768,768]{2,1,0:T(8,128)} %copy-done.22) | copy-start | bytes 7077892
  205.6 24.2 %collective-permute-start.35 = (bf16[2,4,80,768]{3,2,1,0:T(8,128)(2,1)S(1)}, bf16[2,4,80,768]{3,2,1,0:T(8,128)(2,1)S(1)}, u32[]{:S(2)}, u32[]{:S(2)}) collective-permute-start(bf16[2,4,80,768]{3,2,1,0:T(8,128)(2,1)S(1)} %fusion.19), channel_id=1, source_target_pairs={{0,4},{4,0},{8,12},{12,8},{16,20},{20,16},{24,28},{28,24},{1,5},{5... | collective-permute-start | bytes 2949128 | tf_op jit(solution)/shard_map/ppermute | solution.py:35
  230.2 12.9 %collective-permute-start.39 = (bf16[4,80,768]{2,1,0:T(8,128)(2,1)S(1)}, bf16[4,80,768]{2,1,0:T(8,128)(2,1)S(1)}, u32[]{:S(2)}, u32[]{:S(2)}) collective-permute-start(bf16[4,80,768]{2,1,0:T(8,128)(2,1)S(1)} %fusion.23), channel_id=1, source_target_pairs={{0,2},{1,3},{2,0},{3,1},{4,6},{5,7},{6,4},{7,5},{8,10},{9,11},{10,... | collective-permute-start | bytes 1474568 | tf_op jit(solution)/shard_map/ppermute | solution.py:35
  232.3 12.9 %collective-permute-start.38 = (bf16[4,80,768]{2,1,0:T(8,128)(2,1)S(1)}, bf16[4,80,768]{2,1,0:T(8,128)(2,1)S(1)}, u32[]{:S(2)}, u32[]{:S(2)}) collective-permute-start(bf16[4,80,768]{2,1,0:T(8,128)(2,1)S(1)} %fusion.22), channel_id=1, source_target_pairs={{0,4},{4,0},{8,12},{12,8},{16,20},{20,16},{24,28},{28,24},{1,5},{5... | collective-permute-start | bytes 1474568 | tf_op jit(solution)/shard_map/ppermute | solution.py:35
  245.7 10.8 %collective-permute-start.42 = (bf16[160,768]{1,0:T(8,128)(2,1)S(1)}, bf16[160,768]{1,0:T(8,128)(2,1)S(1)}, u32[]{:S(2)}, u32[]{:S(2)}) collective-permute-start(bf16[160,768]{1,0:T(8,128)(2,1)S(1)} %get-tuple-element.270), channel_id=1, source_target_pairs={{0,24},{4,28},{8,16},{12,20},{16,8},{20,12},{24,0},{28,4},{1,25},{... | collective-permute-start | bytes 737288 | tf_op jit(solution)/shard_map/ppermute | solution.py:49
  249.1 20.8 %collective-permute-start.41 = (bf16[160,768]{1,0:T(8,128)(2,1)S(1)}, bf16[160,768]{1,0:T(8,128)(2,1)S(1)}, u32[]{:S(2)}, u32[]{:S(2)}) collective-permute-start(bf16[160,768]{1,0:T(8,128)(2,1)S(1)} %get-tuple-element.271), channel_id=1, source_target_pairs={{0,16},{4,20},{8,24},{12,28},{16,0},{20,4},{24,8},{28,12},{1,17},{... | collective-permute-start | bytes 737288 | tf_op jit(solution)/shard_map/ppermute | solution.py:49
  249.5 20.5 %collective-permute-start.40 = (bf16[160,768]{1,0:T(8,128)(2,1)S(1)}, bf16[160,768]{1,0:T(8,128)(2,1)S(1)}, u32[]{:S(2)}, u32[]{:S(2)}) collective-permute-start(bf16[160,768]{1,0:T(8,128)(2,1)S(1)} %get-tuple-element.269), channel_id=1, source_target_pairs={{0,8},{4,12},{8,0},{12,4},{16,24},{20,28},{24,16},{28,20},{1,9},{5... | collective-permute-start | bytes 737288 | tf_op jit(solution)/shard_map/ppermute | solution.py:49
  270.1 7.9 %collective-permute-start.43 = (bf16[160,768]{1,0:T(8,128)(2,1)S(1)}, bf16[160,768]{1,0:T(8,128)(2,1)S(1)}, u32[]{:S(2)}, u32[]{:S(2)}) collective-permute-start(bf16[160,768]{1,0:T(8,128)(2,1)S(1)} %fusion.26), channel_id=1, source_target_pairs={{0,2},{1,3},{2,0},{3,1},{4,6},{5,7},{6,4},{7,5},{8,10},{9,11},{10,... | collective-permute-start | bytes 737288 | tf_op jit(solution)/shard_map/ppermute | solution.py:35
  278.1 1.9 collective-permute-start.44
  285.5 6.5 %copy-start.47 = (f32[1072]{0:T(1024)}, f32[1072]{0:T(1024)S(1)}, u32[]{:S(2)}) copy-start(f32[1072]{0:T(1024)S(1)} %reshape.213) | copy-start | bytes 12868
  289.3 5.4 %copy-start.15 = (f32[384,768]{1,0:T(8,128)S(1)}, f32[384,768]{1,0:T(8,128)}, u32[]{:S(2)}) copy-start(f32[384,768]{1,0:T(8,128)} %refs_0_.6) | copy-start | bytes 3538948
  289.3 5.4 %copy-start.16 = (f32[384,768]{1,0:T(8,128)S(1)}, f32[384,768]{1,0:T(8,128)}, u32[]{:S(2)}) copy-start(f32[384,768]{1,0:T(8,128)} %refs_1_.6) | copy-start | bytes 3538948
  289.3 5.3 %copy-start.17 = (f32[384,768]{1,0:T(8,128)S(1)}, f32[384,768]{1,0:T(8,128)}, u32[]{:S(2)}) copy-start(f32[384,768]{1,0:T(8,128)} %refs_2_.6) | copy-start | bytes 3538948
  294.7 4.8 %copy-start.3 = (bf16[768,768]{1,0:T(8,128)(2,1)S(1)}, bf16[768,768]{1,0:T(8,128)(2,1)}, u32[]{:S(2)}) copy-start(bf16[768,768]{1,0:T(8,128)(2,1)} %get-tuple-element.230.rest_ref) | copy-start | bytes 3538948
  294.7 4.8 %copy-start.4 = (bf16[768,768]{1,0:T(8,128)(2,1)S(1)}, bf16[768,768]{1,0:T(8,128)(2,1)}, u32[]{:S(2)}) copy-start(bf16[768,768]{1,0:T(8,128)(2,1)} %get-tuple-element.229.high_ref) | copy-start | bytes 3538948
  294.7 4.8 %copy-start.14 = (f32[768,384]{1,0:T(8,128)S(1)}, f32[768,384]{1,0:T(8,128)}, u32[]{:S(2)}) copy-start(f32[768,384]{1,0:T(8,128)} %refs_0_.7) | copy-start | bytes 3538948
  294.7 4.8 %copy-start.18 = (f32[768,384]{1,0:T(8,128)S(1)}, f32[768,384]{1,0:T(8,128)}, u32[]{:S(2)}) copy-start(f32[768,384]{1,0:T(8,128)} %refs_1_.7) | copy-start | bytes 3538948
  (41 other events, 114.7 us)
